TPU v7x, 32 devices: a whole 2x2x4 slice. The times are simulated.
32 devices in a mesh: facet: 4 (over z), vis: 8 (over y, x, core).
Axes of the slice: x: 2, y: 2, z: 4, core: 2. Of those that a mesh axis runs over, the one named last changes fastest.
Arguments:
- vis_obs: float32 [4096, 2, 4, 1024], P(('facet', 'vis')), may hold values from -6 to 6
- uv_coords: float32 [4096, 2, 1024], P(('facet', 'vis')), may hold values from -16 to 16
- vis_weight: float32 [4096, 1024], P(('facet', 'vis')), may hold values from 0.5 to 900, as said below
- block_group: int32 [4096, 1], P(('facet', 'vis')), may hold values from 0 to 31; in each aligned block of 128 rows (0 to 127, 128 to 255, ...) at most 8 rows name the same one
- tile_slot: int32 [4096], P(('facet', 'vis')), may hold values from 0 to 63
- w_plane: int32 [4096], P(('facet', 'vis')), may hold values from 0 to 31
- model_tiles: bfloat16 [2048, 2, 32, 128], P(('facet', 'vis')), may hold values from -6 to 6
- w_kernels: bfloat16 [32, 2, 32, 32], replicated, may hold values from -0.75 to 0.75
Outputs:
- residual_vis: float32 [4096, 2, 4, 1024], P(('facet', 'vis'))
- residual_tiles: float32 [2048, 2, 32, 128], P(('facet', 'vis'))
Inputs may be any that keep to these rules, and one draw needn't show every extreme that they name: `block_group`: in the 128 rows of one device (aligned blocks of 128 rows) no group is named by more than 8 rows, a bound that some block reaches. `vis_weight`: Positive.
All inputs are finite; a program needn't handle non-finite values.
Results may differ from a plain program's by a relative error of at most 0.0045.
Values may be sent and summed in bfloat16 or wider, within the bound.
No kernel may reach another device: no remote copies, remote signals or barrier semaphores. Data moves between devices by JAX's collectives and lax.ppermute only.
A program may use at most 128 MiB of HBM per device.

v0:
```python
import math

import jax
import jax.numpy as jnp
from jax import lax
from jax.sharding import PartitionSpec as P


def complex_product(form_text, left_side, right_side):
    real_part = jnp.einsum(
        form_text, left_side[:, 0], right_side[:, 0], preferred_element_type=jnp.float32
    ) - jnp.einsum(form_text, left_side[:, 1], right_side[:, 1], preferred_element_type=jnp.float32)
    imag_part = jnp.einsum(
        form_text, left_side[:, 0], right_side[:, 1], preferred_element_type=jnp.float32
    ) + jnp.einsum(form_text, left_side[:, 1], right_side[:, 0], preferred_element_type=jnp.float32)
    return jnp.stack((real_part, imag_part), axis=1)


def conjugate(operand):
    return jnp.stack((operand[:, 0], -operand[:, 1]), axis=1)


def phasors(coordinates, sub_width):
    offsets = (jnp.arange(sub_width) - sub_width // 2).astype(jnp.float32) * (
        -2.0 * math.pi / sub_width
    )
    angles = coordinates[:, :, None, :] * offsets[None, None, :, None]
    return (jnp.cos(angles), jnp.sin(angles))


def degrid_grid(tile_rows, kernels, coordinates, observed, weights):
    block_count = tile_rows.shape[0]
    sub_width = tile_rows.shape[2]
    span_width = tile_rows.shape[3]
    pol_count = span_width // sub_width
    vis_count = coordinates.shape[-1]
    left_prod = complex_product("nij,njq->niq", kernels, tile_rows).astype(jnp.bfloat16)
    left_prod = left_prod.reshape(block_count, 2, sub_width, pol_count, sub_width)
    kerneled = (
        complex_product("nlpm,nkm->nlpk", left_prod, kernels)
        .reshape(block_count, 2, sub_width, span_width)
        .astype(jnp.bfloat16)
    )
    cosine, sine_part = phasors(coordinates, sub_width)
    along_u = jnp.stack((cosine[:, 0], sine_part[:, 0]), axis=1).astype(jnp.bfloat16)
    phase_real = cosine[:, 1][:, None]
    phase_imag = sine_part[:, 1][:, None]
    spread = complex_product("nlq,nlk->nqk", kerneled, along_u).reshape(
        block_count, 2, pol_count, sub_width, vis_count
    )
    predicted_real = (
        jnp.sum(spread[:, 0] * phase_real - spread[:, 1] * phase_imag, axis=2) / sub_width
    )
    predicted_imag = (
        jnp.sum(spread[:, 0] * phase_imag + spread[:, 1] * phase_real, axis=2) / sub_width
    )
    residual = observed - jnp.stack((predicted_real, predicted_imag), axis=1)
    factor = (weights / sub_width)[:, None, None, :]
    residual_real = residual[:, 0][:, :, None, :]
    residual_imag = residual[:, 1][:, :, None, :]
    weighted_real = (residual_real * phase_real + residual_imag * phase_imag) * factor
    weighted_imag = (residual_imag * phase_real - residual_real * phase_imag) * factor
    weighted = (
        jnp.stack((weighted_real, weighted_imag), axis=1)
        .reshape(block_count, 2, span_width, vis_count)
        .astype(jnp.bfloat16)
    )
    gridded = complex_product("nlk,nqk->nlq", conjugate(along_u), weighted).astype(jnp.bfloat16)
    back_prod = complex_product("nji,njq->niq", conjugate(kernels), gridded).astype(jnp.bfloat16)
    back_prod = back_prod.reshape(block_count, 2, sub_width, pol_count, sub_width)
    contribution = complex_product("nlpm,nmk->nlpk", back_prod, conjugate(kernels)).reshape(
        block_count, 2, sub_width, span_width
    )
    return (residual, contribution)


def shards(vis_obs, uv_coords, vis_weight, block_group, tile_slot, w_plane, model_tiles, w_kernels):
    blocks = vis_obs.shape[0]
    groups = lax.axis_size(("facet", "vis"))
    owned_tiles = model_tiles.shape[0]
    tile_shape = model_tiles.shape[1:]
    capacity = max(2, 2 * blocks // groups)
    target = block_group[:, 0]
    markers = (target[:, None] == jnp.arange(groups, dtype=jnp.int32)[None, :]).astype(jnp.int32)
    before = jnp.cumsum(markers, axis=0) - markers
    slot_rank = jnp.sum(before * markers, axis=1)
    position = target * capacity + slot_rank
    wanted = jnp.full((groups * capacity,), -1, jnp.int32).at[position].set(tile_slot)
    requested = lax.all_to_all(
        wanted.reshape(groups, capacity), ("facet", "vis"), split_axis=0, concat_axis=0, tiled=True
    )
    chosen = jnp.take(model_tiles, jnp.maximum(requested, 0).reshape(-1), axis=0)
    chosen = chosen.reshape((groups, capacity) + tile_shape)
    arrived = lax.all_to_all(chosen, ("facet", "vis"), split_axis=0, concat_axis=0, tiled=True)
    arrived = arrived.reshape((groups * capacity,) + tile_shape)
    tile_rows = jnp.take(arrived, position, axis=0)
    kernels = jnp.take(w_kernels, w_plane, axis=0)
    batch_size = math.gcd(blocks, 8)

    def split_blocks(operand):
        return operand.reshape((blocks // batch_size, batch_size) + operand.shape[1:])

    def process(inputs):
        return degrid_grid(inputs[0], inputs[1], inputs[2], inputs[3], inputs[4])

    residual, contribution = lax.map(
        process,
        (
            split_blocks(tile_rows),
            split_blocks(kernels),
            split_blocks(uv_coords),
            split_blocks(vis_obs),
            split_blocks(vis_weight),
        ),
    )
    residual = residual.reshape(vis_obs.shape)
    contribution = contribution.reshape((blocks,) + tile_shape)
    outgoing = (
        jnp.zeros((groups * capacity,) + tile_shape, jnp.float32).at[position].set(contribution)
    )
    outgoing = outgoing.reshape((groups, capacity) + tile_shape)
    returned = lax.all_to_all(outgoing, ("facet", "vis"), split_axis=0, concat_axis=0, tiled=True)
    returned = returned.reshape(groups * capacity, -1)
    selector = (
        requested.reshape(-1)[None, :] == jnp.arange(owned_tiles, dtype=jnp.int32)[:, None]
    ).astype(jnp.float32)
    summed = jnp.dot(
        selector, returned, precision=lax.Precision.HIGHEST, preferred_element_type=jnp.float32
    )
    summed = summed.reshape(model_tiles.shape)
    weight_sum = lax.psum(jnp.sum(vis_weight), ("facet", "vis"))
    scaling = blocks * groups * vis_obs.shape[-1] / weight_sum
    return (residual, summed * scaling)


def solution(mesh):
    in_specs = (
        P(("facet", "vis"), None, None, None),
        P(("facet", "vis"), None, None),
        P(("facet", "vis"), None),
        P(("facet", "vis"), None),
        P(("facet", "vis")),
        P(("facet", "vis")),
        P(("facet", "vis"), None, None, None),
        P(),
    )
    out_specs = (P(("facet", "vis"), None, None, None), P(("facet", "vis"), None, None, None))
    return jax.shard_map(shards, mesh=mesh, in_specs=in_specs, out_specs=out_specs, check_vma=False)
```

profile of v0, /device:TPU:0, one launch (start us, length us, event | category | flops | bytes accessed | tf_op | source)
XLA Modules:
  0.0 884.6 jit_solution(4024056815160483818)
XLA Ops:
  4.4 14.3 %all_to_all.22 = s32[32,1,8]{2,1,0:T(1,128)S(1)} all-to-all(s32[32,1,8]{2,1,0:T(1,128)S(1)} %bitcast.283), channel_id=1, replica_groups=mesh['facet'=4,'vis'=8] {'facet','vis'}, dimensions={0} | all-to-all | bytes 2048 | tf_op jit(solution)/shard_map/all_to_all | solution.py:89
  32.5 91.2 %all-to-all-done.1 = bf16[32,8,2,32,128]{4,3,2,1,0:T(8,128)(2,1)} async-done(((bf16[32,8,2,32,128]{4,3,2,1,0:T(8,128)(2,1)}), bf16[32,8,2,32,128]{4,3,2,1,0:T(8,128)(2,1)}, u32[]{:S(2)}, u32[]{:S(2)}) %all-to-all-start.1) | async-done | bytes 4194336 | tf_op jit(solution)/shard_map/all_to_all | solution.py:94
  128.4 493.5 %while.14 = (s32[]{:T(128)}, f32[16,8,2,4,1024]{4,3,2,1,0:T(4,128)}, f32[16,8,2,32,128]{4,3,2,1,0:T(8,128)}, f32[16,8,2,4,1024]{4,3,2,1,0:T(4,128)}, bf16[16,8,2...) while((s32[]{:T(128)}, ...), condition=%wide.region_6.7_spmd, body=%wide.region_3.6_spmd.sunk | while | flops 593404032 | bytes 89195904 | solution.py:106
  134.3 7.3 multiply_cosine_fusion.2
  165.1 7.3 multiply_cosine_fusion.2
  195.9 7.3 multiply_cosine_fusion.2
  226.8 7.3 multiply_cosine_fusion.2
  257.6 7.3 multiply_cosine_fusion.2
  288.5 7.3 multiply_cosine_fusion.2
  319.3 7.3 multiply_cosine_fusion.2
  350.2 7.3 multiply_cosine_fusion.2
  381.0 7.3 multiply_cosine_fusion.2
  411.9 7.3 multiply_cosine_fusion.2
  442.7 7.3 multiply_cosine_fusion.2
  473.6 7.3 multiply_cosine_fusion.2
  504.4 7.3 multiply_cosine_fusion.2
  535.3 7.3 multiply_cosine_fusion.2
  566.1 7.3 multiply_cosine_fusion.2
  597.0 7.3 multiply_cosine_fusion.2
  626.2 19.4 %scatter_fusion = f32[256,2,32,128]{3,2,1,0:T(8,128)} fusion(f32[256,2,32,128]{3,2,1,0:T(8,128)} %broadcast_in_dim.71, s32[128]{0:T(128)S(1)} %bitcast.288, f32[128,2,32,128]{3,2,1,0:T(8,128)} %bitcast.280), kind=kCustom, calls=%fused_computation.4 | custom fusion | bytes 12583424 | tf_op jit(solution)/shard_map/scatter | solution.py:119
  651.3 203.5 %psum.7 = f32[]{:T(128)} all-reduce(f32[]{:T(128)} %reduce_sum.46), channel_id=1, replica_groups=mesh['facet'=4,'vis'=8] {'facet','vis'}, use_global_device_ids=true, to_apply=%region_9.10 | all-reduce | flops 1 | bytes 8 | tf_op jit(solution)/shard_map/psum | solution.py:131
  856.8 9.4 %reshape.351 = f32[256,8192]{1,0:T(8,128)} reshape(f32[32,8,2,32,128]{4,3,2,1,0:T(8,128)} %all-to-all-done.2) | data formatting | bytes 16777216 | tf_op jit(solution)/shard_map/reshape | solution.py:123
  866.2 9.0 %copy.130 = f32[8192,256]{1,0:T(8,128)} copy(f32[8192,256]{0,1:T(8,128)} %bitcast.275) | data formatting | bytes 16777216 | tf_op jit(solution)/shard_map/dot_general | solution.py:127
  875.2 6.9 convolution_multiply_fusion
  (880 shorter events, 409.0 us)
Async XLA Ops:
  0.6 18.3 %copy-start = (bf16[64,2,32,128]{3,2,1,0:T(8,128)(2,1)S(1)}, bf16[64,2,32,128]{3,2,1,0:T(8,128)(2,1)}, u32[]{:S(2)}) copy-start(bf16[64,2,32,128]{3,2,1,0:T(8,128)(2,1)} %param.16) | copy-start | bytes 3145732
  18.6 3.5 copy-start.3
  25.9 3.7 copy-start.5
  25.9 4.0 copy-start.2
  25.9 97.7 %all-to-all-start.1 = ((bf16[32,8,2,32,128]{4,3,2,1,0:T(8,128)(2,1)}), bf16[32,8,2,32,128]{4,3,2,1,0:T(8,128)(2,1)}, u32[]{:S(2)}, u32[]{:S(2)}) async-start(bf16[32,8,2,32,128]{4,3,2,1,0:T(8,128)(2,1)} %broadcast_select_fusion), calls=%async_computation.1 | async-start | bytes 8388608 | tf_op jit(solution)/shard_map/all_to_all | solution.py:94
  645.6 210.4 %copy-start.4 = (s32[32,1,8]{2,1,0:T(1,128)S(1)}, s32[32,1,8]{2,1,0:T(1,128)}, u32[]{:S(2)}) copy-start(s32[32,1,8]{2,1,0:T(1,128)} %copy-done.3) | copy-start | bytes 3076
  645.6 211.2 %all-to-all-start.2 = ((f32[32,8,2,32,128]{4,3,2,1,0:T(8,128)}), f32[32,8,2,32,128]{4,3,2,1,0:T(8,128)}, u32[]{:S(2)}, u32[]{:S(2)}) async-start(f32[32,8,2,32,128]{4,3,2,1,0:T(8,128)} %bitcast.273), calls=%async_computation.2 | async-start | bytes 16777216 | tf_op jit(solution)/shard_map/all_to_all | solution.py:122
  875.2 9.4 %copy-start.1 = (bf16[64,2,32,128]{3,2,1,0:T(8,128)(2,1)S(1)}, bf16[64,2,32,128]{3,2,1,0:T(8,128)(2,1)}, u32[]{:S(2)}) copy-start(bf16[64,2,32,128]{3,2,1,0:T(8,128)(2,1)} %param.16) | copy-start | bytes 3145732
where the time goes:
time: 889 us; the launch traced here: 885 us
  other arithmetic  240 us (27%)
  blocking collectives  218 us (25%)
  matrix products  182 us (20%)
  local copies, waits for them, and re-layouts  141 us (16%)
  waiting for transfers between devices  91.2 us (10%)
    psum x1, blocking collectives, shards(): weight_sum = lax.psum(jnp.sum(vis_weight), ('facet', 'vis'))  204 us
    cos x16, other arithmetic, phasors(): return (jnp.cos(angles), jnp.sin(angles))  117 us
    all_to_all x1, waiting for transfers between devices, shards(): lax.all_to_all(chosen, ('facet', 'vis'), split_axis=0, concat_axis=0, til...  91.2 us
    dot_general x96, matrix products, complex_product(): jnp.einsum(form_text, left_side[:, 1], right_side[:, 0], preferred_elemen...  63.1 us
    dynamic_update_slice x32, other arithmetic, shards(): lax.map(process, (split_blocks(tile_rows), split_blocks(kernels), split_b...  39.7 us
    dot_general x96, matrix products, complex_product(): jnp.einsum(form_text, left_side[:, 1], right_side[:, 1], preferred_elemen...  38 us
    dot_general x96, matrix products, complex_product(): jnp.einsum(form_text, left_side[:, 0], right_side[:, 0], preferred_elemen...  37 us
    dot_general x96, matrix products, complex_product(): jnp.einsum(form_text, left_side[:, 0], right_side[:, 1], preferred_elemen...  36.6 us
  transfers between devices with their start and end apart: 2, of which 1 were waited for; matrix products, arithmetic and copies ran while one was open for 1% of the time, Pallas kernels for 0%

commit v1 on v0

v1 whole, which is shorter than its diff:
```python
import functools
import math

import jax
import jax.numpy as jnp
from jax import lax
from jax.experimental import pallas as pl
from jax.experimental.pallas import tpu as pltpu
from jax.sharding import PartitionSpec as P

AXES = ("facet", "vis")
BATCH = 8
LANES = 256
TILE = 128
SIN_TERMS = [(-1.0) ** i * (2.0 * math.pi) ** (2 * i + 1) / math.factorial(2 * i + 1) for i in range(8)]
COS_TERMS = [(-1.0) ** i * (2.0 * math.pi) ** (2 * i) / math.factorial(2 * i) for i in range(9)]


def polynomial(terms, square):
    total = jnp.full_like(square, terms[-1])
    for term in terms[-2::-1]:
        total = total * square + term
    return total


def unit_phasor(turns):
    halves = jnp.floor(turns * 2.0 + 0.5)
    part = turns - halves * 0.5
    odd = halves - 2.0 * jnp.floor(halves * 0.5)
    sign = 1.0 - 2.0 * odd
    square = part * part
    return sign * polynomial(COS_TERMS, square), -sign * part * polynomial(SIN_TERMS, square)


def phasor_powers(cosine, sine, count):
    powers = {1: (cosine, sine)}
    for j in range(2, count + 1):
        ar, ai = powers[j // 2]
        br, bi = powers[j - j // 2]
        if j % 2 == 0:
            powers[j] = (ar * ar - ai * ai, 2.0 * ar * ai)
        else:
            powers[j] = (ar * br - ai * bi, ar * bi + ai * br)
    return powers


def rows_dot(left, right, left_dim, right_dim):
    return lax.dot_general(
        left, right, (((left_dim,), (right_dim,)), ((), ())), preferred_element_type=jnp.float32
    )


def split(value):
    high = value.astype(jnp.bfloat16)
    return high, (value - high.astype(jnp.float32)).astype(jnp.bfloat16)


def block_kernel(
    meta, order, slot, plane, tile_ref, obs_ref, u_ref, v_ref, w_ref, left_ref, back_ref, right_ref, *rest, aliased
):
    if aliased:
        old_ref, res_ref, con_ref, fu_ref, fv_ref = rest
    else:
        res_ref, con_ref, fu_ref, fv_ref = rest
    half = fv_ref.shape[0] // 2 - 1
    width = 2 * half
    pols = obs_ref.shape[2]
    step = pl.program_id(0)
    inside = lax.rem(step, BATCH)

    @pl.when((inside == 0) & (step < meta[1]))
    def _():
        cosine, sine = unit_phasor(u_ref[...] * (1.0 / width))
        powers = phasor_powers(cosine, sine, half)
        ones, zeros = jnp.ones_like(cosine), jnp.zeros_like(cosine)
        stride = 2 * width

        def put(row, value):
            for t in range(fu_ref.shape[0]):
                fu_ref[t, pl.ds(row, BATCH, stride=stride), :] = value[:, t * TILE : (t + 1) * TILE]

        put(0, ones)
        put(width, zeros)
        for j in range(1, half + 1):
            real, imag = powers[j]
            if j < half:
                put(j, real)
                put(width + j, imag)
            low = half if j == half else half + j
            put(low, real)
            put(width + low, -imag)
        cosine, sine = unit_phasor(v_ref[...] * (1.0 / width))
        powers = phasor_powers(cosine, sine, half)
        for j in range(1, half + 1):
            fv_ref[j], fv_ref[half + 1 + j] = powers[j]

    which = plane[order[meta[0] + step]]

    def work():
        lane = lax.broadcasted_iota(jnp.int32, (2 * width, pols * width), 1)
        unpaired = lane < 2 * pols
        wide = 2 * pols * width
        band = lax.rem(lax.broadcasted_iota(jnp.int32, (width, wide), 1), pols)

        def paired(full):
            first, second = full[:, : pols * width], full[:, pols * width :]
            total = jnp.where(unpaired, first, first + second)
            change = jnp.where(unpaired, second, first - second)
            return jnp.concatenate([total, change], axis=1)

        spread_kernel = right_ref[which]
        right = jnp.concatenate(
            [
                jnp.where(band == p, spread_kernel[r * width : (r + 1) * width], jnp.zeros((), jnp.bfloat16))
                for r in range(2)
                for p in range(pols)
            ],
            axis=0,
        )
        tile = tile_ref[0].reshape(2 * width, pols * width)
        left = rows_dot(left_ref[which], tile, 1, 0).astype(jnp.bfloat16)
        left_real, left_imag = left[:width], left[width:]
        left = jnp.concatenate(
            [jnp.concatenate([left_real, left_imag], axis=1), jnp.concatenate([-left_imag, left_real], axis=1)],
            axis=0,
        )
        model = paired(rows_dot(left, right, 1, 0)).astype(jnp.bfloat16)
        base = pl.multiple_of(inside * 2 * width, 2 * width)
        sublane = lax.broadcasted_iota(jnp.int32, (2 * pols, LANES), 0)
        turn = jnp.where(sublane < pols, -1.0, 1.0)
        gridded = None
        for start in range(0, u_ref.shape[1], LANES):
            lanes = pl.ds(start, LANES)
            along_u = jnp.concatenate(
                [fu_ref[start // TILE + t, pl.ds(base, 2 * width), :] for t in range(LANES // TILE)], axis=1
            ).astype(jnp.bfloat16)
            spread = rows_dot(model, along_u, 0, 0).reshape(width, 2 * pols, LANES)

            def phase(index):
                return jnp.broadcast_to(fv_ref[index, pl.ds(inside, 1), lanes], (2 * pols, LANES))

            cos_part = spread[0] + spread[half] * phase(half)
            sin_part = -spread[half] * phase(2 * half + 1)
            for j in range(1, half):
                cos_part = cos_part + spread[j] * phase(j)
                sin_part = sin_part + spread[half + j] * phase(half + 1 + j)
            predicted = cos_part + turn * jnp.roll(sin_part, pols, axis=0)
            observed = jnp.concatenate([obs_ref[0, 0, :, lanes], obs_ref[0, 1, :, lanes]], axis=0)
            residual = observed - predicted * (1.0 / width)
            res_ref[0, 0, :, lanes] = residual[:pols]
            res_ref[0, 1, :, lanes] = residual[pols:]
            scaled = residual * (w_ref[pl.ds(inside, 1), lanes] * (1.0 / width))
            turned = -turn * jnp.roll(scaled, pols, axis=0)
            cos_rows, sin_rows = [scaled], [scaled * phase(half) - turned * phase(2 * half + 1)]
            for j in range(1, half):
                cos_rows.append(scaled * phase(j))
                sin_rows.append(turned * phase(half + 1 + j))
            weighted = jnp.concatenate(cos_rows + sin_rows, axis=0).astype(jnp.bfloat16)
            part = rows_dot(along_u, weighted, 1, 1)
            gridded = part if gridded is None else gridded + part
        back = rows_dot(jnp.concatenate(split(paired(gridded)), axis=0), right, 1, 1)
        back = back[: 2 * width] + back[2 * width :]
        span = pols * width
        back_real = back[:width, :span] + back[width:, span:]
        back_imag = back[:width, span:] - back[width:, :span]
        back = jnp.concatenate([back_real, back_imag], axis=0)
        result = rows_dot(back_ref[which], jnp.concatenate(split(back), axis=1), 1, 0)
        result = result[:, :span] + result[:, span:]
        con_ref[0] = result.astype(con_ref.dtype).reshape(con_ref.shape[1:])

    pl.when(step < meta[1])(work)
    if aliased:

        @pl.when((step >= meta[1]) & (step == 0))
        def _():
            res_ref[...] = old_ref[...]
            con_ref[...] = jnp.zeros_like(con_ref)


def process_blocks(steps, base, count, order, slot, plane, tiles, observed, u, v, weight, left, back, right, old=None):
    pols, vis_count = observed.shape[2:]
    width = tiles.shape[2]
    aliased = old is not None
    meta = jnp.stack([base, count]).astype(jnp.int32)

    def item(i, meta):
        return meta[0] + jnp.minimum(i, jnp.maximum(meta[1] - 1, 0))

    def by_block(i, meta, order, slot, plane):
        return (order[item(i, meta)], 0, 0, 0)

    def by_slot(i, meta, order, slot, plane):
        return (slot[order[item(i, meta)]], 0, 0, 0)

    def by_batch(i, meta, order, slot, plane):
        return (lax.div(item(i, meta), BATCH), 0)

    def whole(i, meta, order, slot, plane):
        return (0, 0, 0)

    tile_spec = pl.BlockSpec((1,) + tiles.shape[1:], by_slot)
    vis_spec = pl.BlockSpec((1,) + observed.shape[1:], by_block)
    row_spec = pl.BlockSpec((BATCH, vis_count), by_batch)
    operands = [tiles, observed, u, v, weight, left, back, right]
    in_specs = [tile_spec, vis_spec, row_spec, row_spec, row_spec] + [
        pl.BlockSpec(table.shape, whole) for table in (left, back, right)
    ]
    aliases = {}
    if aliased:
        operands.append(old)
        in_specs.append(vis_spec)
        aliases = {len(operands) + 3: 0}
    return pl.pallas_call(
        functools.partial(block_kernel, aliased=aliased),
        out_shape=(
            jax.ShapeDtypeStruct(observed.shape, jnp.float32),
            jax.ShapeDtypeStruct(tiles.shape, jnp.bfloat16),
        ),
        grid_spec=pltpu.PrefetchScalarGridSpec(
            num_scalar_prefetch=4,
            grid=(steps,),
            in_specs=in_specs,
            out_specs=(vis_spec, tile_spec),
            scratch_shapes=[
                pltpu.VMEM((vis_count // TILE, BATCH * 2 * width, TILE), jnp.float32),
                pltpu.VMEM((width + 2, BATCH, vis_count), jnp.float32),
            ],
        ),
        input_output_aliases=aliases,
        compiler_params=pltpu.CompilerParams(vmem_limit_bytes=40 * 1024 * 1024),
        cost_estimate=pl.CostEstimate(
            flops=steps * 2 * 2 * 2 * width * 2 * pols * width * vis_count,
            bytes_accessed=steps * 2 * pols * vis_count * 40,
            transcendentals=0,
        ),
        name="process_blocks",
    )(meta, order, slot, plane, *operands)


def sum_kernel(requested, scale_ref, *refs, last):
    if last:
        old_ref, arrived_ref, out_ref = refs
        out_ref[...] = old_ref[...]
    else:
        arrived_ref, out_ref = refs
        out_ref[...] = jnp.zeros_like(out_ref)

    @pl.loop(0, arrived_ref.shape[0])
    def _(i):
        tile = requested[i]

        @pl.when(tile >= 0)
        def _():
            out_ref[tile] += arrived_ref[i].astype(jnp.float32)

    if last:
        out_ref[...] = out_ref[...] * scale_ref[0]


def sum_tiles(requested, scale, arrived, owned, old=None):
    shape = (owned,) + arrived.shape[1:]
    operands = [arrived] if old is None else [old, arrived]
    vmem = pl.BlockSpec(memory_space=pltpu.VMEM)
    return pl.pallas_call(
        functools.partial(sum_kernel, last=old is not None),
        out_shape=jax.ShapeDtypeStruct(shape, jnp.float32),
        in_specs=[pl.BlockSpec(memory_space=pltpu.SMEM)] * 2 + [vmem] * len(operands),
        out_specs=vmem,
        compiler_params=pltpu.CompilerParams(vmem_limit_bytes=40 * 1024 * 1024),
        cost_estimate=pl.CostEstimate(flops=arrived.size, bytes_accessed=arrived.size * 4, transcendentals=0),
        name="sum_tiles",
    )(requested, scale, *operands)


def kernel_tables(w_kernels, pols):
    planes, _, width, _ = w_kernels.shape
    half = width // 2
    real, imag = w_kernels[:, 0], w_kernels[:, 1]

    def offsets(table):
        return jnp.concatenate([table[:, half:], table[:, :1], table[:, half - 1 : 0 : -1]], axis=1)

    real_rows, imag_rows = offsets(real), offsets(imag)
    left = jnp.concatenate(
        [jnp.concatenate([real_rows, -imag_rows], axis=2), jnp.concatenate([imag_rows, real_rows], axis=2)], axis=1
    )
    back = jnp.swapaxes(left, 1, 2)
    real_columns, imag_columns = jnp.swapaxes(real_rows, 1, 2), jnp.swapaxes(imag_rows, 1, 2)
    right = jnp.concatenate(
        [
            jnp.stack([real_columns, imag_columns], axis=3),
            jnp.stack([-imag_columns, real_columns], axis=3),
        ],
        axis=1,
    )
    right = jnp.broadcast_to(right[..., None], right.shape + (pols,)).reshape(planes, 2 * width, 2 * width * pols)
    return left, back, right


def exchange(operand):
    return lax.all_to_all(operand, AXES, split_axis=0, concat_axis=0, tiled=True)


def shards(vis_obs, uv_coords, vis_weight, block_group, tile_slot, w_plane, model_tiles, w_kernels):
    blocks = vis_obs.shape[0]
    pols = vis_obs.shape[2]
    groups = lax.axis_size(AXES)
    owned = model_tiles.shape[0]
    tile_shape = model_tiles.shape[1:]
    capacity = max(2, 2 * blocks // groups)
    early = (capacity + 1) // 2
    target = block_group[:, 0]
    markers = target[:, None] == jnp.arange(groups, dtype=jnp.int32)[None, :]
    counts = markers.astype(jnp.int32)
    before = jnp.cumsum(counts, axis=0) - counts
    rank = jnp.sum(jnp.where(markers, before, 0), axis=1)
    ranks = rank[:, None] == jnp.arange(capacity, dtype=jnp.int32)[None, :]
    wanted = jnp.sum(
        jnp.where(markers[:, :, None] & ranks[:, None, :], (tile_slot + 1)[:, None, None], 0), axis=0
    )
    own_weight = jnp.broadcast_to(jnp.sum(vis_weight)[None, None], (groups, 1))
    answers = exchange(jnp.concatenate([wanted.astype(jnp.float32), own_weight], axis=1))
    requested = answers[:, :capacity].astype(jnp.int32) - 1
    weight_sum = jnp.sum(answers[:, capacity])
    scaling = blocks * groups * vis_obs.shape[-1] / weight_sum
    scaling = scaling.reshape(1)

    left, back, right = kernel_tables(w_kernels, pols)
    is_late = rank >= early
    late = is_late.astype(jnp.int32)
    early_count = blocks - jnp.sum(late)
    late_base = (early_count + BATCH - 1) // BATCH * BATCH
    item = jnp.where(is_late, late_base + jnp.cumsum(late) - 1, jnp.cumsum(1 - late) - 1)
    items = jnp.arange(blocks + BATCH, dtype=jnp.int32)
    order = jnp.sum(
        jnp.where(items[:, None] == item[None, :], jnp.arange(blocks, dtype=jnp.int32)[None, :], 0), axis=1
    )
    slot = jnp.where(is_late, target * (capacity - early) + rank - early, target * early + rank)
    u = jnp.take(uv_coords[:, 0], order, axis=0, mode="clip")
    v = jnp.take(uv_coords[:, 1], order, axis=0, mode="clip")
    weight = jnp.take(vis_weight, order, axis=0, mode="clip")

    def send_tiles(part):
        chosen = jnp.take(model_tiles, jnp.maximum(part, 0).reshape(-1), axis=0, mode="clip")
        arrived = exchange(chosen.reshape(part.shape + tile_shape))
        return arrived.reshape((-1,) + tile_shape)

    def send_back(part):
        returned = exchange(part.reshape((groups, -1) + tile_shape))
        return returned.reshape(-1, tile_shape[0] * tile_shape[1], tile_shape[2])

    first, second = requested[:, :early], requested[:, early:]
    tiles_first = send_tiles(first)
    tiles_second = send_tiles(second)
    tables = (left, back, right)
    zero = jnp.zeros((), jnp.int32)
    residual, sent_first = process_blocks(
        blocks, zero, early_count, order, slot, w_plane, tiles_first, vis_obs, u, v, weight, *tables
    )
    late_most = blocks * (capacity - early) // capacity
    residual, sent_second = process_blocks(
        late_most,
        late_base,
        blocks - early_count,
        order,
        slot,
        w_plane,
        tiles_second,
        vis_obs,
        u,
        v,
        weight,
        *tables,
        residual,
    )
    summed = sum_tiles(first.reshape(-1), scaling, send_back(sent_first), owned)
    summed = sum_tiles(second.reshape(-1), scaling, send_back(sent_second), owned, summed)
    return residual, summed.reshape(model_tiles.shape)


def solution(mesh):
    rows = P(AXES)
    in_specs = (rows,) * 7 + (P(),)
    return jax.shard_map(shards, mesh=mesh, in_specs=in_specs, out_specs=(rows, rows), check_vma=False)
```

time: 889 us -> 429 us (0.48)
  other arithmetic: 240 us -> 18.6 us
  Pallas kernels: 0 us -> 207 us
  blocking collectives: 218 us -> 14.3 us
  matrix products: 182 us -> 0 us
  local copies, waits for them, and re-layouts: 141 us -> 70.3 us
  starting transfers between devices: 7.61 us -> 23.4 us
    pallas_call x0 -> x4, Pallas kernels: none -> 207 us  [the longest x2 200 us: process_blocks(): pl.pallas_call(functools.partial(block_kernel, aliased=aliased), out_shap...]
    psum x1 -> x0, blocking collectives: 204 us -> none  [shards(): weight_sum = lax.psum(jnp.sum(vis_weight), ('facet', 'vis'))]
    dot_general x385 -> x0, matrix products: 182 us -> none  [the longest x96 63.1 us: complex_product(): jnp.einsum(form_text, left_side[:, 1], right_side[:, 0], preferred_elemen...]
    cos x16 -> x0, other arithmetic: 117 us -> none  [phasors(): return (jnp.cos(angles), jnp.sin(angles))]
    squeeze x144 -> x1, local copies, waits for them, and re-layouts: 47 us -> 1.18 us  [shards(): v = jnp.take(uv_coords[:, 1], order, axis=0, mode='clip')]
    dynamic_update_slice x32 -> x0, other arithmetic: 39.7 us -> none  [shards(): lax.map(process, (split_blocks(tile_rows), split_blocks(kernels), split_b...]
    unnamed x13 -> x64, local copies, waits for them, and re-layouts: 2.57 us -> 31.6 us
    scatter x2 -> x0, local copies, waits for them, and re-layouts: 20.5 us -> none  [the longest x1 19.4 us: shards(): jnp.zeros((groups * capacity,) + tile_shape, jnp.float32).at[position]]
  transfers between devices with their start and end apart: 2 -> 4, of which waited for: 1 -> 2; matrix products, arithmetic and copies ran while one was open for 1% -> 12% of each run, Pallas kernels for 0% -> 47%
where the time goes in v1:
time: 429 us; the launch traced here: 427 us
  Pallas kernels  207 us (48%)
  waiting for transfers between devices  90 us (21%)
  local copies, waits for them, and re-layouts  70.3 us (16%)
  starting transfers between devices  23.4 us (5%)
  other arithmetic  18.6 us (4%)
  blocking collectives  14.3 us (3%)
    pallas_call x2, Pallas kernels, process_blocks(): pl.pallas_call(functools.partial(block_kernel, aliased=aliased), out_shap...  200 us
    all_to_all x4, waiting for transfers between devices, exchange(): lax.all_to_all(operand, AXES, split_axis=0, concat_axis=0, tiled=True)  90 us
    unnamed x64, local copies, waits for them, and re-layouts  31.6 us
    all_to_all x4, starting transfers between devices, exchange(): lax.all_to_all(operand, AXES, split_axis=0, concat_axis=0, tiled=True)  23.4 us
    all_to_all x1, blocking collectives, exchange(): lax.all_to_all(operand, AXES, split_axis=0, concat_axis=0, tiled=True)  14.3 us
  transfers between devices with their start and end apart: 4, of which 2 were waited for; matrix products, arithmetic and copies ran while one was open for 12% of the time, Pallas kernels for 47%

profile of v1, /device:TPU:0, one launch (start us, length us, event | category | flops | bytes accessed | tf_op | source)
XLA Modules:
  0.0 426.6 jit_solution(3203344292715786554)
XLA Ops:
  6.3 14.3 %all_to_all.32 = f32[32,1,9]{2,1,0:T(1,128)S(1)} all-to-all(f32[32,1,9]{2,1,0:T(1,128)S(1)} %bitcast.67), channel_id=1, replica_groups=mesh['facet'=4,'vis'=8] {'facet','vis'}, dimensions={0} | all-to-all | bytes 2304 | tf_op jit(solution)/shard_map/all_to_all | solution.py:301
  21.4 2.1 gather_fusion.4
  23.5 2.7 all-to-all-start.2
  26.4 2.1 gather_fusion
  28.5 46.7 %all-to-all-done.2 = bf16[32,4,2,32,128]{4,3,2,1,0:T(8,128)(2,1)S(1)} async-done(((bf16[32,4,2,32,128]{4,3,2,1,0:T(8,128)(2,1)}), bf16[32,4,2,32,128]{4,3,2,1,0:T(8,128)(2,1)S(1)}, u32[]{:S(2)}, u32[]{:S(2)}) %all-to-all-start.2) | async-done | bytes 2097184 | tf_op jit(solution)/shard_map/all_to_all | solution.py:301
  76.5 3.9 all-to-all-start.1
  99.0 3.1 maximum_maximum_fusion.1
  105.5 2.3 maximum_maximum_fusion
  107.8 2.8 copy.50
  110.8 2.9 gather_fusion.3
  113.8 2.5 fusion.4
  117.4 2.9 gather_fusion.2
  120.3 2.9 gather_fusion.1
  123.3 2.7 broadcast_in_dim.67
  126.0 3.6 copy.54.right_ref
  137.7 2.2 copy-done.21
  139.9 151.9 %process_blocks.2 = (f32[128,2,4,1024]{3,2,1,0:T(4,128)}, bf16[128,2,32,128]{3,2,1,0:T(8,128)(2,1)S(1)}) custom-call(s32[2]{0:T(128)S(1)} %pad_add_fusion.1.meta, s32[136]{0:T(256)S(1)} %select_reduce_fusion.1.order, s32[128]{0:T(128)S(1)} %get-tuple-element.22.slot, s32[128]{0:T(128)S(1)} %copy-done.23, bf16[128,2,32,128]{3,2,1,0:T(8,128)(2,1)S(1)} %bitcast.47, ...), custom_call_target="tpu_custom_call" | custom-call | flops 8589934592 | bytes 41943040 | tf_op jit(solution)/shard_map/process_blocks/pallas_call | solution.py:213
  294.4 12.9 %all-to-all-start.3 = ((bf16[32,4,2,32,128]{4,3,2,1,0:T(8,128)(2,1)}), bf16[32,4,2,32,128]{4,3,2,1,0:T(8,128)(2,1)S(1)}, u32[]{:S(2)}, u32[]{:S(2)}) async-start(bf16[32,4,2,32,128]{4,3,2,1,0:T(8,128)(2,1)} %bitcast.49), calls=%async_computation.3 | async-start | bytes 4194304 | tf_op jit(solution)/shard_map/all_to_all | solution.py:301
  316.0 2.2 copy-done.22
  318.2 47.7 %process_blocks.3 = (f32[128,2,4,1024]{3,2,1,0:T(4,128)}, bf16[128,2,32,128]{3,2,1,0:T(8,128)(2,1)S(1)}) custom-call(s32[2]{0:T(128)S(1)} %pad_add_fusion.meta, s32[136]{0:T(256)S(1)} %select_reduce_fusion.1.order, s32[128]{0:T(128)S(1)} %get-tuple-element.22.slot, s32[128]{0:T(128)S(1)} %copy-done.23, ...), custom_call_target="tpu_custom_call", output_to_operand_aliasing={{0}: (12, {})} | custom-call | flops 4294967296 | bytes 20971520 | tf_op jit(solution)/shard_map/process_blocks/pallas_call | solution.py:213
  367.2 3.9 all-to-all-start.4
  372.7 2.6 sum_tiles.2.refs_0_
  376.7 43.3 %all-to-all-done.4 = bf16[32,4,2,32,128]{4,3,2,1,0:T(8,128)(2,1)} async-done(((bf16[32,4,2,32,128]{4,3,2,1,0:T(8,128)(2,1)}), bf16[32,4,2,32,128]{4,3,2,1,0:T(8,128)(2,1)}, u32[]{:S(2)}, u32[]{:S(2)}) %all-to-all-start.4) | async-done | bytes 2097184 | tf_op jit(solution)/shard_map/all_to_all | solution.py:301
  421.6 5.0 %sum_tiles.3 = f32[64,64,128]{2,1,0:T(8,128)} custom-call(s32[128]{0:T(128)S(1)} %reshape.172.requested, f32[1]{0:T(128)} %bitcast.24.scale_ref, f32[64,64,128]{2,1,0:T(8,128)S(1)} %copy-done.2, bf16[128,64,128]{2,1,0:T(8,128)(2,1)} %bitcast.28.refs_1_), custom_call_target="tpu_custom_call" | custom-call | flops 1048576 | bytes 4194304 | tf_op jit(solution)/shard_map/sum_tiles/pallas_call | solution.py:264
  (108 shorter events, 54.5 us)
Async XLA Ops:
  0.6 20.8 %copy-start = (bf16[64,2,32,128]{3,2,1,0:T(8,128)(2,1)S(1)}, bf16[64,2,32,128]{3,2,1,0:T(8,128)(2,1)}, u32[]{:S(2)}) copy-start(bf16[64,2,32,128]{3,2,1,0:T(8,128)(2,1)} %param.14) | copy-start | bytes 3145732
  3.2 86.7 %copy-start.29 = (s32[128]{0:T(128)}, s32[128]{0:T(128)S(1)}, u32[]{:S(2)}) copy-start(s32[128]{0:T(128)S(1)} %select_reduce_fusion.2) | copy-start | bytes 1540
  23.5 51.7 %all-to-all-start.2 = ((bf16[32,4,2,32,128]{4,3,2,1,0:T(8,128)(2,1)}), bf16[32,4,2,32,128]{4,3,2,1,0:T(8,128)(2,1)S(1)}, u32[]{:S(2)}, u32[]{:S(2)}) async-start(bf16[32,4,2,32,128]{4,3,2,1,0:T(8,128)(2,1)} %bitcast.54), calls=%async_computation.2 | async-start | bytes 4194304 | tf_op jit(solution)/shard_map/all_to_all | solution.py:301
  75.2 1.3 copy-start.5
  76.5 216.5 %all-to-all-start.1 = ((bf16[32,4,2,32,128]{4,3,2,1,0:T(8,128)(2,1)}), bf16[32,4,2,32,128]{4,3,2,1,0:T(8,128)(2,1)S(1)}, u32[]{:S(2)}, u32[]{:S(2)}) async-start(bf16[32,4,2,32,128]{4,3,2,1,0:T(8,128)(2,1)} %bitcast.53), calls=%async_computation.1 | async-start | bytes 4194304 | tf_op jit(solution)/shard_map/all_to_all | solution.py:301
  84.7 1.7 copy-start.24
  105.4 5.2 %copy-start.28 = (s32[128,1]{0,1:T(1,128)S(1)}, s32[128,1]{0,1:T(1,128)}, u32[]{:S(2)}) copy-start(s32[128,1]{0,1:T(1,128)} %param.11) | copy-start | bytes 1540
  105.5 5.2 %copy-start.30 = (s32[128]{0:T(128)S(1)}, s32[128]{0:T(128)}, u32[]{:S(2)}) copy-start(s32[128]{0:T(128)} %copy-done.29) | copy-start | bytes 1540
  126.0 3.7 copy-start.23
  129.6 1.6 copy-start.6
  132.2 1.2 copy-start.11
  137.7 2.2 copy-start.21
  291.7 1.3 copy-start.8
  293.0 1.3 copy-start.3
  294.4 72.8 %all-to-all-start.3 = ((bf16[32,4,2,32,128]{4,3,2,1,0:T(8,128)(2,1)}), bf16[32,4,2,32,128]{4,3,2,1,0:T(8,128)(2,1)S(1)}, u32[]{:S(2)}, u32[]{:S(2)}) async-start(bf16[32,4,2,32,128]{4,3,2,1,0:T(8,128)(2,1)} %bitcast.49), calls=%async_computation.3 | async-start | bytes 4194304 | tf_op jit(solution)/shard_map/all_to_all | solution.py:301
  307.9 1.6 copy-start.4
  310.6 1.2 copy-start.12
  316.0 2.2 copy-start.22
  365.9 1.3 copy-start.7
  367.2 3.9 copy-start.27
  367.2 4.0 copy-start.26
  367.2 52.8 %all-to-all-start.4 = ((bf16[32,4,2,32,128]{4,3,2,1,0:T(8,128)(2,1)}), bf16[32,4,2,32,128]{4,3,2,1,0:T(8,128)(2,1)}, u32[]{:S(2)}, u32[]{:S(2)}) async-start(bf16[32,4,2,32,128]{4,3,2,1,0:T(8,128)(2,1)} %bitcast.48), calls=%async_computation.4 | async-start | bytes 4194304 | tf_op jit(solution)/shard_map/all_to_all | solution.py:301
  375.4 1.3 copy-start.1
  420.0 1.6 copy-start.2
  (11 other events, 11.2 us)

commit v2 on v1

v2 whole, which is shorter than its diff:
```python
import functools
import math

import jax
import jax.numpy as jnp
from jax import lax
from jax.experimental import pallas as pl
from jax.experimental.pallas import tpu as pltpu
from jax.sharding import PartitionSpec as P

AXES = ("facet", "vis")
BATCH = 8
LANES = 512
TILE = 128
UNROLL = 4
VMEM_BYTES = 60 * 1024 * 1024
SIN_TERMS = [(-1.0) ** i * (2.0 * math.pi) ** (2 * i + 1) / math.factorial(2 * i + 1) for i in range(8)]
COS_TERMS = [(-1.0) ** i * (2.0 * math.pi) ** (2 * i) / math.factorial(2 * i) for i in range(9)]


def polynomial(terms, square):
    total = jnp.full_like(square, terms[-1])
    for term in terms[-2::-1]:
        total = total * square + term
    return total


def unit_phasor(turns):
    halves = jnp.floor(turns * 2.0 + 0.5)
    part = turns - halves * 0.5
    odd = halves - 2.0 * jnp.floor(halves * 0.5)
    sign = 1.0 - 2.0 * odd
    square = part * part
    return sign * polynomial(COS_TERMS, square), -sign * part * polynomial(SIN_TERMS, square)


def phasor_powers(cosine, sine, count):
    powers = {1: (cosine, sine)}
    for j in range(2, count + 1):
        ar, ai = powers[j // 2]
        br, bi = powers[j - j // 2]
        if j % 2 == 0:
            powers[j] = (ar * ar - ai * ai, 2.0 * ar * ai)
        else:
            powers[j] = (ar * br - ai * bi, ar * bi + ai * br)
    return powers


def rows_dot(left, right, left_dim, right_dim):
    return lax.dot_general(
        left, right, (((left_dim,), (right_dim,)), ((), ())), preferred_element_type=jnp.float32
    )


def split(value):
    high = value.astype(jnp.bfloat16)
    return high, (value - high.astype(jnp.float32)).astype(jnp.bfloat16)


def block_kernel(
    meta, order, slot, plane, tiles, observed, u_ref, v_ref, w_ref, left_ref, back_ref, right_ref, turned_ref, *rest, aliased
):
    if aliased:
        rest = rest[1:]
    res, con, fu_ref, fv_ref, tile_buf, obs_buf, model_buf, grid_buf, res_buf, con_buf, in_sems, out_sems = rest
    half = fv_ref.shape[0] // 2 - 1
    width = 2 * half
    pols = obs_buf.shape[3]
    span = pols * width
    vis_count = u_ref.shape[1]
    step = pl.program_id(0)
    base, count = meta[0], meta[1]

    def block_at(at, k):
        return order[base + jnp.minimum(at * BATCH + k, count - 1)]

    def incoming(at, k):
        block = block_at(at, k)
        turn = lax.rem(at, 2)
        return (
            pltpu.make_async_copy(tiles.at[slot[block]], tile_buf.at[turn, k], in_sems.at[0, turn, k]),
            pltpu.make_async_copy(observed.at[block], obs_buf.at[turn, k], in_sems.at[1, turn, k]),
        )

    def outgoing(at, k):
        block = block_at(at, k)
        return (
            pltpu.make_async_copy(con_buf.at[k], con.at[slot[block]], out_sems.at[0, k]),
            pltpu.make_async_copy(res_buf.at[k], res.at[block], out_sems.at[1, k]),
        )

    def start_incoming(at):
        for k in range(BATCH):
            for copy in incoming(at, k):
                copy.start()

    def make_phasors():
        cosine, sine = unit_phasor(u_ref[...] * (1.0 / width))
        powers = phasor_powers(cosine, sine, half)

        def put(row, value):
            for t in range(vis_count // TILE):
                fu_ref[t, row * BATCH : (row + 1) * BATCH, :] = value[:, t * TILE : (t + 1) * TILE]

        put(0, jnp.ones_like(cosine))
        put(width, jnp.zeros_like(cosine))
        for j in range(1, half + 1):
            real, imag = powers[j]
            if j < half:
                put(j, real)
                put(width + j, imag)
            low = half if j == half else half + j
            put(low, real)
            put(width + low, -imag)
        cosine, sine = unit_phasor(v_ref[...] * (1.0 / width))
        powers = phasor_powers(cosine, sine, half)
        for j in range(1, half + 1):
            fv_ref[j], fv_ref[half + 1 + j] = powers[j]

    wide = 2 * span
    unpaired = lax.broadcasted_iota(jnp.int32, (2 * width, span), 1) < 2 * pols

    def paired(full):
        first, second = full[:, :span], full[:, span:]
        total = jnp.where(unpaired, first, first + second)
        change = jnp.where(unpaired, second, first - second)
        return jnp.concatenate([total, change], axis=1)

    def from_right(which):
        band = lax.rem(lax.broadcasted_iota(jnp.int32, (width, wide), 1), pols)
        table = right_ref[which]
        zero = jnp.zeros((), jnp.bfloat16)
        return jnp.concatenate(
            [jnp.where(band == p, table[r * width : (r + 1) * width], zero) for r in range(2) for p in range(pols)],
            axis=0,
        )

    def make_model(k):
        which = plane[block_at(step, k)]
        tile = tile_buf[lax.rem(step, 2), k].reshape(2 * width, span)
        left = rows_dot(left_ref[which], tile, 1, 0).astype(jnp.bfloat16)
        left_real, left_imag = left[:width], left[width:]
        left = jnp.concatenate(
            [jnp.concatenate([left_real, left_imag], axis=1), jnp.concatenate([-left_imag, left_real], axis=1)],
            axis=0,
        )
        model_buf[k] = paired(rows_dot(left, from_right(which), 1, 0)).astype(jnp.bfloat16)

    turn = jnp.where(lax.broadcasted_iota(jnp.int32, (2 * pols, LANES), 0) < pols, -1.0, 1.0)

    def degrid_and_grid(k):
        model = model_buf[k]
        gridded = None
        for start in range(0, vis_count, LANES):
            lanes = pl.ds(start, LANES)
            along_u = jnp.concatenate(
                [
                    fu_ref[start // TILE + t, pl.ds(k, 2 * width, stride=BATCH), :]
                    for t in range(LANES // TILE)
                ],
                axis=1,
            ).astype(jnp.bfloat16)
            spread = rows_dot(model, along_u, 0, 0).reshape(width, 2 * pols, LANES)

            def phase(index):
                return jnp.broadcast_to(fv_ref[index, pl.ds(k, 1), lanes], (2 * pols, LANES))

            cos_part = spread[0] + spread[half] * phase(half)
            sin_part = -spread[half] * phase(2 * half + 1)
            for j in range(1, half):
                cos_part = cos_part + spread[j] * phase(j)
                sin_part = sin_part + spread[half + j] * phase(half + 1 + j)
            predicted = cos_part + turn * jnp.roll(sin_part, pols, axis=0)
            given = obs_buf[lax.rem(step, 2), k, :, :, lanes]
            residual = jnp.concatenate([given[0], given[1]], axis=0) - predicted * (1.0 / width)
            res_buf[k, 0, :, lanes] = residual[:pols]
            res_buf[k, 1, :, lanes] = residual[pols:]
            scaled = residual * (w_ref[pl.ds(k, 1), lanes] * (1.0 / width))
            turned = -turn * jnp.roll(scaled, pols, axis=0)
            cos_rows, sin_rows = [scaled], [scaled * phase(half) - turned * phase(2 * half + 1)]
            for j in range(1, half):
                cos_rows.append(scaled * phase(j))
                sin_rows.append(turned * phase(half + 1 + j))
            weighted = jnp.concatenate(cos_rows + sin_rows, axis=0).astype(jnp.bfloat16)
            part = rows_dot(along_u, weighted, 1, 1)
            gridded = part if gridded is None else gridded + part
        grid_buf[k] = gridded

    def make_contribution(k):
        which = plane[block_at(step, k)]
        back = rows_dot(jnp.concatenate(split(paired(grid_buf[k])), axis=0), turned_ref[which], 1, 0)
        back = back[: 2 * width] + back[2 * width :]
        back_real = back[:width, :span] + back[width:, span:]
        back_imag = back[:width, span:] - back[width:, :span]
        back = jnp.concatenate([back_real, back_imag], axis=0)
        result = rows_dot(back_ref[which], jnp.concatenate(split(back), axis=1), 1, 0)
        result = result[:, :span] + result[:, span:]
        con_buf[k] = result.astype(con_buf.dtype).reshape(con_buf.shape[1:])

    @pl.when(step * BATCH < count)
    def _():
        @pl.when(step == 0)
        def _():
            start_incoming(step)

        @pl.when((step + 1) * BATCH < count)
        def _():
            start_incoming(step + 1)

        make_phasors()
        for k in range(BATCH):
            for copy in incoming(step, k):
                copy.wait()
        for k in range(BATCH):
            make_model(k)

        @pl.when(step > 0)
        def _():
            for k in range(BATCH):
                for copy in outgoing(step - 1, k):
                    copy.wait()

        @pl.loop(0, BATCH // UNROLL)
        def _(i):
            for k in range(UNROLL):
                degrid_and_grid(i * UNROLL + k)

        for k in range(BATCH):
            make_contribution(k)
        last = (step + 1) * BATCH >= count
        for k in range(BATCH):

            @pl.when(step * BATCH + k < count)
            def _():
                for copy in outgoing(step, k):
                    copy.start()

        for k in range(BATCH):

            @pl.when(last & (step * BATCH + k < count))
            def _():
                for copy in outgoing(step, k):
                    copy.wait()


def process_blocks(most, base, count, order, slot, plane, tiles, observed, u, v, weight, tables, old=None):
    pols, vis_count = observed.shape[2:]
    width = tiles.shape[2]
    meta = jnp.stack([base, count]).astype(jnp.int32)

    def by_batch(i, meta, order, slot, plane):
        return (lax.div(meta[0] + jnp.minimum(i * BATCH, jnp.maximum(meta[1] - 1, 0)), BATCH), 0)

    def whole(i, meta, order, slot, plane):
        return (0, 0, 0)

    row_spec = pl.BlockSpec((BATCH, vis_count), by_batch)
    hbm = pl.BlockSpec(memory_space=pl.ANY)
    operands = [tiles, observed, u, v, weight, *tables]
    in_specs = [hbm, hbm, row_spec, row_spec, row_spec] + [
        pl.BlockSpec(table.shape, whole) for table in tables
    ]
    aliases = {}
    if old is not None:
        operands.append(old)
        in_specs.append(hbm)
        aliases = {len(operands) + 3: 0}
    tile_shape, vis_shape = tiles.shape[1:], observed.shape[1:]
    return pl.pallas_call(
        functools.partial(block_kernel, aliased=old is not None),
        out_shape=(
            jax.ShapeDtypeStruct(observed.shape, jnp.float32),
            jax.ShapeDtypeStruct(tiles.shape, jnp.bfloat16),
        ),
        grid_spec=pltpu.PrefetchScalarGridSpec(
            num_scalar_prefetch=4,
            grid=((most + BATCH - 1) // BATCH,),
            in_specs=in_specs,
            out_specs=(hbm, hbm),
            scratch_shapes=[
                pltpu.VMEM((vis_count // TILE, BATCH * 2 * width, TILE), jnp.float32),
                pltpu.VMEM((width + 2, BATCH, vis_count), jnp.float32),
                pltpu.VMEM((2, BATCH) + tile_shape, jnp.bfloat16),
                pltpu.VMEM((2, BATCH) + vis_shape, jnp.float32),
                pltpu.VMEM((BATCH, 2 * width, 2 * pols * width), jnp.bfloat16),
                pltpu.VMEM((BATCH, 2 * width, 2 * pols * width), jnp.float32),
                pltpu.VMEM((BATCH,) + vis_shape, jnp.float32),
                pltpu.VMEM((BATCH,) + tile_shape, jnp.bfloat16),
                pltpu.SemaphoreType.DMA((2, 2, BATCH)),
                pltpu.SemaphoreType.DMA((2, BATCH)),
            ],
        ),
        input_output_aliases=aliases,
        compiler_params=pltpu.CompilerParams(vmem_limit_bytes=VMEM_BYTES),
        cost_estimate=pl.CostEstimate(
            flops=most * 2 * 2 * 2 * width * 2 * pols * width * vis_count,
            bytes_accessed=most * 2 * pols * vis_count * 40,
            transcendentals=0,
        ),
        name="process_blocks",
    )(meta, order, slot, plane, *operands)


def sum_kernel(requested, scale_ref, *refs, last):
    if last:
        old_ref, arrived_ref, out_ref = refs
        out_ref[...] = old_ref[...]
    else:
        arrived_ref, out_ref = refs
        out_ref[...] = jnp.zeros_like(out_ref)

    @pl.loop(0, arrived_ref.shape[0])
    def _(i):
        tile = requested[i]

        @pl.when(tile >= 0)
        def _():
            out_ref[tile] += arrived_ref[i].astype(jnp.float32)

    if last:
        out_ref[...] = out_ref[...] * scale_ref[0]


def sum_tiles(requested, scale, arrived, owned, old=None):
    shape = (owned,) + arrived.shape[1:]
    operands = [arrived] if old is None else [old, arrived]
    vmem = pl.BlockSpec(memory_space=pltpu.VMEM)
    return pl.pallas_call(
        functools.partial(sum_kernel, last=old is not None),
        out_shape=jax.ShapeDtypeStruct(shape, jnp.float32),
        in_specs=[pl.BlockSpec(memory_space=pltpu.SMEM)] * 2 + [vmem] * len(operands),
        out_specs=vmem,
        compiler_params=pltpu.CompilerParams(vmem_limit_bytes=VMEM_BYTES),
        cost_estimate=pl.CostEstimate(flops=arrived.size, bytes_accessed=arrived.size * 4, transcendentals=0),
        name="sum_tiles",
    )(requested, scale, *operands)


def kernel_tables(w_kernels, pols):
    planes, _, width, _ = w_kernels.shape
    half = width // 2
    real, imag = w_kernels[:, 0], w_kernels[:, 1]

    def offsets(table):
        return jnp.concatenate([table[:, half:], table[:, :1], table[:, half - 1 : 0 : -1]], axis=1)

    real_rows, imag_rows = offsets(real), offsets(imag)
    left = jnp.concatenate(
        [jnp.concatenate([real_rows, -imag_rows], axis=2), jnp.concatenate([imag_rows, real_rows], axis=2)], axis=1
    )
    back = jnp.swapaxes(left, 1, 2)
    real_columns, imag_columns = jnp.swapaxes(real_rows, 1, 2), jnp.swapaxes(imag_rows, 1, 2)
    right = jnp.concatenate(
        [
            jnp.stack([real_columns, imag_columns], axis=3),
            jnp.stack([-imag_columns, real_columns], axis=3),
        ],
        axis=1,
    )
    columns = jnp.swapaxes(right.reshape(planes, 2 * width, 2 * width), 1, 2).reshape(planes, 2 * width, 1, 2, 1, width)
    same = jnp.eye(pols, dtype=jnp.bool_).reshape(1, 1, pols, 1, pols, 1)
    turned = jnp.where(same, columns, jnp.zeros((), columns.dtype))
    turned = turned.reshape(planes, 2 * width * pols, 2 * width * pols)
    right = jnp.broadcast_to(right[..., None], right.shape + (pols,)).reshape(planes, 2 * width, 2 * width * pols)
    return left, back, right, turned


def exchange(operand):
    return lax.all_to_all(operand, AXES, split_axis=0, concat_axis=0, tiled=True)


def shards(vis_obs, uv_coords, vis_weight, block_group, tile_slot, w_plane, model_tiles, w_kernels):
    blocks = vis_obs.shape[0]
    pols = vis_obs.shape[2]
    groups = lax.axis_size(AXES)
    owned = model_tiles.shape[0]
    tile_shape = model_tiles.shape[1:]
    capacity = max(2, 2 * blocks // groups)
    early = max(1, 3 * capacity // 8)
    target = block_group[:, 0]
    markers = target[:, None] == jnp.arange(groups, dtype=jnp.int32)[None, :]
    counts = markers.astype(jnp.int32)
    before = jnp.cumsum(counts, axis=0) - counts
    rank = jnp.sum(jnp.where(markers, before, 0), axis=1)
    ranks = rank[:, None] == jnp.arange(capacity, dtype=jnp.int32)[None, :]
    wanted = jnp.sum(
        jnp.where(markers[:, :, None] & ranks[:, None, :], (tile_slot + 1)[:, None, None], 0), axis=0
    )
    own_weight = jnp.broadcast_to(jnp.sum(vis_weight)[None, None], (groups, 1))
    answers = exchange(jnp.concatenate([wanted.astype(jnp.float32), own_weight], axis=1))
    requested = answers[:, :capacity].astype(jnp.int32) - 1
    weight_sum = jnp.sum(answers[:, capacity])
    scaling = blocks * groups * vis_obs.shape[-1] / weight_sum
    scaling = scaling.reshape(1)

    tables = kernel_tables(w_kernels, pols)
    is_late = rank >= early
    late = is_late.astype(jnp.int32)
    early_count = blocks - jnp.sum(late)
    late_base = (early_count + BATCH - 1) // BATCH * BATCH
    item = jnp.where(is_late, late_base + jnp.cumsum(late) - 1, jnp.cumsum(1 - late) - 1)
    items = jnp.arange(blocks + BATCH, dtype=jnp.int32)
    order = jnp.sum(
        jnp.where(items[:, None] == item[None, :], jnp.arange(blocks, dtype=jnp.int32)[None, :], 0), axis=1
    )
    slot = jnp.where(is_late, target * (capacity - early) + rank - early, target * early + rank)
    u = jnp.take(uv_coords[:, 0], order, axis=0, mode="clip")
    v = jnp.take(uv_coords[:, 1], order, axis=0, mode="clip")
    weight = jnp.take(vis_weight, order, axis=0, mode="clip")

    def choose(part):
        chosen = jnp.take(model_tiles, jnp.maximum(part, 0).reshape(-1), axis=0, mode="clip")
        return chosen.reshape(part.shape + tile_shape)

    def send_tiles(chosen):
        return exchange(chosen).reshape((-1,) + tile_shape)

    def send_back(part):
        returned = exchange(part.reshape((groups, -1) + tile_shape))
        return returned.reshape(-1, tile_shape[0] * tile_shape[1], tile_shape[2])

    first, second = requested[:, :early], requested[:, early:]
    tiles_first = send_tiles(choose(first))
    chosen, order, slot, u, v, weight, tables = lax.optimization_barrier(
        (choose(second), order, slot, u, v, weight, tables)
    )
    tiles_second = send_tiles(chosen)
    given = (vis_obs, u, v, weight, tables)
    zero = jnp.zeros((), jnp.int32)
    residual, sent_first = process_blocks(
        blocks, zero, early_count, order, slot, w_plane, tiles_first, *given
    )
    late_most = blocks * (capacity - early) // capacity
    residual, sent_second = process_blocks(
        late_most, late_base, blocks - early_count, order, slot, w_plane, tiles_second, *given, residual
    )
    summed = sum_tiles(first.reshape(-1), scaling, send_back(sent_first), owned)
    summed = sum_tiles(second.reshape(-1), scaling, send_back(sent_second), owned, summed)
    return residual, summed.reshape(model_tiles.shape)


def solution(mesh):
    rows = P(AXES)
    in_specs = (rows,) * 7 + (P(),)
    return jax.shard_map(shards, mesh=mesh, in_specs=in_specs, out_specs=(rows, rows), check_vma=False)
```

time: 429 us -> 288 us (0.67)
  Pallas kernels: 207 us -> 115 us
  waiting for transfers between devices: 90 us -> 58.8 us
  blocking collectives: 14.3 us -> 0 us
  local copies, waits for them, and re-layouts: 70.3 us -> 59.2 us
  starting transfers between devices: 23.4 us -> 32.6 us
    pallas_call x2, Pallas kernels: 200 us -> 104 us  [process_blocks(): pl.pallas_call(functools.partial(block_kernel, aliased=old is not None),...]
    broadcast_in_dim x2 -> x7, local copies, waits for them, and re-layouts: 0.2 us -> 32.8 us  [the longest x5 32.6 us: kernel_tables(): turned = jnp.where(same, columns, jnp.zeros((), columns.dtype))]
    all_to_all x4 -> x5, waiting for transfers between devices: 90 us -> 58.8 us  [exchange(): lax.all_to_all(operand, AXES, split_axis=0, concat_axis=0, tiled=True)]
    unnamed x64 -> x34, local copies, waits for them, and re-layouts: 31.6 us -> 1.55 us
    all_to_all x1 -> x0, blocking collectives: 14.3 us -> none  [exchange(): lax.all_to_all(operand, AXES, split_axis=0, concat_axis=0, tiled=True)]
    all_to_all x4 -> x5, starting transfers between devices: 23.4 us -> 32.6 us  [exchange(): lax.all_to_all(operand, AXES, split_axis=0, concat_axis=0, tiled=True)]
    select_n x0 -> x1, other arithmetic: none -> 4.42 us  [kernel_tables(): turned = jnp.where(same, columns, jnp.zeros((), columns.dtype))]
  transfers between devices with their start and end apart: 4 -> 5, of which waited for: 2 -> 2; matrix products, arithmetic and copies ran while one was open for 12% -> 23% of each run, Pallas kernels for 47% -> 38%
where the time goes in v2:
time: 288 us; the launch traced here: 286 us
  Pallas kernels  115 us (40%)
  local copies, waits for them, and re-layouts  59.2 us (21%)
  waiting for transfers between devices  58.8 us (20%)
  starting transfers between devices  32.6 us (11%)
  other arithmetic  17.2 us (6%)
  between operations  3.31 us (1%)
    pallas_call x2, Pallas kernels, process_blocks(): pl.pallas_call(functools.partial(block_kernel, aliased=old is not None),...  104 us
    all_to_all x5, waiting for transfers between devices, exchange(): lax.all_to_all(operand, AXES, split_axis=0, concat_axis=0, tiled=True)  58.8 us
    broadcast_in_dim x5, local copies, waits for them, and re-layouts, kernel_tables(): turned = jnp.where(same, columns, jnp.zeros((), columns.dtype))  32.6 us
    all_to_all x5, starting transfers between devices, exchange(): lax.all_to_all(operand, AXES, split_axis=0, concat_axis=0, tiled=True)  32.6 us
    pallas_call x2, Pallas kernels, sum_tiles(): pl.pallas_call(functools.partial(sum_kernel, last=old is not None), out_s...  10.9 us
  transfers between devices with their start and end apart: 5, of which 2 were waited for; matrix products, arithmetic and copies ran while one was open for 23% of the time, Pallas kernels for 38%

profile of v2, /device:TPU:0, one launch (start us, length us, event | category | flops | bytes accessed | tf_op | source)
XLA Modules:
  0.0 286.3 jit_solution(10832464029262774451)
XLA Ops:
  3.9 1.8 reduce_sum.57
  6.9 7.3 %all-to-all-start = ((f32[32,1,9]{2,1,0:T(1,128)}), f32[32,1,9]{2,1,0:T(1,128)S(1)}, u32[]{:S(2)}, u32[]{:S(2)}) async-start(f32[32,1,9]{2,1,0:T(1,128)} %bitcast.4), calls=%async_computation | async-start | bytes 32768 | tf_op jit(solution)/shard_map/all_to_all | solution.py:369
  15.3 6.0 %all-to-all-done = f32[32,1,9]{2,1,0:T(1,128)S(1)} async-done(((f32[32,1,9]{2,1,0:T(1,128)}), f32[32,1,9]{2,1,0:T(1,128)S(1)}, u32[]{:S(2)}, u32[]{:S(2)}) %all-to-all-start) | async-done | bytes 1184 | tf_op jit(solution)/shard_map/all_to_all | solution.py:369
  21.4 1.9 gather_fusion.4
  23.4 3.4 %all-to-all-start.2 = ((bf16[32,3,2,32,128]{4,3,2,1,0:T(8,128)(2,1)}), bf16[32,3,2,32,128]{4,3,2,1,0:T(8,128)(2,1)}, u32[]{:S(2)}, u32[]{:S(2)}) async-start(bf16[32,3,2,32,128]{4,3,2,1,0:T(8,128)(2,1)} %bitcast.25), calls=%async_computation.2 | async-start | bytes 3145728 | tf_op jit(solution)/shard_map/all_to_all | solution.py:369
  31.3 1.6 gather_fusion.3
  32.9 2.5 fusion.4
  35.6 1.6 gather_fusion.1
  37.2 1.6 gather_fusion.2
  43.2 2.3 copy.59
  45.6 6.1 %broadcast_in_dim.101 = bf16[32,64,4,2,4,32]{5,4,3,2,1,0:T(4,128)(2,1)} broadcast(bf16[32,64,2,32]{3,2,1,0:T(2,128)(2,1)S(1)} %copy.59), dimensions={0,1,3,5} | broadcast | bytes 4456448 | tf_op jit(solution)/shard_map/jit(_where)/broadcast_in_dim | solution.py:362
  51.7 23.5 %broadcast_in_dim.102 = bf16[32,256,256]{2,1,0:T(8,128)(2,1)} reshape(bf16[32,64,4,2,4,32]{5,4,3,2,1,0:T(4,128)(2,1)} %broadcast_in_dim.101) | data formatting | bytes 8388608 | tf_op jit(solution)/shard_map/jit(_where)/broadcast_in_dim | solution.py:362
  75.9 1.7 maximum_maximum_fusion.1
  77.5 4.4 %broadcast_select_fusion.turned_ref = bf16[32,256,256]{2,1,0:T(8,128)(2,1)} fusion(bf16[32,256,256]{2,1,0:T(8,128)(2,1)} %broadcast_in_dim.102, pred[256,256]{1,0:T(8,128)(4,1)S(1)} %broadcast_in_dim.98), kind=kLoop, calls=%fused_computation.5 | loop fusion | flops 2097152 | bytes 8454144 | tf_op jit(solution)/shard_map/jit(_where)/select_n | solution.py:362
  82.2 2.6 gather_fusion
  86.1 6.1 %all-to-all-start.1 = ((bf16[32,5,2,32,128]{4,3,2,1,0:T(8,128)(2,1)}), bf16[32,5,2,32,128]{4,3,2,1,0:T(8,128)(2,1)}, u32[]{:S(2)}, u32[]{:S(2)}) async-start(bf16[32,5,2,32,128]{4,3,2,1,0:T(8,128)(2,1)} %bitcast.49), calls=%async_computation.1 | async-start | bytes 5242880 | tf_op jit(solution)/shard_map/all_to_all | solution.py:369
  93.6 2.5 copy.63.right_ref
  97.1 66.2 %process_blocks.2 = (f32[128,2,4,1024]{3,2,1,0:T(4,128)}, bf16[96,2,32,128]{3,2,1,0:T(8,128)(2,1)}) custom-call(s32[2]{0:T(128)} %pad_add_fusion.1.meta, s32[136]{0:T(256)} %copy-done.15, s32[128]{0:T(128)} %get-tuple-element.17.slot, s32[128]{0:T(128)} %plane.3, bf16[96,2,32,128]{3,2,1,0:T(8,128)(2,1)} %bitcast.26.tiles, f32[128,2,4,1024]{3,2,1,0:T(4,128)} %observed.3, ...), custom_call_target="tpu_custom_call" | custom-call | flops 8589934592 | bytes 41943040 | tf_op jit(solution)/shard_map/process_blocks/pallas_call | solution.py:269
  163.3 9.8 %all-to-all-start.3 = ((bf16[32,3,2,32,128]{4,3,2,1,0:T(8,128)(2,1)}), bf16[32,3,2,32,128]{4,3,2,1,0:T(8,128)(2,1)S(1)}, u32[]{:S(2)}, u32[]{:S(2)}) async-start(bf16[32,3,2,32,128]{4,3,2,1,0:T(8,128)(2,1)} %bitcast.67), calls=%async_computation.3 | async-start | bytes 3145728 | tf_op jit(solution)/shard_map/all_to_all | solution.py:369
  174.4 38.2 %process_blocks.3 = (f32[128,2,4,1024]{3,2,1,0:T(4,128)}, bf16[160,2,32,128]{3,2,1,0:T(8,128)(2,1)}) custom-call(s32[2]{0:T(128)} %pad_add_fusion.meta, s32[136]{0:T(256)} %copy-done.15, s32[128]{0:T(128)} %get-tuple-element.17.slot, s32[128]{0:T(128)} %plane.3, bf16[160,2,32,128]{3,2,1,0:T(8,128)(2,1)} %bitcast.23.tiles, ...), custom_call_target="tpu_custom_call", output_to_operand_aliasing={{0}: (13, {})} | custom-call | flops 5368709120 | bytes 26214400 | tf_op jit(solution)/shard_map/process_blocks/pallas_call | solution.py:269
  213.8 6.0 %all-to-all-start.4 = ((bf16[32,5,2,32,128]{4,3,2,1,0:T(8,128)(2,1)}), bf16[32,5,2,32,128]{4,3,2,1,0:T(8,128)(2,1)}, u32[]{:S(2)}, u32[]{:S(2)}) async-start(bf16[32,5,2,32,128]{4,3,2,1,0:T(8,128)(2,1)} %bitcast.61), calls=%async_computation.4 | async-start | bytes 5242880 | tf_op jit(solution)/shard_map/all_to_all | solution.py:369
  222.7 4.5 %sum_tiles.2.refs_0_ = f32[64,64,128]{2,1,0:T(8,128)} custom-call(s32[96]{0:T(128)} %reshape.191.requested, f32[1]{0:T(128)} %bitcast.27.scale_ref, bf16[96,64,128]{2,1,0:T(8,128)(2,1)} %bitcast.59), custom_call_target="tpu_custom_call" | custom-call | flops 786432 | bytes 3145728 | tf_op jit(solution)/shard_map/sum_tiles/pallas_call | solution.py:328
  227.2 52.8 %all-to-all-done.4 = bf16[32,5,2,32,128]{4,3,2,1,0:T(8,128)(2,1)} async-done(((bf16[32,5,2,32,128]{4,3,2,1,0:T(8,128)(2,1)}), bf16[32,5,2,32,128]{4,3,2,1,0:T(8,128)(2,1)}, u32[]{:S(2)}, u32[]{:S(2)}) %all-to-all-start.4) | async-done | bytes 2621472 | tf_op jit(solution)/shard_map/all_to_all | solution.py:369
  279.9 6.3 %sum_tiles.3 = f32[64,64,128]{2,1,0:T(8,128)} custom-call(s32[160]{0:T(256)} %reshape.189.requested, f32[1]{0:T(128)} %bitcast.27.scale_ref, f32[64,64,128]{2,1,0:T(8,128)} %sum_tiles.2.refs_0_, bf16[160,64,128]{2,1,0:T(8,128)(2,1)} %bitcast.31.refs_1_), custom_call_target="tpu_custom_call" | custom-call | flops 1310720 | bytes 5242880 | tf_op jit(solution)/shard_map/sum_tiles/pallas_call | solution.py:328
  (88 shorter events, 22.2 us)
Async XLA Ops:
  0.6 20.8 %copy-start = (bf16[64,2,32,128]{3,2,1,0:T(8,128)(2,1)S(1)}, bf16[64,2,32,128]{3,2,1,0:T(8,128)(2,1)}, u32[]{:S(2)}) copy-start(bf16[64,2,32,128]{3,2,1,0:T(8,128)(2,1)} %param.14) | copy-start | bytes 3145732
  6.9 14.4 %all-to-all-start = ((f32[32,1,9]{2,1,0:T(1,128)}), f32[32,1,9]{2,1,0:T(1,128)S(1)}, u32[]{:S(2)}, u32[]{:S(2)}) async-start(f32[32,1,9]{2,1,0:T(1,128)} %bitcast.4), calls=%async_computation | async-start | bytes 32768 | tf_op jit(solution)/shard_map/all_to_all | solution.py:369
  23.4 62.7 %all-to-all-start.2 = ((bf16[32,3,2,32,128]{4,3,2,1,0:T(8,128)(2,1)}), bf16[32,3,2,32,128]{4,3,2,1,0:T(8,128)(2,1)}, u32[]{:S(2)}, u32[]{:S(2)}) async-start(bf16[32,3,2,32,128]{4,3,2,1,0:T(8,128)(2,1)} %bitcast.25), calls=%async_computation.2 | async-start | bytes 3145728 | tf_op jit(solution)/shard_map/all_to_all | solution.py:369
  26.8 3.8 %copy-start.14 = (s32[128,1]{0,1:T(1,128)S(1)}, s32[128,1]{0,1:T(1,128)}, u32[]{:S(2)}) copy-start(s32[128,1]{0,1:T(1,128)} %param.11) | copy-start | bytes 1540
  26.8 4.5 %copy-start.2 = (f32[128,1024]{1,0:T(8,128)S(1)}, f32[128,1024]{1,0:T(8,128)}, u32[]{:S(2)}) copy-start(f32[128,1024]{1,0:T(8,128)} %param.10) | copy-start | bytes 1572868
  29.9 10.4 %copy-start.7 = (bf16[32,16,32]{1,2,0:T(8,128)(2,1)}, bf16[32,16,32]{1,2,0:T(8,128)(2,1)S(1)}, u32[]{:S(2)}) copy-start(bf16[32,16,32]{1,2,0:T(8,128)(2,1)S(1)} %slice.68) | copy-start | bytes 98308
  31.3 1.7 copy-start.15
  37.2 1.8 copy-start.13
  39.1 1.5 copy-start.5
  39.2 1.3 copy-start.9
  41.8 9.9 %copy-start.4 = (bf16[32,64,32,2]{1,0,3,2:T(8,128)(2,1)}, bf16[32,64,32,2]{1,0,3,2:T(8,128)(2,1)S(1)}, u32[]{:S(2)}) copy-start(bf16[32,64,32,2]{1,0,3,2:T(8,128)(2,1)S(1)} %copy.56) | copy-start | bytes 786436
  51.7 24.2 %copy-start.6 = (bf16[32,15,32]{1,2,0:T(8,128)(2,1)S(1)}, bf16[32,15,32]{1,2,0:T(8,128)(2,1)}, u32[]{:S(2)}) copy-start(bf16[32,15,32]{1,2,0:T(8,128)(2,1)} %copy-done.5) | copy-start | bytes 92164
  51.7 24.2 %copy-start.8 = (bf16[32,16,32]{1,2,0:T(8,128)(2,1)S(1)}, bf16[32,16,32]{1,2,0:T(8,128)(2,1)}, u32[]{:S(2)}) copy-start(bf16[32,16,32]{1,2,0:T(8,128)(2,1)} %copy-done.7) | copy-start | bytes 98308
  51.7 24.2 %copy-start.10 = (bf16[32,15,32]{1,2,0:T(8,128)(2,1)S(1)}, bf16[32,15,32]{1,2,0:T(8,128)(2,1)}, u32[]{:S(2)}) copy-start(bf16[32,15,32]{1,2,0:T(8,128)(2,1)} %copy-done.9) | copy-start | bytes 92164
  51.7 24.2 %copy-start.12 = (bf16[32,32,32]{1,2,0:T(8,128)(2,1)S(1)}, bf16[32,32,32]{1,2,0:T(8,128)(2,1)}, u32[]{:S(2)}) copy-start(bf16[32,32,32]{1,2,0:T(8,128)(2,1)} %neg.6) | copy-start | bytes 196612
  86.1 77.2 %all-to-all-start.1 = ((bf16[32,5,2,32,128]{4,3,2,1,0:T(8,128)(2,1)}), bf16[32,5,2,32,128]{4,3,2,1,0:T(8,128)(2,1)}, u32[]{:S(2)}, u32[]{:S(2)}) async-start(bf16[32,5,2,32,128]{4,3,2,1,0:T(8,128)(2,1)} %bitcast.49), calls=%async_computation.1 | async-start | bytes 5242880 | tf_op jit(solution)/shard_map/all_to_all | solution.py:369
  92.2 3.9 %copy-start.11 = (bf16[32,64,64]{1,2,0:T(8,128)(2,1)S(1)}, bf16[32,64,64]{1,2,0:T(8,128)(2,1)}, u32[]{:S(2)}) copy-start(bf16[32,64,64]{1,2,0:T(8,128)(2,1)} %maximum_maximum_fusion.1) | copy-start | bytes 786436
  163.3 49.3 %all-to-all-start.3 = ((bf16[32,3,2,32,128]{4,3,2,1,0:T(8,128)(2,1)}), bf16[32,3,2,32,128]{4,3,2,1,0:T(8,128)(2,1)S(1)}, u32[]{:S(2)}, u32[]{:S(2)}) async-start(bf16[32,3,2,32,128]{4,3,2,1,0:T(8,128)(2,1)} %bitcast.67), calls=%async_computation.3 | async-start | bytes 3145728 | tf_op jit(solution)/shard_map/all_to_all | solution.py:369
  212.6 1.1 copy-start.3
  213.8 66.2 %all-to-all-start.4 = ((bf16[32,5,2,32,128]{4,3,2,1,0:T(8,128)(2,1)}), bf16[32,5,2,32,128]{4,3,2,1,0:T(8,128)(2,1)}, u32[]{:S(2)}, u32[]{:S(2)}) async-start(bf16[32,5,2,32,128]{4,3,2,1,0:T(8,128)(2,1)} %bitcast.61), calls=%async_computation.4 | async-start | bytes 5242880 | tf_op jit(solution)/shard_map/all_to_all | solution.py:369
  279.9 6.3 %copy-start.1 = (bf16[64,2,32,128]{3,2,1,0:T(8,128)(2,1)S(1)}, bf16[64,2,32,128]{3,2,1,0:T(8,128)(2,1)}, u32[]{:S(2)}) copy-start(bf16[64,2,32,128]{3,2,1,0:T(8,128)(2,1)} %param.14) | copy-start | bytes 3145732

commit v3 on v2

--- a/solution.py
+++ b/solution.py
@@ -3,12 +3,13 @@
 
 import jax
 import jax.numpy as jnp
+import numpy as np
 from jax import lax
 from jax.experimental import pallas as pl
 from jax.experimental.pallas import tpu as pltpu
+from jax.sharding import Mesh
 from jax.sharding import PartitionSpec as P
 
-AXES = ("facet", "vis")
 BATCH = 8
 LANES = 512
 TILE = 128
@@ -58,11 +59,9 @@
 
 
 def block_kernel(
-    meta, order, slot, plane, tiles, observed, u_ref, v_ref, w_ref, left_ref, back_ref, right_ref, turned_ref, *rest, aliased
+    meta, order, slot, plane, tiles, observed, u_ref, v_ref, w_ref, left_ref, back_ref, right_ref, turned_ref, *rest, carried
 ):
-    if aliased:
-        rest = rest[1:]
-    res, con, fu_ref, fv_ref, tile_buf, obs_buf, model_buf, grid_buf, res_buf, con_buf, in_sems, out_sems = rest
+    res, con, fu_ref, fv_ref, tile_buf, obs_buf, model_buf, grid_buf, res_buf, con_buf, in_sems, out_sems = rest[carried:]
     half = fv_ref.shape[0] // 2 - 1
     width = 2 * half
     pols = obs_buf.shape[3]
@@ -243,7 +242,7 @@
                     copy.wait()
 
 
-def process_blocks(most, base, count, order, slot, plane, tiles, observed, u, v, weight, tables, old=None):
+def process_blocks(most, base, count, order, slot, plane, tiles, observed, u, v, weight, tables, carried=()):
     pols, vis_count = observed.shape[2:]
     width = tiles.shape[2]
     meta = jnp.stack([base, count]).astype(jnp.int32)
@@ -260,14 +259,12 @@
     in_specs = [hbm, hbm, row_spec, row_spec, row_spec] + [
         pl.BlockSpec(table.shape, whole) for table in tables
     ]
-    aliases = {}
-    if old is not None:
-        operands.append(old)
-        in_specs.append(hbm)
-        aliases = {len(operands) + 3: 0}
+    aliases = {len(operands) + 4 + i: i for i in range(len(carried))}
+    operands += carried
+    in_specs += [hbm] * len(carried)
     tile_shape, vis_shape = tiles.shape[1:], observed.shape[1:]
     return pl.pallas_call(
-        functools.partial(block_kernel, aliased=old is not None),
+        functools.partial(block_kernel, carried=len(carried)),
         out_shape=(
             jax.ShapeDtypeStruct(observed.shape, jnp.float32),
             jax.ShapeDtypeStruct(tiles.shape, jnp.bfloat16),
@@ -301,13 +298,8 @@
     )(meta, order, slot, plane, *operands)
 
 
-def sum_kernel(requested, scale_ref, *refs, last):
-    if last:
-        old_ref, arrived_ref, out_ref = refs
-        out_ref[...] = old_ref[...]
-    else:
-        arrived_ref, out_ref = refs
-        out_ref[...] = jnp.zeros_like(out_ref)
+def sum_kernel(requested, arrived_ref, out_ref, total_ref):
+    total_ref[...] = jnp.zeros_like(total_ref)
 
     @pl.loop(0, arrived_ref.shape[0])
     def _(i):
@@ -315,131 +307,173 @@
 
         @pl.when(tile >= 0)
         def _():
-            out_ref[tile] += arrived_ref[i].astype(jnp.float32)
-
-    if last:
-        out_ref[...] = out_ref[...] * scale_ref[0]
-
-
-def sum_tiles(requested, scale, arrived, owned, old=None):
+            total_ref[tile] += arrived_ref[i].astype(jnp.float32)
+
+    out_ref[...] = total_ref[...].astype(out_ref.dtype)
+
+
+def sum_tiles(requested, arrived, owned, dtype):
     shape = (owned,) + arrived.shape[1:]
-    operands = [arrived] if old is None else [old, arrived]
     vmem = pl.BlockSpec(memory_space=pltpu.VMEM)
     return pl.pallas_call(
-        functools.partial(sum_kernel, last=old is not None),
-        out_shape=jax.ShapeDtypeStruct(shape, jnp.float32),
-        in_specs=[pl.BlockSpec(memory_space=pltpu.SMEM)] * 2 + [vmem] * len(operands),
+        sum_kernel,
+        out_shape=jax.ShapeDtypeStruct(shape, dtype),
+        in_specs=[pl.BlockSpec(memory_space=pltpu.SMEM), vmem],
         out_specs=vmem,
+        scratch_shapes=[pltpu.VMEM(shape, jnp.float32)],
         compiler_params=pltpu.CompilerParams(vmem_limit_bytes=VMEM_BYTES),
         cost_estimate=pl.CostEstimate(flops=arrived.size, bytes_accessed=arrived.size * 4, transcendentals=0),
         name="sum_tiles",
-    )(requested, scale, *operands)
+    )(requested, arrived)
+
+
+def table_kernel(planes_ref, signs_ref, spread_ref, gather_ref, repeat_ref, left_ref, back_ref, right_ref, turned_ref):
+    size = left_ref.shape[1]
+    wide = right_ref.shape[2]
+    pols = wide // size
+    row = lax.rem(lax.broadcasted_iota(jnp.int32, (wide, wide), 0), pols)
+    column = lax.rem(lax.div(lax.broadcasted_iota(jnp.int32, (wide, wide), 1), size // 2), pols)
+    same = row == column
+    zero = jnp.zeros((), jnp.bfloat16)
+
+    def exact(left, right, left_dim=1):
+        return rows_dot(left, right, left_dim, 0).astype(jnp.bfloat16)
+
+    for k in range(planes_ref.shape[0]):
+        both = exact(signs_ref[...], planes_ref[k])
+        left = jnp.concatenate([both[:size], both[size:]], axis=1)
+        left_ref[k] = left
+        back = exact(left, jnp.eye(size, dtype=jnp.bfloat16), 0)
+        back_ref[k] = back
+        right_ref[k] = exact(back, spread_ref[...])
+        turned_ref[k] = jnp.where(same, exact(exact(gather_ref[...], left), repeat_ref[...]), zero)
 
 
 def kernel_tables(w_kernels, pols):
     planes, _, width, _ = w_kernels.shape
     half = width // 2
-    real, imag = w_kernels[:, 0], w_kernels[:, 1]
-
-    def offsets(table):
-        return jnp.concatenate([table[:, half:], table[:, :1], table[:, half - 1 : 0 : -1]], axis=1)
-
-    real_rows, imag_rows = offsets(real), offsets(imag)
-    left = jnp.concatenate(
-        [jnp.concatenate([real_rows, -imag_rows], axis=2), jnp.concatenate([imag_rows, real_rows], axis=2)], axis=1
-    )
-    back = jnp.swapaxes(left, 1, 2)
-    real_columns, imag_columns = jnp.swapaxes(real_rows, 1, 2), jnp.swapaxes(imag_rows, 1, 2)
-    right = jnp.concatenate(
-        [
-            jnp.stack([real_columns, imag_columns], axis=3),
-            jnp.stack([-imag_columns, real_columns], axis=3),
-        ],
-        axis=1,
-    )
-    columns = jnp.swapaxes(right.reshape(planes, 2 * width, 2 * width), 1, 2).reshape(planes, 2 * width, 1, 2, 1, width)
-    same = jnp.eye(pols, dtype=jnp.bool_).reshape(1, 1, pols, 1, pols, 1)
-    turned = jnp.where(same, columns, jnp.zeros((), columns.dtype))
-    turned = turned.reshape(planes, 2 * width * pols, 2 * width * pols)
-    right = jnp.broadcast_to(right[..., None], right.shape + (pols,)).reshape(planes, 2 * width, 2 * width * pols)
-    return left, back, right, turned
-
-
-def exchange(operand):
-    return lax.all_to_all(operand, AXES, split_axis=0, concat_axis=0, tiled=True)
+    size, wide = 2 * width, 2 * width * pols
+    rows = np.concatenate([np.arange(half, width), [0], np.arange(half - 1, 0, -1)])
+    pick = np.eye(width)[rows]
+    none = np.zeros_like(pick)
+    signs = np.block([[pick, none], [none, pick], [none, -pick], [pick, none]])
+    spread = np.zeros((2, width, width, 2, pols))
+    repeat = np.zeros((2, width, 2, pols, width))
+    for r in range(2):
+        for n in range(width):
+            spread[r, n, n, r] = 1.0
+            repeat[r, n, r, :, n] = 1.0
+    spread, repeat = spread.reshape(size, wide), repeat.reshape(size, wide)
+    constants = [jnp.asarray(table, jnp.bfloat16) for table in (signs, spread, spread.T, repeat)]
+    part = math.gcd(planes, 8)
+
+    def by_part(shape):
+        return pl.BlockSpec((part,) + shape, lambda i: (i, 0, 0))
+
+    shapes = [(size, size), (size, size), (size, wide), (wide, wide)]
+    return pl.pallas_call(
+        table_kernel,
+        grid=(planes // part,),
+        out_shape=[jax.ShapeDtypeStruct((planes,) + shape, jnp.bfloat16) for shape in shapes],
+        in_specs=[by_part((size, width))] + [pl.BlockSpec(table.shape, lambda i: (0, 0)) for table in constants],
+        out_specs=[by_part(shape) for shape in shapes],
+        compiler_params=pltpu.CompilerParams(vmem_limit_bytes=VMEM_BYTES),
+        name="kernel_tables",
+    )(w_kernels.reshape(planes, size, width), *constants)
 
 
 def shards(vis_obs, uv_coords, vis_weight, block_group, tile_slot, w_plane, model_tiles, w_kernels):
-    blocks = vis_obs.shape[0]
-    pols = vis_obs.shape[2]
-    groups = lax.axis_size(AXES)
+    blocks, _, pols, vis_count = vis_obs.shape
+    peers = lax.axis_size("peer")
+    groups = 2 * peers
     owned = model_tiles.shape[0]
     tile_shape = model_tiles.shape[1:]
+    flat_shape = (tile_shape[0] * tile_shape[1], tile_shape[2])
     capacity = max(2, 2 * blocks // groups)
-    early = max(1, 3 * capacity // 8)
+    swap = [(0, 1), (1, 0)]
+    mirrored = lax.ppermute(model_tiles, "half", swap)
+
     target = block_group[:, 0]
-    markers = target[:, None] == jnp.arange(groups, dtype=jnp.int32)[None, :]
+    far = lax.rem(lax.div(target, peers) + lax.axis_index("half"), 2)
+    peer = lax.rem(target, peers)
+    holder = far * peers + peer
+    markers = holder[:, None] == jnp.arange(groups, dtype=jnp.int32)[None, :]
     counts = markers.astype(jnp.int32)
     before = jnp.cumsum(counts, axis=0) - counts
     rank = jnp.sum(jnp.where(markers, before, 0), axis=1)
     ranks = rank[:, None] == jnp.arange(capacity, dtype=jnp.int32)[None, :]
     wanted = jnp.sum(
         jnp.where(markers[:, :, None] & ranks[:, None, :], (tile_slot + 1)[:, None, None], 0), axis=0
-    )
-    own_weight = jnp.broadcast_to(jnp.sum(vis_weight)[None, None], (groups, 1))
-    answers = exchange(jnp.concatenate([wanted.astype(jnp.float32), own_weight], axis=1))
-    requested = answers[:, :capacity].astype(jnp.int32) - 1
-    weight_sum = jnp.sum(answers[:, capacity])
-    scaling = blocks * groups * vis_obs.shape[-1] / weight_sum
-    scaling = scaling.reshape(1)
+    ).astype(jnp.float32)
+    own_weight = jnp.broadcast_to(jnp.sum(vis_weight)[None, None], (peers, 1))
+
+    def exchange(operand):
+        return lax.all_to_all(operand, "peer", split_axis=0, concat_axis=0, tiled=True)
+
+    answers = exchange(jnp.concatenate([wanted[:peers], wanted[peers:], own_weight], axis=1))
+    near_request = answers[:, :capacity].astype(jnp.int32) - 1
+    far_request = answers[:, capacity : 2 * capacity].astype(jnp.int32) - 1
+    half_weight = jnp.sum(answers[:, 2 * capacity]).reshape(1)
+    weight_sum = half_weight + lax.ppermute(half_weight, "half", swap)
+    scaling = blocks * groups * vis_count / weight_sum
 
     tables = kernel_tables(w_kernels, pols)
-    is_late = rank >= early
-    late = is_late.astype(jnp.int32)
-    early_count = blocks - jnp.sum(late)
-    late_base = (early_count + BATCH - 1) // BATCH * BATCH
-    item = jnp.where(is_late, late_base + jnp.cumsum(late) - 1, jnp.cumsum(1 - late) - 1)
+    near_count = blocks - jnp.sum(far)
+    far_base = (near_count + BATCH - 1) // BATCH * BATCH
+    item = jnp.where(far == 1, far_base + jnp.cumsum(far) - 1, jnp.cumsum(1 - far) - 1)
     items = jnp.arange(blocks + BATCH, dtype=jnp.int32)
     order = jnp.sum(
         jnp.where(items[:, None] == item[None, :], jnp.arange(blocks, dtype=jnp.int32)[None, :], 0), axis=1
     )
-    slot = jnp.where(is_late, target * (capacity - early) + rank - early, target * early + rank)
+    slot = peer * capacity + rank
     u = jnp.take(uv_coords[:, 0], order, axis=0, mode="clip")
     v = jnp.take(uv_coords[:, 1], order, axis=0, mode="clip")
     weight = jnp.take(vis_weight, order, axis=0, mode="clip")
 
-    def choose(part):
-        chosen = jnp.take(model_tiles, jnp.maximum(part, 0).reshape(-1), axis=0, mode="clip")
-        return chosen.reshape(part.shape + tile_shape)
+    def choose(tiles, request):
+        chosen = jnp.take(tiles, jnp.maximum(request, 0).reshape(-1), axis=0, mode="clip")
+        return chosen.reshape(request.shape + tile_shape)
 
     def send_tiles(chosen):
         return exchange(chosen).reshape((-1,) + tile_shape)
 
-    def send_back(part):
-        returned = exchange(part.reshape((groups, -1) + tile_shape))
-        return returned.reshape(-1, tile_shape[0] * tile_shape[1], tile_shape[2])
-
-    first, second = requested[:, :early], requested[:, early:]
-    tiles_first = send_tiles(choose(first))
+    def send_back(part, request, dtype):
+        returned = exchange(part.reshape((peers, capacity) + tile_shape)).reshape((-1,) + flat_shape)
+        return sum_tiles(request.reshape(-1), returned, owned, dtype)
+
+    near_tiles = send_tiles(choose(model_tiles, near_request))
     chosen, order, slot, u, v, weight, tables = lax.optimization_barrier(
-        (choose(second), order, slot, u, v, weight, tables)
+        (choose(mirrored, far_request), order, slot, u, v, weight, tables)
     )
-    tiles_second = send_tiles(chosen)
+    far_tiles = send_tiles(chosen)
     given = (vis_obs, u, v, weight, tables)
     zero = jnp.zeros((), jnp.int32)
-    residual, sent_first = process_blocks(
-        blocks, zero, early_count, order, slot, w_plane, tiles_first, *given
+    opening = max(BATCH, blocks // 4 // BATCH * BATCH)
+    first_count = jnp.minimum(near_count, opening)
+    residual, near_sent = process_blocks(opening, zero, first_count, order, slot, w_plane, near_tiles, *given)
+    residual, far_sent = process_blocks(
+        blocks, far_base, blocks - near_count, order, slot, w_plane, far_tiles, *given, (residual,)
     )
-    late_most = blocks * (capacity - early) // capacity
-    residual, sent_second = process_blocks(
-        late_most, late_base, blocks - early_count, order, slot, w_plane, tiles_second, *given, residual
+    relayed = lax.ppermute(send_back(far_sent, far_request, jnp.bfloat16), "half", swap)
+    residual, near_sent = process_blocks(
+        blocks - opening,
+        zero + opening,
+        near_count - first_count,
+        order,
+        slot,
+        w_plane,
+        near_tiles,
+        *given,
+        (residual, near_sent),
     )
-    summed = sum_tiles(first.reshape(-1), scaling, send_back(sent_first), owned)
-    summed = sum_tiles(second.reshape(-1), scaling, send_back(sent_second), owned, summed)
+    summed = send_back(near_sent, near_request, jnp.float32)
+    summed = (summed + relayed.astype(jnp.float32)) * scaling
     return residual, summed.reshape(model_tiles.shape)
 
 
 def solution(mesh):
-    rows = P(AXES)
+    devices = mesh.devices.reshape(2, -1)
+    halves = Mesh(devices, ("half", "peer"))
+    rows = P(("half", "peer"))
     in_specs = (rows,) * 7 + (P(),)
-    return jax.shard_map(shards, mesh=mesh, in_specs=in_specs, out_specs=(rows, rows), check_vma=False)
+    return jax.shard_map(shards, mesh=halves, in_specs=in_specs, out_specs=(rows, rows), check_vma=False)

time: 288 us -> 279 us (0.969)
  local copies, waits for them, and re-layouts: 59.2 us -> 18.1 us
  Pallas kernels: 115 us -> 133 us
  blocking collectives: 0 us -> 11.6 us
  waiting for transfers between devices: 58.8 us -> 66.9 us
  other arithmetic: 17.2 us -> 13.5 us
    ppermute x0 -> x3, waiting for transfers between devices: none -> 66.9 us  [the longest x1 45.3 us: shards(): weight_sum = half_weight + lax.ppermute(half_weight, 'half', swap)]
    all_to_all x5 -> x4, waiting for transfers between devices: 58.8 us -> 0.01 us  [exchange(): lax.all_to_all(operand, 'peer', split_axis=0, concat_axis=0, tiled=True)]
    broadcast_in_dim x8 -> x2, local copies, waits for them, and re-layouts: 34.1 us -> 0.17 us  [choose(): jnp.take(tiles, jnp.maximum(request, 0).reshape(-1), axis=0, mode='clip')]
    pallas_call x4 -> x6, Pallas kernels: 115 us -> 133 us  [the longest x3 110 us: process_blocks(): pl.pallas_call(functools.partial(block_kernel, carried=len(carried)), out...]
    all_to_all x0 -> x1, blocking collectives: none -> 11.6 us  [exchange(): lax.all_to_all(operand, 'peer', split_axis=0, concat_axis=0, tiled=True)]
    all_to_all x5 -> x4, starting transfers between devices: 32.6 us -> 24.8 us  [exchange(): lax.all_to_all(operand, 'peer', split_axis=0, concat_axis=0, tiled=True)]
    ppermute x0 -> x3, starting transfers between devices: none -> 6.29 us  [the longest x1 3.63 us: shards(): lax.ppermute(send_back(far_sent, far_request, jnp.bfloat16), 'half', swap)]
    select_n x2 -> x1, other arithmetic: 4.95 us -> 0.01 us  [shards(): jnp.where(far == 1, far_base + jnp.cumsum(far) - 1, jnp.cumsum(1 - far) - 1)]
  transfers between devices with their start and end apart: 5 -> 7, of which waited for: 2 -> 2; matrix products, arithmetic and copies ran while one was open for 23% -> 6% of each run, Pallas kernels for 38% -> 30%
where the time goes in v3:
time: 279 us; the launch traced here: 277 us
  Pallas kernels  133 us (48%)
  waiting for transfers between devices  66.9 us (24%)
  starting transfers between devices  31.1 us (11%)
  local copies, waits for them, and re-layouts  18.1 us (6%)
  other arithmetic  13.5 us (5%)
  blocking collectives  11.6 us (4%)
  between operations  3.51 us (1%)
    pallas_call x3, Pallas kernels, process_blocks(): pl.pallas_call(functools.partial(block_kernel, carried=len(carried)), out...  110 us
    ppermute x1, waiting for transfers between devices, shards(): weight_sum = half_weight + lax.ppermute(half_weight, 'half', swap)  45.3 us
    all_to_all x4, starting transfers between devices, exchange(): lax.all_to_all(operand, 'peer', split_axis=0, concat_axis=0, tiled=True)  24.8 us
    ppermute x1, waiting for transfers between devices, shards(): mirrored = lax.ppermute(model_tiles, 'half', swap)  21.6 us
    pallas_call x1, Pallas kernels, kernel_tables(): pl.pallas_call(table_kernel, grid=(planes // part,), out_shape=[jax.Shape...  12.6 us
    all_to_all x1, blocking collectives, exchange(): lax.all_to_all(operand, 'peer', split_axis=0, concat_axis=0, tiled=True)  11.6 us
    pallas_call x2, Pallas kernels, sum_tiles(): pl.pallas_call(sum_kernel, out_shape=jax.ShapeDtypeStruct(shape, dtype),...  9.98 us
  transfers between devices with their start and end apart: 7, of which 2 were waited for; matrix products, arithmetic and copies ran while one was open for 6% of the time, Pallas kernels for 30%

profile of v3, /device:TPU:0, one launch (start us, length us, event | category | flops | bytes accessed | tf_op | source)
XLA Modules:
  0.0 277.2 jit_solution(9304255184050640844)
XLA Ops:
  3.9 1.8 reduce_sum.57
  6.5 11.6 %all_to_all.32 = f32[16,1,17]{2,1,0:T(1,128)S(1)} all-to-all(f32[16,1,17]{2,1,0:T(1,128)S(1)} %bitcast.49), channel_id=1, replica_groups=mesh['facet'=4,'vis'=8] {'facet':(2)2,'vis'}, dimensions={0} | all-to-all | bytes 2176 | tf_op jit(solution)/shard_map/all_to_all | solution.py:411
  18.3 2.1 gather_fusion.4
  20.4 3.9 %all-to-all-start.1 = ((bf16[16,8,2,32,128]{4,3,2,1,0:T(8,128)(2,1)}), bf16[16,8,2,32,128]{4,3,2,1,0:T(8,128)(2,1)S(1)}, u32[]{:S(2)}, u32[]{:S(2)}) async-start(bf16[16,8,2,32,128]{4,3,2,1,0:T(8,128)(2,1)} %bitcast.10), calls=%async_computation.1 | async-start | bytes 4194304 | tf_op jit(solution)/shard_map/all_to_all | solution.py:411
  24.3 2.7 collective-permute-start
  29.6 1.6 gather_fusion.3
  31.3 2.6 fusion.8
  34.1 1.6 gather_fusion.2
  35.7 1.6 gather_fusion.1
  37.3 12.6 %kernel_tables.1 = (bf16[32,64,64]{2,1,0:T(8,128)(2,1)}, bf16[32,64,64]{2,1,0:T(8,128)(2,1)}, bf16[32,64,256]{2,1,0:T(8,128)(2,1)}, bf16[32,256,256]{2,1,0:T(8,128)(2,1)}) custom-call(bf16[32,64,32]{2,1,0:T(8,128)(2,1)} %bitcast.46, bf16[128,64]{1,0:T(8,128)(2,1)} %constant.75.clone.signs_ref, bf16[64,256]{1,0:T(8,128)(2,1)} %constant.76.clone.spread_ref, ...), custom_call_target="tpu_custom_call" | custom-call | tf_op jit(solution)/shard_map/kernel_tables/pallas_call | solution.py:374
  50.0 21.6 %collective-permute-done = bf16[64,2,32,128]{3,2,1,0:T(8,128)(2,1)} collective-permute-done((bf16[64,2,32,128]{3,2,1,0:T(8,128)(2,1)}, bf16[64,2,32,128]{3,2,1,0:T(8,128)(2,1)}, u32[]{:S(2)}, u32[]{:S(2)}) %collective-permute-start) | collective-permute-done | bytes 1048608 | tf_op jit(solution)/shard_map/ppermute | solution.py:394
  71.5 3.4 %gather_fusion = bf16[128,2,32,128]{3,2,1,0:T(8,128)(2,1)} fusion(bf16[64,2,32,128]{3,2,1,0:T(8,128)(2,1)} %collective-permute-done, s32[1024]{0:T(1024)S(1)} %pad_clamp_fusion.2), kind=kCustom, calls=%fused_computation | custom fusion | bytes 4194816 | tf_op jit(solution)/shard_map/jit(_take)/gather | solution.py:434
  74.9 1.3 copy-done.2
  76.2 10.8 %all-to-all-start.2 = ((bf16[16,8,2,32,128]{4,3,2,1,0:T(8,128)(2,1)}), bf16[16,8,2,32,128]{4,3,2,1,0:T(8,128)(2,1)}, u32[]{:S(2)}, u32[]{:S(2)}) async-start(bf16[16,8,2,32,128]{4,3,2,1,0:T(8,128)(2,1)} %bitcast.6), calls=%async_computation.2 | async-start | bytes 4194304 | tf_op jit(solution)/shard_map/all_to_all | solution.py:411
  89.6 27.2 %process_blocks.3 = (f32[128,2,4,1024]{3,2,1,0:T(4,128)}, bf16[128,2,32,128]{3,2,1,0:T(8,128)(2,1)}) custom-call(s32[2]{0:T(128)} %pad_add_fusion.2.meta, s32[136]{0:T(256)} %copy-done.4, s32[128]{0:T(128)} %get-tuple-element.27.slot, s32[128]{0:T(128)} %plane.5, bf16[128,2,32,128]{3,2,1,0:T(8,128)(2,1)} %bitcast.41, f32[128,2,4,1024]{3,2,1,0:T(4,128)} %observed.5, ...), custom_call_target="tpu_custom_call" | custom-call | flops 2147483648 | bytes 10485760 | tf_op jit(solution)/shard_map/process_blocks/pallas_call | solution.py:266
  116.9 49.8 %process_blocks.4 = (f32[128,2,4,1024]{3,2,1,0:T(4,128)}, bf16[128,2,32,128]{3,2,1,0:T(8,128)(2,1)}) custom-call(s32[2]{0:T(128)} %pad_add_fusion.1.meta, s32[136]{0:T(256)} %copy-done.4, s32[128]{0:T(128)} %get-tuple-element.27.slot, s32[128]{0:T(128)} %plane.5, bf16[128,2,32,128]{3,2,1,0:T(8,128)(2,1)} %bitcast.14.tiles, ...), custom_call_target="tpu_custom_call", output_to_operand_aliasing={{0}: (13, {})} | custom-call | flops 8589934592 | bytes 41943040 | tf_op jit(solution)/shard_map/process_blocks/pallas_call | solution.py:266
  166.7 5.1 %all-to-all-start.4 = ((bf16[16,8,2,32,128]{4,3,2,1,0:T(8,128)(2,1)}), bf16[16,8,2,32,128]{4,3,2,1,0:T(8,128)(2,1)S(1)}, u32[]{:S(2)}, u32[]{:S(2)}) async-start(bf16[16,8,2,32,128]{4,3,2,1,0:T(8,128)(2,1)} %bitcast.44), calls=%async_computation.4 | async-start | bytes 4194304 | tf_op jit(solution)/shard_map/all_to_all | solution.py:411
  172.4 32.9 %process_blocks.5 = (f32[128,2,4,1024]{3,2,1,0:T(4,128)}, bf16[128,2,32,128]{3,2,1,0:T(8,128)(2,1)}) custom-call(s32[2]{0:T(128)} %pad_add_fusion.meta, s32[136]{0:T(256)} %copy-done.4, s32[128]{0:T(128)} %get-tuple-element.27.slot, s32[128]{0:T(128)} %plane.5, bf16[128,2,32,128]{3,2,1,0:T(8,128)(2,1)} %bitcast.42, ...), custom_call_target="tpu_custom_call", output_to_operand_aliasing={{0}: (13, {}), {1}: (14, {})} | custom-call | flops 6442450944 | bytes 31457280 | tf_op jit(solution)/shard_map/process_blocks/pallas_call | solution.py:266
  206.6 5.1 %all-to-all-start.3 = ((bf16[16,8,2,32,128]{4,3,2,1,0:T(8,128)(2,1)}), bf16[16,8,2,32,128]{4,3,2,1,0:T(8,128)(2,1)}, u32[]{:S(2)}, u32[]{:S(2)}) async-start(bf16[16,8,2,32,128]{4,3,2,1,0:T(8,128)(2,1)} %bitcast.43), calls=%async_computation.3 | async-start | bytes 4194304 | tf_op jit(solution)/shard_map/all_to_all | solution.py:411
  212.3 4.8 %sum_tiles.3 = bf16[64,64,128]{2,1,0:T(8,128)(2,1)} custom-call(s32[128]{0:T(128)} %reshape.173.requested, bf16[128,64,128]{2,1,0:T(8,128)(2,1)} %bitcast.40), custom_call_target="tpu_custom_call" | custom-call | flops 1048576 | bytes 4194304 | tf_op jit(solution)/shard_map/sum_tiles/pallas_call | solution.py:318
  217.1 3.6 %collective-permute-start.1 = (bf16[64,64,128]{2,1,0:T(8,128)(2,1)}, bf16[64,64,128]{2,1,0:T(8,128)(2,1)S(1)}, u32[]{:S(2)}, u32[]{:S(2)}) collective-permute-start(bf16[64,64,128]{2,1,0:T(8,128)(2,1)} %sum_tiles.3), channel_id=1, source_target_pairs={{0,16},{16,0},{1,17},{17,1},{2,18},{18,2},{3,19},{19,3},{4,20},{20... | collective-permute-start | bytes 3145736 | tf_op jit(solution)/shard_map/ppermute | solution.py:457
  222.0 45.3 %collective-permute-done.2 = f32[1]{0:T(128)} collective-permute-done((f32[1]{0:T(128)}, f32[1]{0:T(128)}, u32[]{:S(2)}, u32[]{:S(2)}) %collective-permute-start.2) | collective-permute-done | bytes 36 | tf_op jit(solution)/shard_map/ppermute | solution.py:417
  268.6 5.1 %sum_tiles.2 = f32[64,64,128]{2,1,0:T(8,128)} custom-call(s32[128]{0:T(128)} %reshape.170.requested, bf16[128,64,128]{2,1,0:T(8,128)(2,1)} %bitcast.17.arrived_ref), custom_call_target="tpu_custom_call" | custom-call | flops 1048576 | bytes 4194304 | tf_op jit(solution)/shard_map/sum_tiles/pallas_call | solution.py:318
  273.8 3.4 %add_multiply_fusion = f32[64,64,128]{2,1,0:T(8,128)} fusion(f32[64,64,128]{2,1,0:T(8,128)} %sum_tiles.2, bf16[64,64,128]{2,1,0:T(8,128)(2,1)S(1)} %collective-permute-done.1, f32[]{:T(128)} %bitcast.21), kind=kLoop, calls=%fused_computation.5 | loop fusion | flops 1572864 | bytes 5242884 | tf_op jit(solution)/shard_map/mul | solution.py:470
  (51 shorter events, 12.2 us)
Async XLA Ops:
  0.6 17.6 %copy-start.3 = (bf16[64,2,32,128]{3,2,1,0:T(8,128)(2,1)S(1)}, bf16[64,2,32,128]{3,2,1,0:T(8,128)(2,1)}, u32[]{:S(2)}) copy-start(bf16[64,2,32,128]{3,2,1,0:T(8,128)(2,1)} %param.18) | copy-start | bytes 3145732
  20.4 6.6 %copy-start.5 = (s32[128,1]{0,1:T(1,128)S(1)}, s32[128,1]{0,1:T(1,128)}, u32[]{:S(2)}) copy-start(s32[128,1]{0,1:T(1,128)} %param.15) | copy-start | bytes 1540
  20.4 9.2 %copy-start = (f32[128,1024]{1,0:T(8,128)S(1)}, f32[128,1024]{1,0:T(8,128)}, u32[]{:S(2)}) copy-start(f32[128,1024]{1,0:T(8,128)} %param.14) | copy-start | bytes 1572868
  20.4 54.5 %all-to-all-start.1 = ((bf16[16,8,2,32,128]{4,3,2,1,0:T(8,128)(2,1)}), bf16[16,8,2,32,128]{4,3,2,1,0:T(8,128)(2,1)S(1)}, u32[]{:S(2)}, u32[]{:S(2)}) async-start(bf16[16,8,2,32,128]{4,3,2,1,0:T(8,128)(2,1)} %bitcast.10), calls=%async_computation.1 | async-start | bytes 4194304 | tf_op jit(solution)/shard_map/all_to_all | solution.py:411
  24.3 47.3 %collective-permute-start = (bf16[64,2,32,128]{3,2,1,0:T(8,128)(2,1)}, bf16[64,2,32,128]{3,2,1,0:T(8,128)(2,1)}, u32[]{:S(2)}, u32[]{:S(2)}) collective-permute-start(bf16[64,2,32,128]{3,2,1,0:T(8,128)(2,1)} %param.18), channel_id=1, source_target_pairs={{0,16},{16,0},{1,17},{17,1},{2,18},{18,2},{3,19},{19,3},{4,20},{20... | collective-permute-start | bytes 3145736 | tf_op jit(solution)/shard_map/ppermute | solution.py:394
  29.6 1.7 copy-start.4
  74.9 1.3 copy-start.2
  76.2 40.6 %all-to-all-start.2 = ((bf16[16,8,2,32,128]{4,3,2,1,0:T(8,128)(2,1)}), bf16[16,8,2,32,128]{4,3,2,1,0:T(8,128)(2,1)}, u32[]{:S(2)}, u32[]{:S(2)}) async-start(bf16[16,8,2,32,128]{4,3,2,1,0:T(8,128)(2,1)} %bitcast.6), calls=%async_computation.2 | async-start | bytes 4194304 | tf_op jit(solution)/shard_map/all_to_all | solution.py:411
  166.7 38.6 %all-to-all-start.4 = ((bf16[16,8,2,32,128]{4,3,2,1,0:T(8,128)(2,1)}), bf16[16,8,2,32,128]{4,3,2,1,0:T(8,128)(2,1)S(1)}, u32[]{:S(2)}, u32[]{:S(2)}) async-start(bf16[16,8,2,32,128]{4,3,2,1,0:T(8,128)(2,1)} %bitcast.44), calls=%async_computation.4 | async-start | bytes 4194304 | tf_op jit(solution)/shard_map/all_to_all | solution.py:411
  205.3 1.3 copy-start.1
  206.6 62.0 %all-to-all-start.3 = ((bf16[16,8,2,32,128]{4,3,2,1,0:T(8,128)(2,1)}), bf16[16,8,2,32,128]{4,3,2,1,0:T(8,128)(2,1)}, u32[]{:S(2)}, u32[]{:S(2)}) async-start(bf16[16,8,2,32,128]{4,3,2,1,0:T(8,128)(2,1)} %bitcast.43), calls=%async_computation.3 | async-start | bytes 4194304 | tf_op jit(solution)/shard_map/all_to_all | solution.py:411
  217.1 56.6 %collective-permute-start.1 = (bf16[64,64,128]{2,1,0:T(8,128)(2,1)}, bf16[64,64,128]{2,1,0:T(8,128)(2,1)S(1)}, u32[]{:S(2)}, u32[]{:S(2)}) collective-permute-start(bf16[64,64,128]{2,1,0:T(8,128)(2,1)} %sum_tiles.3), channel_id=1, source_target_pairs={{0,16},{16,0},{1,17},{17,1},{2,18},{18,2},{3,19},{19,3},{4,20},{20... | collective-permute-start | bytes 3145736 | tf_op jit(solution)/shard_map/ppermute | solution.py:457
  221.4 45.9 %collective-permute-start.2 = (f32[1]{0:T(128)}, f32[1]{0:T(128)}, u32[]{:S(2)}, u32[]{:S(2)}) collective-permute-start(f32[1]{0:T(128)} %bitcast.20), channel_id=1, source_target_pairs={{0,16},{16,0},{1,17},{17,1},{2,18},{18,2},{3,19},{19,3},{4,20},{20... | collective-permute-start | bytes 20 | tf_op jit(solution)/shard_map/ppermute | solution.py:417

commit v4 on v3

--- a/solution.py
+++ b/solution.py
@@ -13,7 +13,8 @@
 BATCH = 8
 LANES = 512
 TILE = 128
-UNROLL = 4
+ROWS = 8
+UNROLL = 8
 VMEM_BYTES = 60 * 1024 * 1024
 SIN_TERMS = [(-1.0) ** i * (2.0 * math.pi) ** (2 * i + 1) / math.factorial(2 * i + 1) for i in range(8)]
 COS_TERMS = [(-1.0) ** i * (2.0 * math.pi) ** (2 * i) / math.factorial(2 * i) for i in range(9)]
@@ -62,7 +63,8 @@
     meta, order, slot, plane, tiles, observed, u_ref, v_ref, w_ref, left_ref, back_ref, right_ref, turned_ref, *rest, carried
 ):
     res, con, fu_ref, fv_ref, tile_buf, obs_buf, model_buf, grid_buf, res_buf, con_buf, in_sems, out_sems = rest[carried:]
-    half = fv_ref.shape[0] // 2 - 1
+    quarter = fv_ref.shape[0] // 2 - 1
+    half = 2 * quarter
     width = 2 * half
     pols = obs_buf.shape[3]
     span = pols * width
@@ -102,28 +104,62 @@
                 fu_ref[t, row * BATCH : (row + 1) * BATCH, :] = value[:, t * TILE : (t + 1) * TILE]
 
         put(0, jnp.ones_like(cosine))
-        put(width, jnp.zeros_like(cosine))
-        for j in range(1, half + 1):
+        put(half, powers[half][0])
+        put(width, powers[half][1])
+        for j in range(1, half):
             real, imag = powers[j]
-            if j < half:
-                put(j, real)
-                put(width + j, imag)
-            low = half if j == half else half + j
-            put(low, real)
-            put(width + low, -imag)
+            put(j, real)
+            put(half + j, imag)
+        for j in range(1, ROWS):
+            put(width + j, jnp.zeros_like(cosine))
         cosine, sine = unit_phasor(v_ref[...] * (1.0 / width))
-        powers = phasor_powers(cosine, sine, half)
-        for j in range(1, half + 1):
-            fv_ref[j], fv_ref[half + 1 + j] = powers[j]
+        powers = phasor_powers(cosine, sine, quarter)
+        for j in range(1, quarter + 1):
+            fv_ref[j], fv_ref[quarter + 1 + j] = powers[j]
 
     wide = 2 * span
-    unpaired = lax.broadcasted_iota(jnp.int32, (2 * width, span), 1) < 2 * pols
+    basis = 2 * (width + ROWS)
+    lane = lax.broadcasted_iota(jnp.int32, (basis, span), 1)
+    unpaired = lax.rem(lane, span // 2) < 2 * pols
+    direct = lane < span // 2
+    start_row = lax.broadcasted_iota(jnp.int32, (half, span), 0) == 0
+    lone_row = start_row[:ROWS]
 
     def paired(full):
-        first, second = full[:, :span], full[:, span:]
-        total = jnp.where(unpaired, first, first + second)
-        change = jnp.where(unpaired, second, first - second)
-        return jnp.concatenate([total, change], axis=1)
+        other = jnp.roll(full, span // 2, axis=1)
+        return jnp.where(unpaired, full, jnp.where(direct, full + other, other - full))
+
+    def fold(full):
+        total, change = full[:, :span] + full[:, span:], full[:, :span] - full[:, span:]
+
+        def pairs(real, imag):
+            ahead, behind = real[:half], real[half:]
+            above, below = imag[:half], imag[half:]
+            return [jnp.where(start_row, ahead, ahead + behind), jnp.where(start_row, behind, above - below)], (
+                jnp.where(lone_row, -below[:ROWS], 0.0)
+            )
+
+        cos_pairs, cos_lone = pairs(total[:width], total[width:])
+        sin_pairs, sin_lone = pairs(change[width:], -change[:width])
+        return paired(jnp.concatenate(cos_pairs + sin_pairs + [cos_lone, sin_lone], axis=0))
+
+    def unfold(sums):
+        sums = paired(sums)
+        cos_cos, sin_cos, cos_sin, sin_sin = [sums[i * half : (i + 1) * half] for i in range(4)]
+        lone_cos = sums[4 * half :]
+        lone_sin = jnp.concatenate([sums[4 * half + ROWS :]] * 2, axis=0)
+        ahead = [cos_cos, jnp.where(start_row, 0.0, sin_cos), cos_sin, jnp.where(start_row, 0.0, sin_sin)]
+        behind = [
+            jnp.where(start_row, sin_cos, cos_cos),
+            -jnp.where(start_row, lone_cos, sin_cos),
+            jnp.where(start_row, sin_sin, cos_sin),
+            -jnp.where(start_row, lone_sin, sin_sin),
+        ]
+        columns = []
+        for side in (1.0, -1.0):
+            rows = [[cc - side * ss, sc + side * cs] for cc, sc, cs, ss in (ahead, behind)]
+            columns.append(jnp.concatenate([rows[0][0], rows[1][0], rows[0][1], rows[1][1]], axis=0))
+        return jnp.concatenate(columns, axis=1)
 
     def from_right(which):
         band = lax.rem(lax.broadcasted_iota(jnp.int32, (width, wide), 1), pols)
@@ -143,7 +179,7 @@
             [jnp.concatenate([left_real, left_imag], axis=1), jnp.concatenate([-left_imag, left_real], axis=1)],
             axis=0,
         )
-        model_buf[k] = paired(rows_dot(left, from_right(which), 1, 0)).astype(jnp.bfloat16)
+        model_buf[k] = fold(rows_dot(left, from_right(which), 1, 0)).astype(jnp.bfloat16)
 
     turn = jnp.where(lax.broadcasted_iota(jnp.int32, (2 * pols, LANES), 0) < pols, -1.0, 1.0)
 
@@ -154,21 +190,25 @@
             lanes = pl.ds(start, LANES)
             along_u = jnp.concatenate(
                 [
-                    fu_ref[start // TILE + t, pl.ds(k, 2 * width, stride=BATCH), :]
+                    fu_ref[start // TILE + t, pl.ds(k, width + ROWS, stride=BATCH), :]
                     for t in range(LANES // TILE)
                 ],
                 axis=1,
-            ).astype(jnp.bfloat16)
-            spread = rows_dot(model, along_u, 0, 0).reshape(width, 2 * pols, LANES)
+            ).reshape((width + ROWS) // ROWS, ROWS, LANES)
 
             def phase(index):
                 return jnp.broadcast_to(fv_ref[index, pl.ds(k, 1), lanes], (2 * pols, LANES))
 
-            cos_part = spread[0] + spread[half] * phase(half)
-            sin_part = -spread[half] * phase(2 * half + 1)
-            for j in range(1, half):
+            far_cos, far_sin = phase(quarter), phase(2 * quarter + 1)
+            main, lone = along_u[: width // ROWS], along_u[width // ROWS :]
+            along = jnp.concatenate([main * far_cos, main * far_sin, lone * far_cos, lone * far_sin], axis=0)
+            along = along.reshape(basis, LANES).astype(jnp.bfloat16)
+            spread = rows_dot(model, along, 0, 0).reshape(half, 2 * pols, LANES)
+            cos_part = spread[0] + spread[quarter] * far_cos
+            sin_part = -spread[quarter] * far_sin
+            for j in range(1, quarter):
                 cos_part = cos_part + spread[j] * phase(j)
-                sin_part = sin_part + spread[half + j] * phase(half + 1 + j)
+                sin_part = sin_part + spread[quarter + j] * phase(quarter + 1 + j)
             predicted = cos_part + turn * jnp.roll(sin_part, pols, axis=0)
             given = obs_buf[lax.rem(step, 2), k, :, :, lanes]
             residual = jnp.concatenate([given[0], given[1]], axis=0) - predicted * (1.0 / width)
@@ -176,18 +216,18 @@
             res_buf[k, 1, :, lanes] = residual[pols:]
             scaled = residual * (w_ref[pl.ds(k, 1), lanes] * (1.0 / width))
             turned = -turn * jnp.roll(scaled, pols, axis=0)
-            cos_rows, sin_rows = [scaled], [scaled * phase(half) - turned * phase(2 * half + 1)]
-            for j in range(1, half):
+            cos_rows, sin_rows = [scaled], [scaled * far_cos - turned * far_sin]
+            for j in range(1, quarter):
                 cos_rows.append(scaled * phase(j))
-                sin_rows.append(turned * phase(half + 1 + j))
+                sin_rows.append(turned * phase(quarter + 1 + j))
             weighted = jnp.concatenate(cos_rows + sin_rows, axis=0).astype(jnp.bfloat16)
-            part = rows_dot(along_u, weighted, 1, 1)
+            part = rows_dot(along, weighted, 1, 1)
             gridded = part if gridded is None else gridded + part
         grid_buf[k] = gridded
 
     def make_contribution(k):
         which = plane[block_at(step, k)]
-        back = rows_dot(jnp.concatenate(split(paired(grid_buf[k])), axis=0), turned_ref[which], 1, 0)
+        back = rows_dot(jnp.concatenate(split(unfold(grid_buf[k])), axis=0), turned_ref[which], 1, 0)
         back = back[: 2 * width] + back[2 * width :]
         back_real = back[:width, :span] + back[width:, span:]
         back_imag = back[:width, span:] - back[width:, :span]
@@ -275,12 +315,12 @@
             in_specs=in_specs,
             out_specs=(hbm, hbm),
             scratch_shapes=[
-                pltpu.VMEM((vis_count // TILE, BATCH * 2 * width, TILE), jnp.float32),
-                pltpu.VMEM((width + 2, BATCH, vis_count), jnp.float32),
+                pltpu.VMEM((vis_count // TILE, BATCH * (width + ROWS), TILE), jnp.float32),
+                pltpu.VMEM((width // 2 + 2, BATCH, vis_count), jnp.float32),
                 pltpu.VMEM((2, BATCH) + tile_shape, jnp.bfloat16),
                 pltpu.VMEM((2, BATCH) + vis_shape, jnp.float32),
-                pltpu.VMEM((BATCH, 2 * width, 2 * pols * width), jnp.bfloat16),
-                pltpu.VMEM((BATCH, 2 * width, 2 * pols * width), jnp.float32),
+                pltpu.VMEM((BATCH, 2 * (width + ROWS), pols * width), jnp.bfloat16),
+                pltpu.VMEM((BATCH, 2 * (width + ROWS), pols * width), jnp.float32),
                 pltpu.VMEM((BATCH,) + vis_shape, jnp.float32),
                 pltpu.VMEM((BATCH,) + tile_shape, jnp.bfloat16),
                 pltpu.SemaphoreType.DMA((2, 2, BATCH)),
@@ -298,8 +338,17 @@
     )(meta, order, slot, plane, *operands)
 
 
-def sum_kernel(requested, arrived_ref, out_ref, total_ref):
-    total_ref[...] = jnp.zeros_like(total_ref)
+def sum_kernel(requested, *refs, carried):
+    if carried:
+        scale_ref, arrived_ref, *old_refs, out_ref, total_ref = refs
+        start = 0
+        for old_ref in old_refs:
+            rows = old_ref.shape[1]
+            total_ref[:, start : start + rows] = old_ref[...].astype(jnp.float32)
+            start += rows
+    else:
+        arrived_ref, out_ref, total_ref = refs
+        total_ref[...] = jnp.zeros_like(total_ref)
 
     @pl.loop(0, arrived_ref.shape[0])
     def _(i):
@@ -309,25 +358,27 @@
         def _():
             total_ref[tile] += arrived_ref[i].astype(jnp.float32)
 
-    out_ref[...] = total_ref[...].astype(out_ref.dtype)
-
-
-def sum_tiles(requested, arrived, owned, dtype):
+    total = total_ref[...] * scale_ref[0] if carried else total_ref[...]
+    out_ref[...] = total.astype(out_ref.dtype)
+
+
+def sum_tiles(requested, arrived, owned, dtype, scale=None, old=()):
     shape = (owned,) + arrived.shape[1:]
-    vmem = pl.BlockSpec(memory_space=pltpu.VMEM)
+    vmem, smem = pl.BlockSpec(memory_space=pltpu.VMEM), pl.BlockSpec(memory_space=pltpu.SMEM)
+    carried = len(old) > 0
     return pl.pallas_call(
-        sum_kernel,
+        functools.partial(sum_kernel, carried=carried),
         out_shape=jax.ShapeDtypeStruct(shape, dtype),
-        in_specs=[pl.BlockSpec(memory_space=pltpu.SMEM), vmem],
+        in_specs=[smem, smem, vmem] + [vmem] * len(old) if carried else [smem, vmem],
         out_specs=vmem,
         scratch_shapes=[pltpu.VMEM(shape, jnp.float32)],
         compiler_params=pltpu.CompilerParams(vmem_limit_bytes=VMEM_BYTES),
         cost_estimate=pl.CostEstimate(flops=arrived.size, bytes_accessed=arrived.size * 4, transcendentals=0),
         name="sum_tiles",
-    )(requested, arrived)
-
-
-def table_kernel(planes_ref, signs_ref, spread_ref, gather_ref, repeat_ref, left_ref, back_ref, right_ref, turned_ref):
+    )(requested, *((scale, arrived, *old) if carried else (arrived,)))
+
+
+def table_kernel(planes_ref, signs_ref, columns_ref, spread_ref, gather_ref, repeat_ref, left_ref, back_ref, right_ref, turned_ref):
     size = left_ref.shape[1]
     wide = right_ref.shape[2]
     pols = wide // size
@@ -340,23 +391,36 @@
         return rows_dot(left, right, left_dim, 0).astype(jnp.bfloat16)
 
     for k in range(planes_ref.shape[0]):
-        both = exact(signs_ref[...], planes_ref[k])
-        left = jnp.concatenate([both[:size], both[size:]], axis=1)
+        def embed(signs):
+            both = exact(signs, planes_ref[k])
+            return jnp.concatenate([both[:size], both[size:]], axis=1)
+
+        left = embed(signs_ref[...])
         left_ref[k] = left
         back = exact(left, jnp.eye(size, dtype=jnp.bfloat16), 0)
         back_ref[k] = back
-        right_ref[k] = exact(back, spread_ref[...])
-        turned_ref[k] = jnp.where(same, exact(exact(gather_ref[...], left), repeat_ref[...]), zero)
+        columns = embed(columns_ref[...])
+        right_ref[k] = exact(columns, spread_ref[...], 0)
+        turned_ref[k] = jnp.where(same, exact(exact(gather_ref[...], columns), repeat_ref[...]), zero)
 
 
 def kernel_tables(w_kernels, pols):
     planes, _, width, _ = w_kernels.shape
     half = width // 2
     size, wide = 2 * width, 2 * width * pols
-    rows = np.concatenate([np.arange(half, width), [0], np.arange(half - 1, 0, -1)])
-    pick = np.eye(width)[rows]
-    none = np.zeros_like(pick)
-    signs = np.block([[pick, none], [none, pick], [none, -pick], [pick, none]])
+
+
+    def signs(offsets):
+        pick = np.eye(width)[np.array(offsets) + half]
+        none = np.zeros_like(pick)
+        return np.block([[pick, none], [none, pick], [none, -pick], [pick, none]])
+
+    def paired(count):
+        return [*range(count), -count, *range(-1, -count, -1)]
+
+    quarter = half // 2
+    rows = signs(paired(half))
+    columns = signs([c + side * quarter for side in (1, -1) for c in paired(quarter)])
     spread = np.zeros((2, width, width, 2, pols))
     repeat = np.zeros((2, width, 2, pols, width))
     for r in range(2):
@@ -364,7 +428,7 @@
             spread[r, n, n, r] = 1.0
             repeat[r, n, r, :, n] = 1.0
     spread, repeat = spread.reshape(size, wide), repeat.reshape(size, wide)
-    constants = [jnp.asarray(table, jnp.bfloat16) for table in (signs, spread, spread.T, repeat)]
+    constants = [jnp.asarray(table, jnp.bfloat16) for table in (rows, columns, spread, spread.T, repeat)]
     part = math.gcd(planes, 8)
 
     def by_part(shape):
@@ -378,6 +442,7 @@
         in_specs=[by_part((size, width))] + [pl.BlockSpec(table.shape, lambda i: (0, 0)) for table in constants],
         out_specs=[by_part(shape) for shape in shapes],
         compiler_params=pltpu.CompilerParams(vmem_limit_bytes=VMEM_BYTES),
+        cost_estimate=pl.CostEstimate(flops=planes * wide * wide * size * 4, bytes_accessed=planes * wide * wide * 2, transcendentals=0),
         name="kernel_tables",
     )(w_kernels.reshape(planes, size, width), *constants)
 
@@ -391,7 +456,11 @@
     flat_shape = (tile_shape[0] * tile_shape[1], tile_shape[2])
     capacity = max(2, 2 * blocks // groups)
     swap = [(0, 1), (1, 0)]
-    mirrored = lax.ppermute(model_tiles, "half", swap)
+    cut = 3 * owned // 8
+    mirrored_low = lax.ppermute(model_tiles[:cut], "half", swap)
+    high_tiles, mirrored_low = lax.optimization_barrier((model_tiles[cut:], mirrored_low))
+    mirrored_high = lax.ppermute(high_tiles, "half", swap)
+    mirrored = jnp.concatenate([mirrored_low, mirrored_high], axis=0)
 
     target = block_group[:, 0]
     far = lax.rem(lax.div(target, peers) + lax.axis_index("half"), 2)
@@ -437,10 +506,10 @@
     def send_tiles(chosen):
         return exchange(chosen).reshape((-1,) + tile_shape)
 
-    def send_back(part, request, dtype):
-        returned = exchange(part.reshape((peers, capacity) + tile_shape)).reshape((-1,) + flat_shape)
-        return sum_tiles(request.reshape(-1), returned, owned, dtype)
-
+    def send_back(part):
+        return exchange(part.reshape((peers, capacity) + part.shape[1:])).reshape((peers * capacity,) + part.shape[1:])
+
+    near_request, mirrored_low = lax.optimization_barrier((near_request, mirrored_low))
     near_tiles = send_tiles(choose(model_tiles, near_request))
     chosen, order, slot, u, v, weight, tables = lax.optimization_barrier(
         (choose(mirrored, far_request), order, slot, u, v, weight, tables)
@@ -454,7 +523,10 @@
     residual, far_sent = process_blocks(
         blocks, far_base, blocks - near_count, order, slot, w_plane, far_tiles, *given, (residual,)
     )
-    relayed = lax.ppermute(send_back(far_sent, far_request, jnp.bfloat16), "half", swap)
+    far_sum = sum_tiles(
+        far_request.reshape(-1), send_back(far_sent).reshape((-1,) + flat_shape), owned, jnp.bfloat16
+    )
+    relayed = lax.ppermute(far_sum, "half", swap)
     residual, near_sent = process_blocks(
         blocks - opening,
         zero + opening,
@@ -466,8 +538,9 @@
         *given,
         (residual, near_sent),
     )
-    summed = send_back(near_sent, near_request, jnp.float32)
-    summed = (summed + relayed.astype(jnp.float32)) * scaling
+    near_sent, far_sum = lax.optimization_barrier((near_sent, far_sum))
+    returned = send_back(near_sent).reshape((-1,) + flat_shape)
+    summed = sum_tiles(near_request.reshape(-1), returned, owned, jnp.float32, scaling, [relayed])
     return residual, summed.reshape(model_tiles.shape)
 
 

time: 279 us -> 260 us (0.932)
  the two profiles are of different devices: /device:TPU:0 before, /device:TPU:10 now
where the time goes in v4:
time: 260 us; the launch traced here: 261 us
  Pallas kernels  110 us (42%)
  waiting for transfers between devices  70.1 us (27%)
  starting transfers between devices  43 us (17%)
  local copies, waits for them, and re-layouts  21.5 us (8%)
  other arithmetic  13 us (5%)
  between operations  3.49 us (1%)
    pallas_call x3, Pallas kernels, process_blocks(): pl.pallas_call(functools.partial(block_kernel, carried=len(carried)), out...  80.1 us
    ppermute x1, waiting for transfers between devices, shards(): weight_sum = half_weight + lax.ppermute(half_weight, 'half', swap)  50.5 us
    all_to_all x5, starting transfers between devices, exchange(): lax.all_to_all(operand, 'peer', split_axis=0, concat_axis=0, tiled=True)  28.4 us
    pallas_call x1, Pallas kernels, kernel_tables(): pl.pallas_call(table_kernel, grid=(planes // part,), out_shape=[jax.Shape...  19.6 us
    ppermute x1, waiting for transfers between devices, shards(): mirrored_high = lax.ppermute(high_tiles, 'half', swap)  11.3 us
    pallas_call x2, Pallas kernels, sum_tiles(): pl.pallas_call(functools.partial(sum_kernel, carried=carried), out_shape=...  10.2 us
    ppermute x1, starting transfers between devices, shards(): relayed = lax.ppermute(far_sum, 'half', swap)  8.48 us
    all_to_all x5, waiting for transfers between devices, exchange(): lax.all_to_all(operand, 'peer', split_axis=0, concat_axis=0, tiled=True)  6.9 us
  transfers between devices with their start and end apart: 9, of which 5 were waited for; matrix products, arithmetic and copies ran while one was open for 10% of the time, Pallas kernels for 26%

profile of v4, /device:TPU:10, one launch (start us, length us, event | category | flops | bytes accessed | tf_op | source)
XLA Modules:
  0.0 260.9 jit_solution(8001130184398413336)
XLA Ops:
  1.8 2.7 %collective-permute-start = (bf16[24,2,32,128]{3,2,1,0:T(8,128)(2,1)S(1)}, bf16[24,2,32,128]{3,2,1,0:T(8,128)(2,1)S(1)}, u32[]{:S(2)}, u32[]{:S(2)}) collective-permute-start(bf16[24,2,32,128]{3,2,1,0:T(8,128)(2,1)S(1)} %slice.28), channel_id=1, source_target_pairs={{0,16},{16,0},{1,17},{17,1},{2,18},{18,2},{3,19},{19,3},{4,20},{20... | collective-permute-start | bytes 1179656 | tf_op jit(solution)/shard_map/ppermute | solution.py:460
  7.6 1.8 reduce_sum.57
  10.8 5.2 %all-to-all-start = ((f32[16,1,17]{2,1,0:T(1,128)}), f32[16,1,17]{2,1,0:T(1,128)S(1)}, u32[]{:S(2)}, u32[]{:S(2)}) async-start(f32[16,1,17]{2,1,0:T(1,128)} %bitcast.4), calls=%async_computation | async-start | bytes 16384 | tf_op jit(solution)/shard_map/all_to_all | solution.py:480
  16.8 2.2 all-to-all-done
  21.2 2.1 gather_fusion.4
  23.4 5.3 %all-to-all-start.1 = ((bf16[16,8,2,32,128]{4,3,2,1,0:T(8,128)(2,1)}), bf16[16,8,2,32,128]{4,3,2,1,0:T(8,128)(2,1)S(1)}, u32[]{:S(2)}, u32[]{:S(2)}) async-start(bf16[16,8,2,32,128]{4,3,2,1,0:T(8,128)(2,1)} %bitcast.10), calls=%async_computation.1 | async-start | bytes 4194304 | tf_op jit(solution)/shard_map/all_to_all | solution.py:480
  33.5 3.4 %collective-permute-start.1 = (bf16[40,2,32,128]{3,2,1,0:T(8,128)(2,1)}, bf16[40,2,32,128]{3,2,1,0:T(8,128)(2,1)}, u32[]{:S(2)}, u32[]{:S(2)}) collective-permute-start(bf16[40,2,32,128]{3,2,1,0:T(8,128)(2,1)} %slice.27), channel_id=1, source_target_pairs={{0,16},{16,0},{1,17},{17,1},{2,18},{18,2},{3,19},{19,3},{4,20},{20... | collective-permute-start | bytes 1966088 | tf_op jit(solution)/shard_map/ppermute | solution.py:462
  36.9 2.6 fusion.8
  39.7 1.8 gather_fusion.2
  41.5 1.9 gather_fusion.1
  43.4 19.6 %kernel_tables.1 = (bf16[32,64,64]{2,1,0:T(8,128)(2,1)}, bf16[32,64,64]{2,1,0:T(8,128)(2,1)}, bf16[32,64,256]{2,1,0:T(8,128)(2,1)}, bf16[32,256,256]{2,1,0:T(8,128)(2,1)}) custom-call(bf16[32,64,32]{2,1,0:T(8,128)(2,1)} %bitcast.48, bf16[128,64]{1,0:T(8,128)(2,1)} %constant.77.clone.signs_ref, bf16[128,64]{1,0:T(8,128)(2,1)} %constant.78.clone.columns_ref, ...), custom_call_target="tpu_custom_call" | custom-call | flops 536870912 | bytes 4194304 | tf_op jit(solution)/shard_map/kernel_tables/pallas_call | solution.py:438
  63.6 11.3 %collective-permute-done.1 = bf16[40,2,32,128]{3,2,1,0:T(8,128)(2,1)} collective-permute-done((bf16[40,2,32,128]{3,2,1,0:T(8,128)(2,1)}, bf16[40,2,32,128]{3,2,1,0:T(8,128)(2,1)}, u32[]{:S(2)}, u32[]{:S(2)}) %collective-permute-start.1) | collective-permute-done | bytes 655392 | tf_op jit(solution)/shard_map/ppermute | solution.py:462
  76.1 2.3 gather_fusion
  79.7 4.5 %all-to-all-start.2 = ((bf16[16,8,2,32,128]{4,3,2,1,0:T(8,128)(2,1)}), bf16[16,8,2,32,128]{4,3,2,1,0:T(8,128)(2,1)}, u32[]{:S(2)}, u32[]{:S(2)}) async-start(bf16[16,8,2,32,128]{4,3,2,1,0:T(8,128)(2,1)} %bitcast.6), calls=%async_computation.2 | async-start | bytes 4194304 | tf_op jit(solution)/shard_map/all_to_all | solution.py:480
  86.8 20.3 %process_blocks.3 = (f32[128,2,4,1024]{3,2,1,0:T(4,128)}, bf16[128,2,32,128]{3,2,1,0:T(8,128)(2,1)}) custom-call(s32[2]{0:T(128)} %pad_add_fusion.2.meta, s32[136]{0:T(256)} %copy-done.9, s32[128]{0:T(128)} %get-tuple-element.33.slot, s32[128]{0:T(128)} %plane.5, bf16[128,2,32,128]{3,2,1,0:T(8,128)(2,1)} %bitcast.41, f32[128,2,4,1024]{3,2,1,0:T(4,128)} %observed.5, ...), custom_call_target="tpu_custom_call" | custom-call | flops 2147483648 | bytes 10485760 | tf_op jit(solution)/shard_map/process_blocks/pallas_call | solution.py:306
  107.0 4.7 %all-to-all-done.2 = bf16[16,8,2,32,128]{4,3,2,1,0:T(8,128)(2,1)} async-done(((bf16[16,8,2,32,128]{4,3,2,1,0:T(8,128)(2,1)}), bf16[16,8,2,32,128]{4,3,2,1,0:T(8,128)(2,1)}, u32[]{:S(2)}, u32[]{:S(2)}) %all-to-all-start.2) | async-done | bytes 2097184 | tf_op jit(solution)/shard_map/all_to_all | solution.py:480
  111.7 32.0 %process_blocks.4 = (f32[128,2,4,1024]{3,2,1,0:T(4,128)}, bf16[128,2,32,128]{3,2,1,0:T(8,128)(2,1)}) custom-call(s32[2]{0:T(128)} %pad_add_fusion.1.meta, s32[136]{0:T(256)} %copy-done.9, s32[128]{0:T(128)} %get-tuple-element.33.slot, s32[128]{0:T(128)} %plane.5, bf16[128,2,32,128]{3,2,1,0:T(8,128)(2,1)} %bitcast.14.tiles, ...), custom_call_target="tpu_custom_call", output_to_operand_aliasing={{0}: (13, {})} | custom-call | flops 8589934592 | bytes 41943040 | tf_op jit(solution)/shard_map/process_blocks/pallas_call | solution.py:306
  143.8 7.8 %all-to-all-start.3 = ((bf16[16,8,2,32,128]{4,3,2,1,0:T(8,128)(2,1)}), bf16[16,8,2,32,128]{4,3,2,1,0:T(8,128)(2,1)S(1)}, u32[]{:S(2)}, u32[]{:S(2)}) async-start(bf16[16,8,2,32,128]{4,3,2,1,0:T(8,128)(2,1)} %bitcast.44), calls=%async_computation.3 | async-start | bytes 4194304 | tf_op jit(solution)/shard_map/all_to_all | solution.py:480
  152.9 27.8 %process_blocks.5 = (f32[128,2,4,1024]{3,2,1,0:T(4,128)}, bf16[128,2,32,128]{3,2,1,0:T(8,128)(2,1)}) custom-call(s32[2]{0:T(128)} %pad_add_fusion.meta, s32[136]{0:T(256)} %copy-done.9, s32[128]{0:T(128)} %get-tuple-element.33.slot, s32[128]{0:T(128)} %plane.5, bf16[128,2,32,128]{3,2,1,0:T(8,128)(2,1)} %bitcast.42, ...), custom_call_target="tpu_custom_call", output_to_operand_aliasing={{0}: (13, {}), {1}: (14, {})} | custom-call | flops 6442450944 | bytes 31457280 | tf_op jit(solution)/shard_map/process_blocks/pallas_call | solution.py:306
  182.0 4.7 %sum_tiles.2 = bf16[64,64,128]{2,1,0:T(8,128)(2,1)} custom-call(s32[128]{0:T(128)} %reshape.165.requested, bf16[128,64,128]{2,1,0:T(8,128)(2,1)} %bitcast.39), custom_call_target="tpu_custom_call" | custom-call | flops 1048576 | bytes 4194304 | tf_op jit(solution)/shard_map/sum_tiles/pallas_call | solution.py:369
  186.7 5.6 %all-to-all-start.4 = ((bf16[16,8,2,32,128]{4,3,2,1,0:T(8,128)(2,1)}), bf16[16,8,2,32,128]{4,3,2,1,0:T(8,128)(2,1)S(1)}, u32[]{:S(2)}, u32[]{:S(2)}) async-start(bf16[16,8,2,32,128]{4,3,2,1,0:T(8,128)(2,1)} %bitcast.43), calls=%async_computation.4 | async-start | bytes 4194304 | tf_op jit(solution)/shard_map/all_to_all | solution.py:480
  192.3 8.5 %collective-permute-start.3 = (bf16[64,64,128]{2,1,0:T(8,128)(2,1)S(1)}, bf16[64,64,128]{2,1,0:T(8,128)(2,1)}, u32[]{:S(2)}, u32[]{:S(2)}) collective-permute-start(bf16[64,64,128]{2,1,0:T(8,128)(2,1)S(1)} %copy-done.5), channel_id=1, source_target_pairs={{0,16},{16,0},{1,17},{17,1},{2,18},{18,2},{3,19},{19,3},{4,20},{20... | collective-permute-start | bytes 3145736 | tf_op jit(solution)/shard_map/ppermute | solution.py:529
  201.5 50.5 %collective-permute-done.2 = f32[1]{0:T(128)} collective-permute-done((f32[1]{0:T(128)}, f32[1]{0:T(128)}, u32[]{:S(2)}, u32[]{:S(2)}) %collective-permute-start.2) | collective-permute-done | bytes 36 | tf_op jit(solution)/shard_map/ppermute | solution.py:486
  255.4 5.5 %sum_tiles.3 = f32[64,64,128]{2,1,0:T(8,128)} custom-call(s32[128]{0:T(128)} %reshape.163.requested, f32[1]{0:T(128)S(6)} %div.57.refs_0_, bf16[128,64,128]{2,1,0:T(8,128)(2,1)} %bitcast.40, bf16[64,64,128]{2,1,0:T(8,128)(2,1)} %collective-permute-done.3.refs_2_), custom_call_target="tpu_custom_call" | custom-call | flops 1048576 | bytes 4194304 | tf_op jit(solution)/shard_map/sum_tiles/pallas_call | solution.py:369
  (67 shorter events, 23.4 us)
Async XLA Ops:
  0.6 15.3 %copy-start.1 = (bf16[64,2,32,128]{3,2,1,0:T(8,128)(2,1)S(1)}, bf16[64,2,32,128]{3,2,1,0:T(8,128)(2,1)}, u32[]{:S(2)}) copy-start(bf16[64,2,32,128]{3,2,1,0:T(8,128)(2,1)} %param.19) | copy-start | bytes 3145732
  1.8 19.4 %collective-permute-start = (bf16[24,2,32,128]{3,2,1,0:T(8,128)(2,1)S(1)}, bf16[24,2,32,128]{3,2,1,0:T(8,128)(2,1)S(1)}, u32[]{:S(2)}, u32[]{:S(2)}) collective-permute-start(bf16[24,2,32,128]{3,2,1,0:T(8,128)(2,1)S(1)} %slice.28), channel_id=1, source_target_pairs={{0,16},{16,0},{1,17},{17,1},{2,18},{18,2},{3,19},{19,3},{4,20},{20... | collective-permute-start | bytes 1179656 | tf_op jit(solution)/shard_map/ppermute | solution.py:460
  10.8 8.3 %all-to-all-start = ((f32[16,1,17]{2,1,0:T(1,128)}), f32[16,1,17]{2,1,0:T(1,128)S(1)}, u32[]{:S(2)}, u32[]{:S(2)}) async-start(f32[16,1,17]{2,1,0:T(1,128)} %bitcast.4), calls=%async_computation | async-start | bytes 16384 | tf_op jit(solution)/shard_map/all_to_all | solution.py:480
  23.4 5.4 %copy-start.10 = (s32[128,1]{0,1:T(1,128)S(1)}, s32[128,1]{0,1:T(1,128)}, u32[]{:S(2)}) copy-start(s32[128,1]{0,1:T(1,128)} %param.16) | copy-start | bytes 1540
  23.4 8.5 %copy-start = (f32[128,1024]{1,0:T(8,128)S(1)}, f32[128,1024]{1,0:T(8,128)}, u32[]{:S(2)}) copy-start(f32[128,1024]{1,0:T(8,128)} %param.15) | copy-start | bytes 1572868
  23.4 55.0 %all-to-all-start.1 = ((bf16[16,8,2,32,128]{4,3,2,1,0:T(8,128)(2,1)}), bf16[16,8,2,32,128]{4,3,2,1,0:T(8,128)(2,1)S(1)}, u32[]{:S(2)}, u32[]{:S(2)}) async-start(bf16[16,8,2,32,128]{4,3,2,1,0:T(8,128)(2,1)} %bitcast.10), calls=%async_computation.1 | async-start | bytes 4194304 | tf_op jit(solution)/shard_map/all_to_all | solution.py:480
  31.3 0.5 copy-start.9
  31.9 1.6 copy-start.8
  33.5 41.4 %collective-permute-start.1 = (bf16[40,2,32,128]{3,2,1,0:T(8,128)(2,1)}, bf16[40,2,32,128]{3,2,1,0:T(8,128)(2,1)}, u32[]{:S(2)}, u32[]{:S(2)}) collective-permute-start(bf16[40,2,32,128]{3,2,1,0:T(8,128)(2,1)} %slice.27), channel_id=1, source_target_pairs={{0,16},{16,0},{1,17},{17,1},{2,18},{18,2},{3,19},{19,3},{4,20},{20... | collective-permute-start | bytes 1966088 | tf_op jit(solution)/shard_map/ppermute | solution.py:462
  41.5 21.5 %copy-start.7 = (s32[16,8]{1,0:T(8,128)S(1)}, s32[16,8]{1,0:T(8,128)}, u32[]{:S(2)}) copy-start(s32[16,8]{1,0:T(8,128)} %get-tuple-element.59) | copy-start | bytes 1540
  78.4 1.3 copy-start.4
  79.7 32.0 %all-to-all-start.2 = ((bf16[16,8,2,32,128]{4,3,2,1,0:T(8,128)(2,1)}), bf16[16,8,2,32,128]{4,3,2,1,0:T(8,128)(2,1)}, u32[]{:S(2)}, u32[]{:S(2)}) async-start(bf16[16,8,2,32,128]{4,3,2,1,0:T(8,128)(2,1)} %bitcast.6), calls=%async_computation.2 | async-start | bytes 4194304 | tf_op jit(solution)/shard_map/all_to_all | solution.py:480
  143.7 8.4 %copy-start.6 = (s32[16,8]{1,0:T(8,128)S(1)}, s32[16,8]{1,0:T(8,128)}, u32[]{:S(2)}) copy-start(s32[16,8]{1,0:T(8,128)} %get-tuple-element.58) | copy-start | bytes 1540
  143.8 36.9 %all-to-all-start.3 = ((bf16[16,8,2,32,128]{4,3,2,1,0:T(8,128)(2,1)}), bf16[16,8,2,32,128]{4,3,2,1,0:T(8,128)(2,1)S(1)}, u32[]{:S(2)}, u32[]{:S(2)}) async-start(bf16[16,8,2,32,128]{4,3,2,1,0:T(8,128)(2,1)} %bitcast.44), calls=%async_computation.3 | async-start | bytes 4194304 | tf_op jit(solution)/shard_map/all_to_all | solution.py:480
  180.7 1.3 copy-start.2
  186.7 5.6 %copy-start.5 = (bf16[64,64,128]{2,1,0:T(8,128)(2,1)S(1)}, bf16[64,64,128]{2,1,0:T(8,128)(2,1)}, u32[]{:S(2)}) copy-start(bf16[64,64,128]{2,1,0:T(8,128)(2,1)} %sum_tiles.2) | copy-start | bytes 3145732
  186.7 67.3 %all-to-all-start.4 = ((bf16[16,8,2,32,128]{4,3,2,1,0:T(8,128)(2,1)}), bf16[16,8,2,32,128]{4,3,2,1,0:T(8,128)(2,1)S(1)}, u32[]{:S(2)}, u32[]{:S(2)}) async-start(bf16[16,8,2,32,128]{4,3,2,1,0:T(8,128)(2,1)} %bitcast.43), calls=%async_computation.4 | async-start | bytes 4194304 | tf_op jit(solution)/shard_map/all_to_all | solution.py:480
  192.3 61.7 %collective-permute-start.3 = (bf16[64,64,128]{2,1,0:T(8,128)(2,1)S(1)}, bf16[64,64,128]{2,1,0:T(8,128)(2,1)}, u32[]{:S(2)}, u32[]{:S(2)}) collective-permute-start(bf16[64,64,128]{2,1,0:T(8,128)(2,1)S(1)} %copy-done.5), channel_id=1, source_target_pairs={{0,16},{16,0},{1,17},{17,1},{2,18},{18,2},{3,19},{19,3},{4,20},{20... | collective-permute-start | bytes 3145736 | tf_op jit(solution)/shard_map/ppermute | solution.py:529
  201.5 50.5 %collective-permute-start.2 = (f32[1]{0:T(128)}, f32[1]{0:T(128)}, u32[]{:S(2)}, u32[]{:S(2)}) collective-permute-start(f32[1]{0:T(128)} %bitcast.16), channel_id=1, source_target_pairs={{0,16},{16,0},{1,17},{17,1},{2,18},{18,2},{3,19},{19,3},{4,20},{20... | collective-permute-start | bytes 20 | tf_op jit(solution)/shard_map/ppermute | solution.py:486
  254.0 1.3 copy-start.3

commit v5 on v4

--- a/solution.py
+++ b/solution.py
@@ -10,10 +10,13 @@
 from jax.sharding import Mesh
 from jax.sharding import PartitionSpec as P
 
+AXES = ("facet", "vis")
 BATCH = 8
 LANES = 512
 TILE = 128
 ROWS = 8
+OPENING = 2
+MIRROR_PARTS = (0, 3, 8)
 UNROLL = 8
 VMEM_BYTES = 60 * 1024 * 1024
 SIN_TERMS = [(-1.0) ** i * (2.0 * math.pi) ** (2 * i + 1) / math.factorial(2 * i + 1) for i in range(8)]
@@ -338,44 +341,42 @@
     )(meta, order, slot, plane, *operands)
 
 
-def sum_kernel(requested, *refs, carried):
-    if carried:
-        scale_ref, arrived_ref, *old_refs, out_ref, total_ref = refs
-        start = 0
-        for old_ref in old_refs:
-            rows = old_ref.shape[1]
-            total_ref[:, start : start + rows] = old_ref[...].astype(jnp.float32)
-            start += rows
+def sum_kernel(requested, scale_ref, *refs, last):
+    if last:
+        old_ref, arrived_ref, out_ref, total_ref = refs
+        total_ref[: out_ref.shape[0]] = old_ref[...]
     else:
         arrived_ref, out_ref, total_ref = refs
         total_ref[...] = jnp.zeros_like(total_ref)
-
-    @pl.loop(0, arrived_ref.shape[0])
+    unused = out_ref.shape[0]
+    slots = arrived_ref.shape[0]
+    together = math.gcd(slots, 8)
+
+    @pl.loop(0, slots // together)
     def _(i):
-        tile = requested[i]
-
-        @pl.when(tile >= 0)
-        def _():
-            total_ref[tile] += arrived_ref[i].astype(jnp.float32)
-
-    total = total_ref[...] * scale_ref[0] if carried else total_ref[...]
-    out_ref[...] = total.astype(out_ref.dtype)
-
-
-def sum_tiles(requested, arrived, owned, dtype, scale=None, old=()):
+        for k in range(together):
+            at = i * together + k
+            tile = requested[at]
+            total_ref[jnp.where(tile < 0, unused, tile)] += arrived_ref[at].astype(jnp.float32)
+
+    total = total_ref[:unused]
+    out_ref[...] = total * scale_ref[0] if last else total
+
+
+def sum_tiles(requested, scale, arrived, owned, old=None):
     shape = (owned,) + arrived.shape[1:]
-    vmem, smem = pl.BlockSpec(memory_space=pltpu.VMEM), pl.BlockSpec(memory_space=pltpu.SMEM)
-    carried = len(old) > 0
+    operands = [arrived] if old is None else [old, arrived]
+    vmem = pl.BlockSpec(memory_space=pltpu.VMEM)
     return pl.pallas_call(
-        functools.partial(sum_kernel, carried=carried),
-        out_shape=jax.ShapeDtypeStruct(shape, dtype),
-        in_specs=[smem, smem, vmem] + [vmem] * len(old) if carried else [smem, vmem],
+        functools.partial(sum_kernel, last=old is not None),
+        out_shape=jax.ShapeDtypeStruct(shape, jnp.float32),
+        in_specs=[pl.BlockSpec(memory_space=pltpu.SMEM)] * 2 + [vmem] * len(operands),
         out_specs=vmem,
-        scratch_shapes=[pltpu.VMEM(shape, jnp.float32)],
+        scratch_shapes=[pltpu.VMEM((owned + 1,) + shape[1:], jnp.float32)],
         compiler_params=pltpu.CompilerParams(vmem_limit_bytes=VMEM_BYTES),
         cost_estimate=pl.CostEstimate(flops=arrived.size, bytes_accessed=arrived.size * 4, transcendentals=0),
         name="sum_tiles",
-    )(requested, *((scale, arrived, *old) if carried else (arrived,)))
+    )(requested, scale, *operands)
 
 
 def table_kernel(planes_ref, signs_ref, columns_ref, spread_ref, gather_ref, repeat_ref, left_ref, back_ref, right_ref, turned_ref):
@@ -447,106 +448,106 @@
     )(w_kernels.reshape(planes, size, width), *constants)
 
 
+def exchange(operand):
+    return lax.all_to_all(operand, AXES, split_axis=0, concat_axis=0, tiled=True)
+
+
+def request_kernel(target_ref, slot_ref, weight_ref, out_ref, *, capacity):
+    groups, lanes = out_ref.shape
+    blocks = target_ref.shape[1]
+
+    def iota(shape, dim):
+        return lax.broadcasted_iota(jnp.int32, shape, dim)
+
+    named = target_ref[...] == iota((groups, blocks), 0)
+    named_bits = named.astype(jnp.float32).astype(jnp.bfloat16)
+    ahead = (iota((blocks, blocks), 0) < iota((blocks, blocks), 1)).astype(jnp.float32).astype(jnp.bfloat16)
+    before = rows_dot(named_bits, ahead, 1, 0)
+    rank = jnp.sum(jnp.where(named, before, 0.0), axis=0, keepdims=True).astype(jnp.int32)
+    asked = jnp.where(rank == iota((lanes, blocks), 0), slot_ref[...] + 1, 0)
+    wanted = rows_dot(named_bits, asked.astype(jnp.float32).astype(jnp.bfloat16), 1, 1)
+    weight = jnp.sum(weight_ref[...])
+    out_ref[...] = jnp.where(iota((groups, lanes), 1) == capacity, weight, wanted)
+
+
+def requests_of(target, tile_slot, vis_weight, groups, capacity):
+    vmem = pl.BlockSpec(memory_space=pltpu.VMEM)
+    return pl.pallas_call(
+        functools.partial(request_kernel, capacity=capacity),
+        out_shape=jax.ShapeDtypeStruct((groups, TILE), jnp.float32),
+        in_specs=[vmem] * 3,
+        out_specs=vmem,
+        compiler_params=pltpu.CompilerParams(vmem_limit_bytes=VMEM_BYTES),
+        name="requests_of",
+    )(target.reshape(1, -1), tile_slot.reshape(1, -1), vis_weight)
+
+
 def shards(vis_obs, uv_coords, vis_weight, block_group, tile_slot, w_plane, model_tiles, w_kernels):
-    blocks, _, pols, vis_count = vis_obs.shape
-    peers = lax.axis_size("peer")
-    groups = 2 * peers
+    blocks = vis_obs.shape[0]
+    pols = vis_obs.shape[2]
+    groups = lax.axis_size(AXES)
     owned = model_tiles.shape[0]
     tile_shape = model_tiles.shape[1:]
-    flat_shape = (tile_shape[0] * tile_shape[1], tile_shape[2])
     capacity = max(2, 2 * blocks // groups)
-    swap = [(0, 1), (1, 0)]
-    cut = 3 * owned // 8
-    mirrored_low = lax.ppermute(model_tiles[:cut], "half", swap)
-    high_tiles, mirrored_low = lax.optimization_barrier((model_tiles[cut:], mirrored_low))
-    mirrored_high = lax.ppermute(high_tiles, "half", swap)
-    mirrored = jnp.concatenate([mirrored_low, mirrored_high], axis=0)
-
+    early = max(1, 3 * capacity // 8)
     target = block_group[:, 0]
-    far = lax.rem(lax.div(target, peers) + lax.axis_index("half"), 2)
-    peer = lax.rem(target, peers)
-    holder = far * peers + peer
-    markers = holder[:, None] == jnp.arange(groups, dtype=jnp.int32)[None, :]
+    markers = target[:, None] == jnp.arange(groups, dtype=jnp.int32)[None, :]
     counts = markers.astype(jnp.int32)
     before = jnp.cumsum(counts, axis=0) - counts
     rank = jnp.sum(jnp.where(markers, before, 0), axis=1)
-    ranks = rank[:, None] == jnp.arange(capacity, dtype=jnp.int32)[None, :]
-    wanted = jnp.sum(
-        jnp.where(markers[:, :, None] & ranks[:, None, :], (tile_slot + 1)[:, None, None], 0), axis=0
-    ).astype(jnp.float32)
-    own_weight = jnp.broadcast_to(jnp.sum(vis_weight)[None, None], (peers, 1))
-
-    def exchange(operand):
-        return lax.all_to_all(operand, "peer", split_axis=0, concat_axis=0, tiled=True)
-
-    answers = exchange(jnp.concatenate([wanted[:peers], wanted[peers:], own_weight], axis=1))
-    near_request = answers[:, :capacity].astype(jnp.int32) - 1
-    far_request = answers[:, capacity : 2 * capacity].astype(jnp.int32) - 1
-    half_weight = jnp.sum(answers[:, 2 * capacity]).reshape(1)
-    weight_sum = half_weight + lax.ppermute(half_weight, "half", swap)
-    scaling = blocks * groups * vis_count / weight_sum
+    answers = exchange(requests_of(target, tile_slot, vis_weight, groups, capacity))
+    requested = answers[:, :capacity].astype(jnp.int32) - 1
+    weight_sum = jnp.sum(answers[:, capacity])
+    scaling = blocks * groups * vis_obs.shape[-1] / weight_sum
+    scaling = scaling.reshape(1)
 
     tables = kernel_tables(w_kernels, pols)
-    near_count = blocks - jnp.sum(far)
-    far_base = (near_count + BATCH - 1) // BATCH * BATCH
-    item = jnp.where(far == 1, far_base + jnp.cumsum(far) - 1, jnp.cumsum(1 - far) - 1)
+    is_late = rank >= early
+    late = is_late.astype(jnp.int32)
+    early_count = blocks - jnp.sum(late)
+    late_base = (early_count + BATCH - 1) // BATCH * BATCH
+    item = jnp.where(is_late, late_base + jnp.cumsum(late) - 1, jnp.cumsum(1 - late) - 1)
     items = jnp.arange(blocks + BATCH, dtype=jnp.int32)
     order = jnp.sum(
         jnp.where(items[:, None] == item[None, :], jnp.arange(blocks, dtype=jnp.int32)[None, :], 0), axis=1
     )
-    slot = peer * capacity + rank
+    slot = jnp.where(is_late, target * (capacity - early) + rank - early, target * early + rank)
     u = jnp.take(uv_coords[:, 0], order, axis=0, mode="clip")
     v = jnp.take(uv_coords[:, 1], order, axis=0, mode="clip")
     weight = jnp.take(vis_weight, order, axis=0, mode="clip")
 
-    def choose(tiles, request):
-        chosen = jnp.take(tiles, jnp.maximum(request, 0).reshape(-1), axis=0, mode="clip")
-        return chosen.reshape(request.shape + tile_shape)
+    def choose(part):
+        chosen = jnp.take(model_tiles, jnp.maximum(part, 0).reshape(-1), axis=0, mode="clip")
+        return chosen.reshape(part.shape + tile_shape)
 
     def send_tiles(chosen):
         return exchange(chosen).reshape((-1,) + tile_shape)
 
     def send_back(part):
-        return exchange(part.reshape((peers, capacity) + part.shape[1:])).reshape((peers * capacity,) + part.shape[1:])
-
-    near_request, mirrored_low = lax.optimization_barrier((near_request, mirrored_low))
-    near_tiles = send_tiles(choose(model_tiles, near_request))
+        returned = exchange(part.reshape((groups, -1) + tile_shape))
+        return returned.reshape(-1, tile_shape[0] * tile_shape[1], tile_shape[2])
+
+    first, second = requested[:, :early], requested[:, early:]
+    tiles_first = send_tiles(choose(first))
     chosen, order, slot, u, v, weight, tables = lax.optimization_barrier(
-        (choose(mirrored, far_request), order, slot, u, v, weight, tables)
+        (choose(second), order, slot, u, v, weight, tables)
     )
-    far_tiles = send_tiles(chosen)
+    tiles_second = send_tiles(chosen)
     given = (vis_obs, u, v, weight, tables)
     zero = jnp.zeros((), jnp.int32)
-    opening = max(BATCH, blocks // 4 // BATCH * BATCH)
-    first_count = jnp.minimum(near_count, opening)
-    residual, near_sent = process_blocks(opening, zero, first_count, order, slot, w_plane, near_tiles, *given)
-    residual, far_sent = process_blocks(
-        blocks, far_base, blocks - near_count, order, slot, w_plane, far_tiles, *given, (residual,)
+    residual, sent_first = process_blocks(
+        blocks, zero, early_count, order, slot, w_plane, tiles_first, *given
     )
-    far_sum = sum_tiles(
-        far_request.reshape(-1), send_back(far_sent).reshape((-1,) + flat_shape), owned, jnp.bfloat16
+    late_most = blocks * (capacity - early) // capacity
+    residual, sent_second = process_blocks(
+        late_most, late_base, blocks - early_count, order, slot, w_plane, tiles_second, *given, (residual,)
     )
-    relayed = lax.ppermute(far_sum, "half", swap)
-    residual, near_sent = process_blocks(
-        blocks - opening,
-        zero + opening,
-        near_count - first_count,
-        order,
-        slot,
-        w_plane,
-        near_tiles,
-        *given,
-        (residual, near_sent),
-    )
-    near_sent, far_sum = lax.optimization_barrier((near_sent, far_sum))
-    returned = send_back(near_sent).reshape((-1,) + flat_shape)
-    summed = sum_tiles(near_request.reshape(-1), returned, owned, jnp.float32, scaling, [relayed])
+    summed = sum_tiles(first.reshape(-1), scaling, send_back(sent_first), owned)
+    summed = sum_tiles(second.reshape(-1), scaling, send_back(sent_second), owned, summed)
     return residual, summed.reshape(model_tiles.shape)
 
 
 def solution(mesh):
-    devices = mesh.devices.reshape(2, -1)
-    halves = Mesh(devices, ("half", "peer"))
-    rows = P(("half", "peer"))
+    rows = P(AXES)
     in_specs = (rows,) * 7 + (P(),)
-    return jax.shard_map(shards, mesh=halves, in_specs=in_specs, out_specs=(rows, rows), check_vma=False)
+    return jax.shard_map(shards, mesh=mesh, in_specs=in_specs, out_specs=(rows, rows), check_vma=False)

time: 260 us -> 237 us (0.912)
  the two profiles are of different devices: /device:TPU:10 before, /device:TPU:0 now
where the time goes in v5:
time: 237 us; the launch traced here: 236 us
  Pallas kernels  105 us (44%)
  waiting for transfers between devices  81.1 us (34%)
  starting transfers between devices  15.3 us (6%)
  blocking collectives  14.4 us (6%)
  local copies, waits for them, and re-layouts  13.4 us (6%)
  other arithmetic  4.92 us (2%)
  between operations  2.66 us (1%)
    all_to_all x4, waiting for transfers between devices, exchange(): lax.all_to_all(operand, AXES, split_axis=0, concat_axis=0, tiled=True)  81.1 us
    pallas_call x2, Pallas kernels, process_blocks(): pl.pallas_call(functools.partial(block_kernel, carried=len(carried)), out...  74.5 us
    pallas_call x1, Pallas kernels, kernel_tables(): pl.pallas_call(table_kernel, grid=(planes // part,), out_shape=[jax.Shape...  19.6 us
    all_to_all x4, starting transfers between devices, exchange(): lax.all_to_all(operand, AXES, split_axis=0, concat_axis=0, tiled=True)  15.3 us
    all_to_all x1, blocking collectives, exchange(): lax.all_to_all(operand, AXES, split_axis=0, concat_axis=0, tiled=True)  14.4 us
    pallas_call x2, Pallas kernels, sum_tiles(): pl.pallas_call(functools.partial(sum_kernel, last=old is not None), out_s...  8.7 us
  transfers between devices with their start and end apart: 4, of which 4 were waited for; matrix products, arithmetic and copies ran while one was open for 6% of the time, Pallas kernels for 41%

profile of v5, /device:TPU:0, one launch (start us, length us, event | category | flops | bytes accessed | tf_op | source)
XLA Modules:
  0.0 236.5 jit_solution(16212054903713845016)
XLA Ops:
  0.6 2.1 requests_of.1
  2.7 14.4 %all_to_all.32 = f32[32,1,128]{2,1,0:T(1,128)S(1)} all-to-all(f32[32,1,128]{2,1,0:T(1,128)} %bitcast.37), channel_id=1, replica_groups=mesh['facet'=4,'vis'=8] {'facet','vis'}, dimensions={0} | all-to-all | bytes 32768 | tf_op jit(solution)/shard_map/all_to_all | solution.py:452
  17.2 1.9 gather_fusion.4
  19.2 3.5 %all-to-all-start.2 = ((bf16[32,3,2,32,128]{4,3,2,1,0:T(8,128)(2,1)}), bf16[32,3,2,32,128]{4,3,2,1,0:T(8,128)(2,1)}, u32[]{:S(2)}, u32[]{:S(2)}) async-start(bf16[32,3,2,32,128]{4,3,2,1,0:T(8,128)(2,1)} %bitcast.15), calls=%async_computation.2 | async-start | bytes 3145728 | tf_op jit(solution)/shard_map/all_to_all | solution.py:452
  25.9 1.6 gather_fusion.3
  27.6 0.8 fusion.3
  28.6 1.6 gather_fusion.2
  30.2 1.6 gather_fusion.1
  31.9 19.6 %kernel_tables.1 = (bf16[32,64,64]{2,1,0:T(8,128)(2,1)}, bf16[32,64,64]{2,1,0:T(8,128)(2,1)}, bf16[32,64,256]{2,1,0:T(8,128)(2,1)}, bf16[32,256,256]{2,1,0:T(8,128)(2,1)}) custom-call(bf16[32,64,32]{2,1,0:T(8,128)(2,1)} %bitcast.42, bf16[128,64]{1,0:T(8,128)(2,1)} %constant.60.clone.signs_ref, bf16[128,64]{1,0:T(8,128)(2,1)} %constant.61.clone.columns_ref, ...), custom_call_target="tpu_custom_call" | custom-call | flops 536870912 | bytes 4194304 | tf_op jit(solution)/shard_map/kernel_tables/pallas_call | solution.py:439
  51.6 2.6 %gather_fusion = bf16[160,2,32,128]{3,2,1,0:T(8,128)(2,1)} fusion(bf16[64,2,32,128]{3,2,1,0:T(8,128)(2,1)S(1)} %copy-done, s32[1024]{0:T(1024)S(1)} %pad_clamp_fusion.2), kind=kCustom, calls=%fused_computation | custom fusion | bytes 5243520 | tf_op jit(solution)/shard_map/jit(_take)/gather | solution.py:520
  54.2 6.4 %all-to-all-done.2 = bf16[32,3,2,32,128]{4,3,2,1,0:T(8,128)(2,1)} async-done(((bf16[32,3,2,32,128]{4,3,2,1,0:T(8,128)(2,1)}), bf16[32,3,2,32,128]{4,3,2,1,0:T(8,128)(2,1)}, u32[]{:S(2)}, u32[]{:S(2)}) %all-to-all-start.2) | async-done | bytes 1572896 | tf_op jit(solution)/shard_map/all_to_all | solution.py:452
  60.6 3.7 %all-to-all-start.1 = ((bf16[32,5,2,32,128]{4,3,2,1,0:T(8,128)(2,1)}), bf16[32,5,2,32,128]{4,3,2,1,0:T(8,128)(2,1)}, u32[]{:S(2)}, u32[]{:S(2)}) async-start(bf16[32,5,2,32,128]{4,3,2,1,0:T(8,128)(2,1)} %bitcast.30), calls=%async_computation.1 | async-start | bytes 5242880 | tf_op jit(solution)/shard_map/all_to_all | solution.py:452
  65.5 46.8 %process_blocks.2 = (f32[128,2,4,1024]{3,2,1,0:T(4,128)}, bf16[96,2,32,128]{3,2,1,0:T(8,128)(2,1)}) custom-call(s32[2]{0:T(128)} %pad_add_fusion.1.meta, s32[136]{0:T(256)} %copy-done.5, s32[128]{0:T(128)} %get-tuple-element.25.slot, s32[128]{0:T(128)} %plane.3, bf16[96,2,32,128]{3,2,1,0:T(8,128)(2,1)} %bitcast.16.tiles, f32[128,2,4,1024]{3,2,1,0:T(4,128)} %observed.3, ...), custom_call_target="tpu_custom_call" | custom-call | flops 8589934592 | bytes 41943040 | tf_op jit(solution)/shard_map/process_blocks/pallas_call | solution.py:309
  112.3 12.1 %all-to-all-done.1 = bf16[32,5,2,32,128]{4,3,2,1,0:T(8,128)(2,1)} async-done(((bf16[32,5,2,32,128]{4,3,2,1,0:T(8,128)(2,1)}), bf16[32,5,2,32,128]{4,3,2,1,0:T(8,128)(2,1)}, u32[]{:S(2)}, u32[]{:S(2)}) %all-to-all-start.1) | async-done | bytes 2621472 | tf_op jit(solution)/shard_map/all_to_all | solution.py:452
  124.4 4.2 %all-to-all-start.3 = ((bf16[32,3,2,32,128]{4,3,2,1,0:T(8,128)(2,1)}), bf16[32,3,2,32,128]{4,3,2,1,0:T(8,128)(2,1)S(1)}, u32[]{:S(2)}, u32[]{:S(2)}) async-start(bf16[32,3,2,32,128]{4,3,2,1,0:T(8,128)(2,1)} %bitcast.34), calls=%async_computation.3 | async-start | bytes 3145728 | tf_op jit(solution)/shard_map/all_to_all | solution.py:452
  128.6 1.2 pad_add_fusion.meta
  129.8 27.7 %process_blocks.3 = (f32[128,2,4,1024]{3,2,1,0:T(4,128)}, bf16[160,2,32,128]{3,2,1,0:T(8,128)(2,1)}) custom-call(s32[2]{0:T(128)} %pad_add_fusion.meta, s32[136]{0:T(256)} %copy-done.5, s32[128]{0:T(128)} %get-tuple-element.25.slot, s32[128]{0:T(128)} %plane.3, bf16[160,2,32,128]{3,2,1,0:T(8,128)(2,1)} %bitcast.13.tiles, ...), custom_call_target="tpu_custom_call", output_to_operand_aliasing={{0}: (13, {})} | custom-call | flops 5368709120 | bytes 26214400 | tf_op jit(solution)/shard_map/process_blocks/pallas_call | solution.py:309
  157.5 8.7 %all-to-all-done.3 = bf16[32,3,2,32,128]{4,3,2,1,0:T(8,128)(2,1)S(1)} async-done(((bf16[32,3,2,32,128]{4,3,2,1,0:T(8,128)(2,1)}), bf16[32,3,2,32,128]{4,3,2,1,0:T(8,128)(2,1)S(1)}, u32[]{:S(2)}, u32[]{:S(2)}) %all-to-all-start.3) | async-done | bytes 1572896 | tf_op jit(solution)/shard_map/all_to_all | solution.py:452
  166.2 1.1 copy-done.2
  167.3 3.9 %all-to-all-start.4 = ((bf16[32,5,2,32,128]{4,3,2,1,0:T(8,128)(2,1)}), bf16[32,5,2,32,128]{4,3,2,1,0:T(8,128)(2,1)}, u32[]{:S(2)}, u32[]{:S(2)}) async-start(bf16[32,5,2,32,128]{4,3,2,1,0:T(8,128)(2,1)} %bitcast.32), calls=%async_computation.4 | async-start | bytes 5242880 | tf_op jit(solution)/shard_map/all_to_all | solution.py:452
  171.2 0.7 reshape.134.requested
  173.8 3.6 %sum_tiles.2.refs_0_ = f32[64,64,128]{2,1,0:T(8,128)} custom-call(s32[96]{0:T(128)} %reshape.134.requested, f32[1]{0:T(128)} %bitcast.17.scale_ref, bf16[96,64,128]{2,1,0:T(8,128)(2,1)} %bitcast.31), custom_call_target="tpu_custom_call" | custom-call | flops 786432 | bytes 3145728 | tf_op jit(solution)/shard_map/sum_tiles/pallas_call | solution.py:370
  177.4 53.9 %all-to-all-done.4 = bf16[32,5,2,32,128]{4,3,2,1,0:T(8,128)(2,1)} async-done(((bf16[32,5,2,32,128]{4,3,2,1,0:T(8,128)(2,1)}), bf16[32,5,2,32,128]{4,3,2,1,0:T(8,128)(2,1)}, u32[]{:S(2)}, u32[]{:S(2)}) %all-to-all-start.4) | async-done | bytes 2621472 | tf_op jit(solution)/shard_map/all_to_all | solution.py:452
  231.3 5.1 %sum_tiles.3 = f32[64,64,128]{2,1,0:T(8,128)} custom-call(s32[160]{0:T(256)} %reshape.132.requested, f32[1]{0:T(128)} %bitcast.17.scale_ref, f32[64,64,128]{2,1,0:T(8,128)} %sum_tiles.2.refs_0_, bf16[160,64,128]{2,1,0:T(8,128)(2,1)} %bitcast.21.refs_1_), custom_call_target="tpu_custom_call" | custom-call | flops 1310720 | bytes 5242880 | tf_op jit(solution)/shard_map/sum_tiles/pallas_call | solution.py:370
  (36 shorter events, 5.0 us)
Async XLA Ops:
  0.6 16.6 %copy-start = (bf16[64,2,32,128]{3,2,1,0:T(8,128)(2,1)S(1)}, bf16[64,2,32,128]{3,2,1,0:T(8,128)(2,1)}, u32[]{:S(2)}) copy-start(bf16[64,2,32,128]{3,2,1,0:T(8,128)(2,1)} %param.19) | copy-start | bytes 3145732
  17.2 5.5 %copy-start.4 = (s32[128,1]{0,1:T(1,128)S(1)}, s32[128,1]{0,1:T(1,128)}, u32[]{:S(2)}) copy-start(s32[128,1]{0,1:T(1,128)} %param.16) | copy-start | bytes 1540
  19.2 6.7 %copy-start.1 = (f32[128,1024]{1,0:T(8,128)S(1)}, f32[128,1024]{1,0:T(8,128)}, u32[]{:S(2)}) copy-start(f32[128,1024]{1,0:T(8,128)} %weight_ref.1) | copy-start | bytes 1572868
  19.2 41.4 %all-to-all-start.2 = ((bf16[32,3,2,32,128]{4,3,2,1,0:T(8,128)(2,1)}), bf16[32,3,2,32,128]{4,3,2,1,0:T(8,128)(2,1)}, u32[]{:S(2)}, u32[]{:S(2)}) async-start(bf16[32,3,2,32,128]{4,3,2,1,0:T(8,128)(2,1)} %bitcast.15), calls=%async_computation.2 | async-start | bytes 3145728 | tf_op jit(solution)/shard_map/all_to_all | solution.py:452
  24.9 2.7 %copy-start.3 = (f32[128,2,1024]{2,1,0:T(2,128)S(1)}, f32[128,2,1024]{2,1,0:T(2,128)}, u32[]{:S(2)}) copy-start(f32[128,2,1024]{2,1,0:T(2,128)} %param.14) | copy-start | bytes 3145732
  25.9 2.5 %copy-start.5 = (s32[136]{0:T(256)}, s32[136]{0:T(256)S(1)}, u32[]{:S(2)}) copy-start(s32[136]{0:T(256)S(1)} %select_reduce_fusion.order) | copy-start | bytes 1636
  60.6 63.8 %all-to-all-start.1 = ((bf16[32,5,2,32,128]{4,3,2,1,0:T(8,128)(2,1)}), bf16[32,5,2,32,128]{4,3,2,1,0:T(8,128)(2,1)}, u32[]{:S(2)}, u32[]{:S(2)}) async-start(bf16[32,5,2,32,128]{4,3,2,1,0:T(8,128)(2,1)} %bitcast.30), calls=%async_computation.1 | async-start | bytes 5242880 | tf_op jit(solution)/shard_map/all_to_all | solution.py:452
  124.4 41.8 %all-to-all-start.3 = ((bf16[32,3,2,32,128]{4,3,2,1,0:T(8,128)(2,1)}), bf16[32,3,2,32,128]{4,3,2,1,0:T(8,128)(2,1)S(1)}, u32[]{:S(2)}, u32[]{:S(2)}) async-start(bf16[32,3,2,32,128]{4,3,2,1,0:T(8,128)(2,1)} %bitcast.34), calls=%async_computation.3 | async-start | bytes 3145728 | tf_op jit(solution)/shard_map/all_to_all | solution.py:452
  166.2 1.1 copy-start.2
  167.3 64.0 %all-to-all-start.4 = ((bf16[32,5,2,32,128]{4,3,2,1,0:T(8,128)(2,1)}), bf16[32,5,2,32,128]{4,3,2,1,0:T(8,128)(2,1)}, u32[]{:S(2)}, u32[]{:S(2)}) async-start(bf16[32,5,2,32,128]{4,3,2,1,0:T(8,128)(2,1)} %bitcast.32), calls=%async_computation.4 | async-start | bytes 5242880 | tf_op jit(solution)/shard_map/all_to_all | solution.py:452

commit v6 on v5

--- a/solution.py
+++ b/solution.py
@@ -318,7 +318,7 @@
             in_specs=in_specs,
             out_specs=(hbm, hbm),
             scratch_shapes=[
-                pltpu.VMEM((vis_count // TILE, BATCH * (width + ROWS), TILE), jnp.float32),
+                pltpu.VMEM((vis_count // TILE, BATCH * (width + ROWS + 1), TILE), jnp.float32),
                 pltpu.VMEM((width // 2 + 2, BATCH, vis_count), jnp.float32),
                 pltpu.VMEM((2, BATCH) + tile_shape, jnp.bfloat16),
                 pltpu.VMEM((2, BATCH) + vis_shape, jnp.float32),
@@ -373,7 +373,7 @@
         in_specs=[pl.BlockSpec(memory_space=pltpu.SMEM)] * 2 + [vmem] * len(operands),
         out_specs=vmem,
         scratch_shapes=[pltpu.VMEM((owned + 1,) + shape[1:], jnp.float32)],
-        compiler_params=pltpu.CompilerParams(vmem_limit_bytes=VMEM_BYTES),
+        compiler_params=pltpu.CompilerParams(vmem_limit_bytes=VMEM_BYTES // 4),
         cost_estimate=pl.CostEstimate(flops=arrived.size, bytes_accessed=arrived.size * 4, transcendentals=0),
         name="sum_tiles",
     )(requested, scale, *operands)

time: 237 us -> 237 us (level)
  Pallas kernels: 105 us -> 102 us
    pallas_call x2, Pallas kernels: 8.7 us -> 5.8 us  [sum_tiles(): pl.pallas_call(functools.partial(sum_kernel, last=old is not None), out_s...]
  transfers between devices with their start and end apart: 4 -> 4, of which waited for: 4 -> 4; matrix products, arithmetic and copies ran while one was open for 6% -> 6% of each run, Pallas kernels for 41% -> 40%
where the time goes in v6:
time: 237 us; the launch traced here: 236 us
  Pallas kernels  102 us (43%)
  waiting for transfers between devices  83.2 us (35%)
  starting transfers between devices  15.3 us (6%)
  blocking collectives  14.4 us (6%)
  local copies, waits for them, and re-layouts  13.7 us (6%)
  other arithmetic  4.94 us (2%)
  between operations  2.73 us (1%)
    all_to_all x4, waiting for transfers between devices, exchange(): lax.all_to_all(operand, AXES, split_axis=0, concat_axis=0, tiled=True)  83.2 us
    pallas_call x2, Pallas kernels, process_blocks(): pl.pallas_call(functools.partial(block_kernel, carried=len(carried)), out...  74.2 us
    pallas_call x1, Pallas kernels, kernel_tables(): pl.pallas_call(table_kernel, grid=(planes // part,), out_shape=[jax.Shape...  19.6 us
    all_to_all x4, starting transfers between devices, exchange(): lax.all_to_all(operand, AXES, split_axis=0, concat_axis=0, tiled=True)  15.3 us
    all_to_all x1, blocking collectives, exchange(): lax.all_to_all(operand, AXES, split_axis=0, concat_axis=0, tiled=True)  14.4 us
    pallas_call x2, Pallas kernels, sum_tiles(): pl.pallas_call(functools.partial(sum_kernel, last=old is not None), out_s...  5.8 us
  transfers between devices with their start and end apart: 4, of which 4 were waited for; matrix products, arithmetic and copies ran while one was open for 6% of the time, Pallas kernels for 40%

profile of v6, /device:TPU:0, one launch (start us, length us, event | category | flops | bytes accessed | tf_op | source)
XLA Modules:
  0.0 235.9 jit_solution(5002706643739545360)
XLA Ops:
  0.6 2.1 requests_of.1
  2.7 14.4 %all_to_all.32 = f32[32,1,128]{2,1,0:T(1,128)S(1)} all-to-all(f32[32,1,128]{2,1,0:T(1,128)} %bitcast.37), channel_id=1, replica_groups=mesh['facet'=4,'vis'=8] {'facet','vis'}, dimensions={0} | all-to-all | bytes 32768 | tf_op jit(solution)/shard_map/all_to_all | solution.py:452
  17.2 1.9 gather_fusion.4
  19.2 3.5 %all-to-all-start.2 = ((bf16[32,3,2,32,128]{4,3,2,1,0:T(8,128)(2,1)}), bf16[32,3,2,32,128]{4,3,2,1,0:T(8,128)(2,1)}, u32[]{:S(2)}, u32[]{:S(2)}) async-start(bf16[32,3,2,32,128]{4,3,2,1,0:T(8,128)(2,1)} %bitcast.15), calls=%async_computation.2 | async-start | bytes 3145728 | tf_op jit(solution)/shard_map/all_to_all | solution.py:452
  25.9 1.6 gather_fusion.3
  27.6 0.8 fusion.3
  28.6 1.6 gather_fusion.2
  30.2 1.6 gather_fusion.1
  31.9 19.6 %kernel_tables.1 = (bf16[32,64,64]{2,1,0:T(8,128)(2,1)}, bf16[32,64,64]{2,1,0:T(8,128)(2,1)}, bf16[32,64,256]{2,1,0:T(8,128)(2,1)}, bf16[32,256,256]{2,1,0:T(8,128)(2,1)}) custom-call(bf16[32,64,32]{2,1,0:T(8,128)(2,1)} %bitcast.42, bf16[128,64]{1,0:T(8,128)(2,1)} %constant.60.clone.signs_ref, bf16[128,64]{1,0:T(8,128)(2,1)} %constant.61.clone.columns_ref, ...), custom_call_target="tpu_custom_call" | custom-call | flops 536870912 | bytes 4194304 | tf_op jit(solution)/shard_map/kernel_tables/pallas_call | solution.py:439
  51.6 2.6 %gather_fusion = bf16[160,2,32,128]{3,2,1,0:T(8,128)(2,1)} fusion(bf16[64,2,32,128]{3,2,1,0:T(8,128)(2,1)S(1)} %copy-done, s32[1024]{0:T(1024)S(1)} %pad_clamp_fusion.2), kind=kCustom, calls=%fused_computation | custom fusion | bytes 5243520 | tf_op jit(solution)/shard_map/jit(_take)/gather | solution.py:520
  54.2 6.4 %all-to-all-done.2 = bf16[32,3,2,32,128]{4,3,2,1,0:T(8,128)(2,1)} async-done(((bf16[32,3,2,32,128]{4,3,2,1,0:T(8,128)(2,1)}), bf16[32,3,2,32,128]{4,3,2,1,0:T(8,128)(2,1)}, u32[]{:S(2)}, u32[]{:S(2)}) %all-to-all-start.2) | async-done | bytes 1572896 | tf_op jit(solution)/shard_map/all_to_all | solution.py:452
  60.6 3.7 %all-to-all-start.1 = ((bf16[32,5,2,32,128]{4,3,2,1,0:T(8,128)(2,1)}), bf16[32,5,2,32,128]{4,3,2,1,0:T(8,128)(2,1)}, u32[]{:S(2)}, u32[]{:S(2)}) async-start(bf16[32,5,2,32,128]{4,3,2,1,0:T(8,128)(2,1)} %bitcast.31), calls=%async_computation.1 | async-start | bytes 5242880 | tf_op jit(solution)/shard_map/all_to_all | solution.py:452
  65.5 46.6 %process_blocks.2 = (f32[128,2,4,1024]{3,2,1,0:T(4,128)}, bf16[96,2,32,128]{3,2,1,0:T(8,128)(2,1)}) custom-call(s32[2]{0:T(128)} %pad_add_fusion.1.meta, s32[136]{0:T(256)} %copy-done.6, s32[128]{0:T(128)} %get-tuple-element.25.slot, s32[128]{0:T(128)} %plane.3, bf16[96,2,32,128]{3,2,1,0:T(8,128)(2,1)} %bitcast.16.tiles, f32[128,2,4,1024]{3,2,1,0:T(4,128)} %observed.3, ...), custom_call_target="tpu_custom_call" | custom-call | flops 8589934592 | bytes 41943040 | tf_op jit(solution)/shard_map/process_blocks/pallas_call | solution.py:309
  112.2 12.2 %all-to-all-done.1 = bf16[32,5,2,32,128]{4,3,2,1,0:T(8,128)(2,1)} async-done(((bf16[32,5,2,32,128]{4,3,2,1,0:T(8,128)(2,1)}), bf16[32,5,2,32,128]{4,3,2,1,0:T(8,128)(2,1)}, u32[]{:S(2)}, u32[]{:S(2)}) %all-to-all-start.1) | async-done | bytes 2621472 | tf_op jit(solution)/shard_map/all_to_all | solution.py:452
  124.4 4.2 %all-to-all-start.3 = ((bf16[32,3,2,32,128]{4,3,2,1,0:T(8,128)(2,1)}), bf16[32,3,2,32,128]{4,3,2,1,0:T(8,128)(2,1)S(1)}, u32[]{:S(2)}, u32[]{:S(2)}) async-start(bf16[32,3,2,32,128]{4,3,2,1,0:T(8,128)(2,1)} %bitcast.34), calls=%async_computation.3 | async-start | bytes 3145728 | tf_op jit(solution)/shard_map/all_to_all | solution.py:452
  128.6 1.2 pad_add_fusion.meta
  129.8 27.6 %process_blocks.3 = (f32[128,2,4,1024]{3,2,1,0:T(4,128)}, bf16[160,2,32,128]{3,2,1,0:T(8,128)(2,1)}) custom-call(s32[2]{0:T(128)} %pad_add_fusion.meta, s32[136]{0:T(256)} %copy-done.6, s32[128]{0:T(128)} %get-tuple-element.25.slot, s32[128]{0:T(128)} %plane.3, bf16[160,2,32,128]{3,2,1,0:T(8,128)(2,1)} %bitcast.13.tiles, ...), custom_call_target="tpu_custom_call", output_to_operand_aliasing={{0}: (13, {})} | custom-call | flops 5368709120 | bytes 26214400 | tf_op jit(solution)/shard_map/process_blocks/pallas_call | solution.py:309
  157.4 8.7 %all-to-all-done.3 = bf16[32,3,2,32,128]{4,3,2,1,0:T(8,128)(2,1)S(1)} async-done(((bf16[32,3,2,32,128]{4,3,2,1,0:T(8,128)(2,1)}), bf16[32,3,2,32,128]{4,3,2,1,0:T(8,128)(2,1)S(1)}, u32[]{:S(2)}, u32[]{:S(2)}) %all-to-all-start.3) | async-done | bytes 1572896 | tf_op jit(solution)/shard_map/all_to_all | solution.py:452
  166.2 1.1 copy-done.1
  167.3 3.9 %all-to-all-start.4 = ((bf16[32,5,2,32,128]{4,3,2,1,0:T(8,128)(2,1)}), bf16[32,5,2,32,128]{4,3,2,1,0:T(8,128)(2,1)}, u32[]{:S(2)}, u32[]{:S(2)}) async-start(bf16[32,5,2,32,128]{4,3,2,1,0:T(8,128)(2,1)} %bitcast.32), calls=%async_computation.4 | async-start | bytes 5242880 | tf_op jit(solution)/shard_map/all_to_all | solution.py:452
  172.8 1.4 copy-done.2
  174.2 1.3 sum_tiles.2.refs_0_
  175.4 55.9 %all-to-all-done.4 = bf16[32,5,2,32,128]{4,3,2,1,0:T(8,128)(2,1)} async-done(((bf16[32,5,2,32,128]{4,3,2,1,0:T(8,128)(2,1)}), bf16[32,5,2,32,128]{4,3,2,1,0:T(8,128)(2,1)}, u32[]{:S(2)}, u32[]{:S(2)}) %all-to-all-start.4) | async-done | bytes 2621472 | tf_op jit(solution)/shard_map/all_to_all | solution.py:452
  231.3 4.5 %sum_tiles.3 = f32[64,64,128]{2,1,0:T(8,128)} custom-call(s32[160]{0:T(256)S(1)} %reshape.132.requested, f32[1]{0:T(128)} %bitcast.17.scale_ref, f32[64,64,128]{2,1,0:T(8,128)S(1)} %sum_tiles.2.refs_0_, bf16[160,64,128]{2,1,0:T(8,128)(2,1)} %bitcast.21.refs_1_), custom_call_target="tpu_custom_call" | custom-call | flops 1310720 | bytes 5242880 | tf_op jit(solution)/shard_map/sum_tiles/pallas_call | solution.py:370
  (38 shorter events, 4.6 us)
Async XLA Ops:
  0.6 16.6 %copy-start = (bf16[64,2,32,128]{3,2,1,0:T(8,128)(2,1)S(1)}, bf16[64,2,32,128]{3,2,1,0:T(8,128)(2,1)}, u32[]{:S(2)}) copy-start(bf16[64,2,32,128]{3,2,1,0:T(8,128)(2,1)} %param.19) | copy-start | bytes 3145732
  17.2 5.5 %copy-start.5 = (s32[128,1]{0,1:T(1,128)S(1)}, s32[128,1]{0,1:T(1,128)}, u32[]{:S(2)}) copy-start(s32[128,1]{0,1:T(1,128)} %param.16) | copy-start | bytes 1540
  19.2 6.7 %copy-start.3 = (f32[128,1024]{1,0:T(8,128)S(1)}, f32[128,1024]{1,0:T(8,128)}, u32[]{:S(2)}) copy-start(f32[128,1024]{1,0:T(8,128)} %weight_ref.1) | copy-start | bytes 1572868
  19.2 41.4 %all-to-all-start.2 = ((bf16[32,3,2,32,128]{4,3,2,1,0:T(8,128)(2,1)}), bf16[32,3,2,32,128]{4,3,2,1,0:T(8,128)(2,1)}, u32[]{:S(2)}, u32[]{:S(2)}) async-start(bf16[32,3,2,32,128]{4,3,2,1,0:T(8,128)(2,1)} %bitcast.15), calls=%async_computation.2 | async-start | bytes 3145728 | tf_op jit(solution)/shard_map/all_to_all | solution.py:452
  24.9 2.7 %copy-start.4 = (f32[128,2,1024]{2,1,0:T(2,128)S(1)}, f32[128,2,1024]{2,1,0:T(2,128)}, u32[]{:S(2)}) copy-start(f32[128,2,1024]{2,1,0:T(2,128)} %param.14) | copy-start | bytes 3145732
  25.9 2.5 %copy-start.6 = (s32[136]{0:T(256)}, s32[136]{0:T(256)S(1)}, u32[]{:S(2)}) copy-start(s32[136]{0:T(256)S(1)} %select_reduce_fusion.order) | copy-start | bytes 1636
  60.6 63.8 %all-to-all-start.1 = ((bf16[32,5,2,32,128]{4,3,2,1,0:T(8,128)(2,1)}), bf16[32,5,2,32,128]{4,3,2,1,0:T(8,128)(2,1)}, u32[]{:S(2)}, u32[]{:S(2)}) async-start(bf16[32,5,2,32,128]{4,3,2,1,0:T(8,128)(2,1)} %bitcast.31), calls=%async_computation.1 | async-start | bytes 5242880 | tf_op jit(solution)/shard_map/all_to_all | solution.py:452
  124.4 41.8 %all-to-all-start.3 = ((bf16[32,3,2,32,128]{4,3,2,1,0:T(8,128)(2,1)}), bf16[32,3,2,32,128]{4,3,2,1,0:T(8,128)(2,1)S(1)}, u32[]{:S(2)}, u32[]{:S(2)}) async-start(bf16[32,3,2,32,128]{4,3,2,1,0:T(8,128)(2,1)} %bitcast.34), calls=%async_computation.3 | async-start | bytes 3145728 | tf_op jit(solution)/shard_map/all_to_all | solution.py:452
  166.2 1.1 copy-start.1
  167.3 64.0 %all-to-all-start.4 = ((bf16[32,5,2,32,128]{4,3,2,1,0:T(8,128)(2,1)}), bf16[32,5,2,32,128]{4,3,2,1,0:T(8,128)(2,1)}, u32[]{:S(2)}, u32[]{:S(2)}) async-start(bf16[32,5,2,32,128]{4,3,2,1,0:T(8,128)(2,1)} %bitcast.32), calls=%async_computation.4 | async-start | bytes 5242880 | tf_op jit(solution)/shard_map/all_to_all | solution.py:452
  172.7 1.4 copy-start.2

commit v7 on v6

--- a/solution.py
+++ b/solution.py
@@ -15,8 +15,6 @@
 LANES = 512
 TILE = 128
 ROWS = 8
-OPENING = 2
-MIRROR_PARTS = (0, 3, 8)
 UNROLL = 8
 VMEM_BYTES = 60 * 1024 * 1024
 SIN_TERMS = [(-1.0) ** i * (2.0 * math.pi) ** (2 * i + 1) / math.factorial(2 * i + 1) for i in range(8)]
@@ -343,37 +341,73 @@
 
 def sum_kernel(requested, scale_ref, *refs, last):
     if last:
-        old_ref, arrived_ref, out_ref, total_ref = refs
-        total_ref[: out_ref.shape[0]] = old_ref[...]
+        old, arrived, out, total_ref, other_ref, arrived_ref, out_ref, old_ref, in_sems, out_sems, old_sem = refs
+        old_copy = pltpu.make_async_copy(old, old_ref, old_sem)
     else:
-        arrived_ref, out_ref, total_ref = refs
-        total_ref[...] = jnp.zeros_like(total_ref)
-    unused = out_ref.shape[0]
-    slots = arrived_ref.shape[0]
-    together = math.gcd(slots, 8)
-
-    @pl.loop(0, slots // together)
-    def _(i):
-        for k in range(together):
-            at = i * together + k
-            tile = requested[at]
-            total_ref[jnp.where(tile < 0, unused, tile)] += arrived_ref[at].astype(jnp.float32)
-
-    total = total_ref[:unused]
-    out_ref[...] = total * scale_ref[0] if last else total
+        arrived, out, total_ref, other_ref, arrived_ref, out_ref, in_sems, out_sems = refs
+    unused = out.shape[0]
+    parts = in_sems.shape[0]
+    slots = arrived.shape[0] // parts
+    tiles = unused // out_sems.shape[0]
+    together = math.gcd(slots, 8) // 2
+    copies = []
+    for part in range(parts):
+        rows = pl.ds(part * slots, slots)
+        copies.append(pltpu.make_async_copy(arrived.at[rows], arrived_ref.at[rows], in_sems.at[part]))
+        copies[part].start()
+    if last:
+        old_copy.start()
+    total_ref[...] = jnp.zeros_like(total_ref)
+    other_ref[...] = jnp.zeros_like(other_ref)
+
+    for part in range(parts):
+        copies[part].wait()
+
+        @pl.loop(0, slots // (2 * together))
+        def _(i):
+            for k in range(together):
+                at = part * slots + 2 * (i * together + k)
+                tile, other = requested[at], requested[at + 1]
+                tile, other = jnp.where(tile < 0, unused, tile), jnp.where(other < 0, unused, other)
+                value = total_ref[tile] + arrived_ref[at].astype(jnp.float32)
+                beside = other_ref[other] + arrived_ref[at + 1].astype(jnp.float32)
+                total_ref[tile] = value
+                other_ref[other] = beside
+
+    if last:
+        old_copy.wait()
+    sent = []
+    for part in range(out_sems.shape[0]):
+        rows = pl.ds(part * tiles, tiles)
+        total = total_ref[rows] + other_ref[rows]
+        out_ref[rows] = (total + old_ref[rows]) * scale_ref[0] if last else total
+        sent.append(pltpu.make_async_copy(out_ref.at[rows], out.at[rows], out_sems.at[part]))
+        sent[part].start()
+    for copy in sent:
+        copy.wait()
 
 
 def sum_tiles(requested, scale, arrived, owned, old=None):
     shape = (owned,) + arrived.shape[1:]
-    operands = [arrived] if old is None else [old, arrived]
-    vmem = pl.BlockSpec(memory_space=pltpu.VMEM)
+    last = old is not None
+    operands = [old, arrived] if last else [arrived]
+    scratch = [
+        pltpu.VMEM((owned + 1,) + shape[1:], jnp.float32),
+        pltpu.VMEM((owned + 1,) + shape[1:], jnp.float32),
+        pltpu.VMEM(arrived.shape, arrived.dtype),
+        pltpu.VMEM(shape, jnp.float32),
+    ]
+    sems = [pltpu.SemaphoreType.DMA((math.gcd(arrived.shape[0], 4),)), pltpu.SemaphoreType.DMA((math.gcd(owned, 4),))]
+    if last:
+        scratch.append(pltpu.VMEM(shape, jnp.float32))
+        sems.append(pltpu.SemaphoreType.DMA(()))
     return pl.pallas_call(
-        functools.partial(sum_kernel, last=old is not None),
+        functools.partial(sum_kernel, last=last),
         out_shape=jax.ShapeDtypeStruct(shape, jnp.float32),
-        in_specs=[pl.BlockSpec(memory_space=pltpu.SMEM)] * 2 + [vmem] * len(operands),
-        out_specs=vmem,
-        scratch_shapes=[pltpu.VMEM((owned + 1,) + shape[1:], jnp.float32)],
-        compiler_params=pltpu.CompilerParams(vmem_limit_bytes=VMEM_BYTES // 4),
+        in_specs=[pl.BlockSpec(memory_space=pltpu.SMEM)] * 2 + [pl.BlockSpec(memory_space=pl.ANY)] * len(operands),
+        out_specs=pl.BlockSpec(memory_space=pl.ANY),
+        scratch_shapes=scratch + sems,
+        compiler_params=pltpu.CompilerParams(vmem_limit_bytes=VMEM_BYTES // 3),
         cost_estimate=pl.CostEstimate(flops=arrived.size, bytes_accessed=arrived.size * 4, transcendentals=0),
         name="sum_tiles",
     )(requested, scale, *operands)

time: 237 us -> 236 us (level)
  Pallas kernels: 102 us -> 98.8 us
    pallas_call x2, Pallas kernels: 74.2 us -> 70.9 us  [process_blocks(): pl.pallas_call(functools.partial(block_kernel, carried=len(carried)), out...]
  transfers between devices with their start and end apart: 4 -> 4, of which waited for: 4 -> 4; matrix products, arithmetic and copies ran while one was open for 6% -> 6% of each run, Pallas kernels for 40% -> 39%
where the time goes in v7:
time: 236 us; the launch traced here: 235 us
  Pallas kernels  98.8 us (42%)
  waiting for transfers between devices  85.4 us (36%)
  starting transfers between devices  15.3 us (6%)
  blocking collectives  14.4 us (6%)
  local copies, waits for them, and re-layouts  13.7 us (6%)
  other arithmetic  4.94 us (2%)
  between operations  2.89 us (1%)
    all_to_all x4, waiting for transfers between devices, exchange(): lax.all_to_all(operand, AXES, split_axis=0, concat_axis=0, tiled=True)  85.4 us
    pallas_call x2, Pallas kernels, process_blocks(): pl.pallas_call(functools.partial(block_kernel, carried=len(carried)), out...  70.9 us
    pallas_call x1, Pallas kernels, kernel_tables(): pl.pallas_call(table_kernel, grid=(planes // part,), out_shape=[jax.Shape...  19.6 us
    all_to_all x4, starting transfers between devices, exchange(): lax.all_to_all(operand, AXES, split_axis=0, concat_axis=0, tiled=True)  15.3 us
    all_to_all x1, blocking collectives, exchange(): lax.all_to_all(operand, AXES, split_axis=0, concat_axis=0, tiled=True)  14.4 us
    pallas_call x2, Pallas kernels, sum_tiles(): pl.pallas_call(functools.partial(sum_kernel, last=last), out_shape=jax.Sh...  6.28 us
  transfers between devices with their start and end apart: 4, of which 4 were waited for; matrix products, arithmetic and copies ran while one was open for 6% of the time, Pallas kernels for 39%

profile of v7, /device:TPU:0, one launch (start us, length us, event | category | flops | bytes accessed | tf_op | source)
XLA Modules:
  0.0 235.4 jit_solution(1598018469025504902)
XLA Ops:
  0.6 2.1 requests_of.1
  2.7 14.4 %all_to_all.32 = f32[32,1,128]{2,1,0:T(1,128)S(1)} all-to-all(f32[32,1,128]{2,1,0:T(1,128)} %bitcast.37), channel_id=1, replica_groups=mesh['facet'=4,'vis'=8] {'facet','vis'}, dimensions={0} | all-to-all | bytes 32768 | tf_op jit(solution)/shard_map/all_to_all | solution.py:486
  17.2 1.9 gather_fusion.4
  19.2 3.5 %all-to-all-start.2 = ((bf16[32,3,2,32,128]{4,3,2,1,0:T(8,128)(2,1)}), bf16[32,3,2,32,128]{4,3,2,1,0:T(8,128)(2,1)}, u32[]{:S(2)}, u32[]{:S(2)}) async-start(bf16[32,3,2,32,128]{4,3,2,1,0:T(8,128)(2,1)} %bitcast.15), calls=%async_computation.2 | async-start | bytes 3145728 | tf_op jit(solution)/shard_map/all_to_all | solution.py:486
  25.9 1.6 gather_fusion.3
  27.6 0.8 fusion.3
  28.6 1.6 gather_fusion.2
  30.2 1.6 gather_fusion.1
  31.9 19.6 %kernel_tables.1 = (bf16[32,64,64]{2,1,0:T(8,128)(2,1)}, bf16[32,64,64]{2,1,0:T(8,128)(2,1)}, bf16[32,64,256]{2,1,0:T(8,128)(2,1)}, bf16[32,256,256]{2,1,0:T(8,128)(2,1)}) custom-call(bf16[32,64,32]{2,1,0:T(8,128)(2,1)} %bitcast.42, bf16[128,64]{1,0:T(8,128)(2,1)} %constant.60.clone.signs_ref, bf16[128,64]{1,0:T(8,128)(2,1)} %constant.61.clone.columns_ref, ...), custom_call_target="tpu_custom_call" | custom-call | flops 536870912 | bytes 4194304 | tf_op jit(solution)/shard_map/kernel_tables/pallas_call | solution.py:473
  51.6 2.6 %gather_fusion = bf16[160,2,32,128]{3,2,1,0:T(8,128)(2,1)} fusion(bf16[64,2,32,128]{3,2,1,0:T(8,128)(2,1)S(1)} %copy-done, s32[1024]{0:T(1024)S(1)} %pad_clamp_fusion.2), kind=kCustom, calls=%fused_computation | custom fusion | bytes 5243520 | tf_op jit(solution)/shard_map/jit(_take)/gather | solution.py:554
  54.2 6.4 %all-to-all-done.2 = bf16[32,3,2,32,128]{4,3,2,1,0:T(8,128)(2,1)} async-done(((bf16[32,3,2,32,128]{4,3,2,1,0:T(8,128)(2,1)}), bf16[32,3,2,32,128]{4,3,2,1,0:T(8,128)(2,1)}, u32[]{:S(2)}, u32[]{:S(2)}) %all-to-all-start.2) | async-done | bytes 1572896 | tf_op jit(solution)/shard_map/all_to_all | solution.py:486
  60.6 3.7 %all-to-all-start.1 = ((bf16[32,5,2,32,128]{4,3,2,1,0:T(8,128)(2,1)}), bf16[32,5,2,32,128]{4,3,2,1,0:T(8,128)(2,1)}, u32[]{:S(2)}, u32[]{:S(2)}) async-start(bf16[32,5,2,32,128]{4,3,2,1,0:T(8,128)(2,1)} %bitcast.31), calls=%async_computation.1 | async-start | bytes 5242880 | tf_op jit(solution)/shard_map/all_to_all | solution.py:486
  65.5 46.7 %process_blocks.2 = (f32[128,2,4,1024]{3,2,1,0:T(4,128)}, bf16[96,2,32,128]{3,2,1,0:T(8,128)(2,1)}) custom-call(s32[2]{0:T(128)} %pad_add_fusion.1.meta, s32[136]{0:T(256)} %copy-done.6, s32[128]{0:T(128)} %get-tuple-element.25.slot, s32[128]{0:T(128)} %plane.3, bf16[96,2,32,128]{3,2,1,0:T(8,128)(2,1)} %bitcast.16.tiles, f32[128,2,4,1024]{3,2,1,0:T(4,128)} %observed.3, ...), custom_call_target="tpu_custom_call" | custom-call | flops 8589934592 | bytes 41943040 | tf_op jit(solution)/shard_map/process_blocks/pallas_call | solution.py:307
  112.2 12.2 %all-to-all-done.1 = bf16[32,5,2,32,128]{4,3,2,1,0:T(8,128)(2,1)} async-done(((bf16[32,5,2,32,128]{4,3,2,1,0:T(8,128)(2,1)}), bf16[32,5,2,32,128]{4,3,2,1,0:T(8,128)(2,1)}, u32[]{:S(2)}, u32[]{:S(2)}) %all-to-all-start.1) | async-done | bytes 2621472 | tf_op jit(solution)/shard_map/all_to_all | solution.py:486
  124.4 4.2 %all-to-all-start.3 = ((bf16[32,3,2,32,128]{4,3,2,1,0:T(8,128)(2,1)}), bf16[32,3,2,32,128]{4,3,2,1,0:T(8,128)(2,1)S(1)}, u32[]{:S(2)}, u32[]{:S(2)}) async-start(bf16[32,3,2,32,128]{4,3,2,1,0:T(8,128)(2,1)} %bitcast.34), calls=%async_computation.3 | async-start | bytes 3145728 | tf_op jit(solution)/shard_map/all_to_all | solution.py:486
  128.6 1.2 pad_add_fusion.meta
  129.8 24.2 %process_blocks.3 = (f32[128,2,4,1024]{3,2,1,0:T(4,128)}, bf16[160,2,32,128]{3,2,1,0:T(8,128)(2,1)}) custom-call(s32[2]{0:T(128)} %pad_add_fusion.meta, s32[136]{0:T(256)} %copy-done.6, s32[128]{0:T(128)} %get-tuple-element.25.slot, s32[128]{0:T(128)} %plane.3, bf16[160,2,32,128]{3,2,1,0:T(8,128)(2,1)} %bitcast.13.tiles, ...), custom_call_target="tpu_custom_call", output_to_operand_aliasing={{0}: (13, {})} | custom-call | flops 5368709120 | bytes 26214400 | tf_op jit(solution)/shard_map/process_blocks/pallas_call | solution.py:307
  154.1 12.1 %all-to-all-done.3 = bf16[32,3,2,32,128]{4,3,2,1,0:T(8,128)(2,1)S(1)} async-done(((bf16[32,3,2,32,128]{4,3,2,1,0:T(8,128)(2,1)}), bf16[32,3,2,32,128]{4,3,2,1,0:T(8,128)(2,1)S(1)}, u32[]{:S(2)}, u32[]{:S(2)}) %all-to-all-start.3) | async-done | bytes 1572896 | tf_op jit(solution)/shard_map/all_to_all | solution.py:486
  166.2 1.1 copy-done.1
  167.3 3.9 %all-to-all-start.4 = ((bf16[32,5,2,32,128]{4,3,2,1,0:T(8,128)(2,1)}), bf16[32,5,2,32,128]{4,3,2,1,0:T(8,128)(2,1)}, u32[]{:S(2)}, u32[]{:S(2)}) async-start(bf16[32,5,2,32,128]{4,3,2,1,0:T(8,128)(2,1)} %bitcast.32), calls=%async_computation.4 | async-start | bytes 5242880 | tf_op jit(solution)/shard_map/all_to_all | solution.py:486
  172.8 1.4 copy-done.2
  174.2 2.4 %sum_tiles.2.refs_0_ = f32[64,64,128]{2,1,0:T(8,128)S(1)} custom-call(s32[96]{0:T(128)S(1)} %reshape.134.requested, f32[1]{0:T(128)} %bitcast.17.scale_ref, bf16[96,64,128]{2,1,0:T(8,128)(2,1)S(1)} %bitcast.30), custom_call_target="tpu_custom_call" | custom-call | flops 786432 | bytes 3145728 | tf_op jit(solution)/shard_map/sum_tiles/pallas_call | solution.py:404
  176.6 54.7 %all-to-all-done.4 = bf16[32,5,2,32,128]{4,3,2,1,0:T(8,128)(2,1)} async-done(((bf16[32,5,2,32,128]{4,3,2,1,0:T(8,128)(2,1)}), bf16[32,5,2,32,128]{4,3,2,1,0:T(8,128)(2,1)}, u32[]{:S(2)}, u32[]{:S(2)}) %all-to-all-start.4) | async-done | bytes 2621472 | tf_op jit(solution)/shard_map/all_to_all | solution.py:486
  231.3 3.9 %sum_tiles.3 = f32[64,64,128]{2,1,0:T(8,128)} custom-call(s32[160]{0:T(256)S(1)} %reshape.132.requested, f32[1]{0:T(128)} %bitcast.17.scale_ref, f32[64,64,128]{2,1,0:T(8,128)S(1)} %sum_tiles.2.refs_0_, bf16[160,64,128]{2,1,0:T(8,128)(2,1)} %bitcast.21.refs_1_), custom_call_target="tpu_custom_call" | custom-call | flops 1310720 | bytes 5242880 | tf_op jit(solution)/shard_map/sum_tiles/pallas_call | solution.py:404
  (38 shorter events, 4.6 us)
Async XLA Ops:
  0.6 16.6 %copy-start = (bf16[64,2,32,128]{3,2,1,0:T(8,128)(2,1)S(1)}, bf16[64,2,32,128]{3,2,1,0:T(8,128)(2,1)}, u32[]{:S(2)}) copy-start(bf16[64,2,32,128]{3,2,1,0:T(8,128)(2,1)} %param.19) | copy-start | bytes 3145732
  17.2 5.5 %copy-start.5 = (s32[128,1]{0,1:T(1,128)S(1)}, s32[128,1]{0,1:T(1,128)}, u32[]{:S(2)}) copy-start(s32[128,1]{0,1:T(1,128)} %param.16) | copy-start | bytes 1540
  19.2 6.7 %copy-start.3 = (f32[128,1024]{1,0:T(8,128)S(1)}, f32[128,1024]{1,0:T(8,128)}, u32[]{:S(2)}) copy-start(f32[128,1024]{1,0:T(8,128)} %weight_ref.1) | copy-start | bytes 1572868
  19.2 41.4 %all-to-all-start.2 = ((bf16[32,3,2,32,128]{4,3,2,1,0:T(8,128)(2,1)}), bf16[32,3,2,32,128]{4,3,2,1,0:T(8,128)(2,1)}, u32[]{:S(2)}, u32[]{:S(2)}) async-start(bf16[32,3,2,32,128]{4,3,2,1,0:T(8,128)(2,1)} %bitcast.15), calls=%async_computation.2 | async-start | bytes 3145728 | tf_op jit(solution)/shard_map/all_to_all | solution.py:486
  24.9 2.7 %copy-start.4 = (f32[128,2,1024]{2,1,0:T(2,128)S(1)}, f32[128,2,1024]{2,1,0:T(2,128)}, u32[]{:S(2)}) copy-start(f32[128,2,1024]{2,1,0:T(2,128)} %param.14) | copy-start | bytes 3145732
  25.9 2.5 %copy-start.6 = (s32[136]{0:T(256)}, s32[136]{0:T(256)S(1)}, u32[]{:S(2)}) copy-start(s32[136]{0:T(256)S(1)} %select_reduce_fusion.order) | copy-start | bytes 1636
  60.6 63.8 %all-to-all-start.1 = ((bf16[32,5,2,32,128]{4,3,2,1,0:T(8,128)(2,1)}), bf16[32,5,2,32,128]{4,3,2,1,0:T(8,128)(2,1)}, u32[]{:S(2)}, u32[]{:S(2)}) async-start(bf16[32,5,2,32,128]{4,3,2,1,0:T(8,128)(2,1)} %bitcast.31), calls=%async_computation.1 | async-start | bytes 5242880 | tf_op jit(solution)/shard_map/all_to_all | solution.py:486
  124.4 41.8 %all-to-all-start.3 = ((bf16[32,3,2,32,128]{4,3,2,1,0:T(8,128)(2,1)}), bf16[32,3,2,32,128]{4,3,2,1,0:T(8,128)(2,1)S(1)}, u32[]{:S(2)}, u32[]{:S(2)}) async-start(bf16[32,3,2,32,128]{4,3,2,1,0:T(8,128)(2,1)} %bitcast.34), calls=%async_computation.3 | async-start | bytes 3145728 | tf_op jit(solution)/shard_map/all_to_all | solution.py:486
  166.2 1.1 copy-start.1
  167.3 64.0 %all-to-all-start.4 = ((bf16[32,5,2,32,128]{4,3,2,1,0:T(8,128)(2,1)}), bf16[32,5,2,32,128]{4,3,2,1,0:T(8,128)(2,1)}, u32[]{:S(2)}, u32[]{:S(2)}) async-start(bf16[32,5,2,32,128]{4,3,2,1,0:T(8,128)(2,1)} %bitcast.32), calls=%async_computation.4 | async-start | bytes 5242880 | tf_op jit(solution)/shard_map/all_to_all | solution.py:486
  172.7 1.4 copy-start.2
